TPU v7x, 32 devices: a whole 2x2x4 slice. The times are simulated.
32 devices in a mesh: seq: 4 (over y, x), rows: 8 (over z, core).
Axes of the slice: x: 2, y: 2, z: 4, core: 2. Of those that a mesh axis runs over, the one named last changes fastest.
Arguments:
- block_input: bfloat16 [8, 1024, 1024], P('rows', 'seq'), may hold values from -6 to 6
- valid_length: int32 [8], P('rows'), may hold values from 1 to 1024, as said below
- query_weight: bfloat16 [1024, 1024], P(('seq', 'rows')), may hold values from -0.1875 to 0.1875
- key_weight: bfloat16 [1024, 2048], P(('seq', 'rows')), may hold values from -0.1875 to 0.1875
- value_weight: bfloat16 [1024, 2048], P(('seq', 'rows')), may hold values from -0.1875 to 0.1875
- beta_weight: bfloat16 [1024, 16], P(('seq', 'rows')), may hold values from -0.1875 to 0.1875
- decay_weight: bfloat16 [1024, 8], P(('seq', 'rows')), may hold values from -0.1875 to 0.1875
- gate_weight: bfloat16 [1024, 1024], P(('seq', 'rows')), may hold values from -0.1875 to 0.1875
- out_weight: bfloat16 [1024, 1024], P(('seq', 'rows')), may hold values from -0.375 to 0.375
- ffn_gate_weight: bfloat16 [1024, 2816], P(('seq', 'rows')), may hold values from -0.1875 to 0.1875
- ffn_up_weight: bfloat16 [1024, 2816], P(('seq', 'rows')), may hold values from -0.1875 to 0.1875
- ffn_down_weight: bfloat16 [1024, 2816], P(('seq', 'rows')), may hold values from -0.109375 to 0.109375
- norm_gain: bfloat16 [1024], P(('seq', 'rows')), may hold values from 0.5 to 1.5
- ffn_norm_gain: bfloat16 [1024], P(('seq', 'rows')), may hold values from 0.5 to 1.5
- head_norm_gain: float32 [128], replicated, may hold values from 0.5 to 1.5
- decay_log: float32 [8], replicated, may hold values from -2 to 1
- decay_bias: float32 [8], replicated, may hold values from -7 to -2
- conv_weight: float32 [4, 5120], replicated, may hold values from -3 to 3
- output_grad: bfloat16 [8, 1024, 1024], P('rows', 'seq'), may hold values from -6 to 6
Outputs:
- block_output: bfloat16 [8, 1024, 1024], P('rows', 'seq')
- input_grad: float32 [8, 1024, 1024], P('rows', 'seq')
- query_weight_grad: float32 [1024, 1024], P(('seq', 'rows'))
- key_weight_grad: float32 [1024, 2048], P(('seq', 'rows'))
- value_weight_grad: float32 [1024, 2048], P(('seq', 'rows'))
- beta_weight_grad: float32 [1024, 16], P(('seq', 'rows'))
- decay_weight_grad: float32 [1024, 8], P(('seq', 'rows'))
- gate_weight_grad: float32 [1024, 1024], P(('seq', 'rows'))
- out_weight_grad: float32 [1024, 1024], P(('seq', 'rows'))
- ffn_gate_weight_grad: float32 [1024, 2816], P(('seq', 'rows'))
- ffn_up_weight_grad: float32 [1024, 2816], P(('seq', 'rows'))
- ffn_down_weight_grad: float32 [1024, 2816], P(('seq', 'rows'))
- norm_gain_grad: float32 [1024], P(('seq', 'rows'))
- ffn_norm_gain_grad: float32 [1024], P(('seq', 'rows'))
- head_norm_gain_grad: float32 [128], replicated
- decay_log_grad: float32 [8], replicated
- decay_bias_grad: float32 [8], replicated
- conv_weight_grad: float32 [4, 5120], replicated
Inputs may be any that keep to these rules, and one draw needn't show every extreme that they name: `valid_length`: each row's valid tokens come first; in every draw some row has all 1024 tokens valid.
All inputs are finite; a program needn't handle non-finite values.
Results may differ from a plain program's by a relative error of at most 0.01.
Values may be sent and summed in bfloat16 or wider, within the bound.
No kernel may reach another device: no remote copies, remote signals or barrier semaphores. Data moves between devices by JAX's collectives and lax.ppermute only.
A program may use at most 384 MiB of HBM per device.

v0:
```python
import jax
import jax.numpy as jnp
from jax import lax
from jax.sharding import PartitionSpec as P

GROUP = 64


EPS_NORM = 1e-06
EPS_KEY = 1e-06
EPS_HEAD = 1e-05
HIGHEST = lax.Precision.HIGHEST


def passed_along(array, axis, by):
    length = lax.axis_size(axis)
    pairs = [(i, i + by) for i in range(length) if 0 <= i + by < length]
    return lax.ppermute(array, axis, pairs)


def carried_in(part, axis, combine, identity):
    place = lax.axis_index(axis)
    gathered = jax.tree.map(lambda a: lax.all_gather(a, axis), part)
    state = jax.tree.map(lambda a, e: jnp.zeros_like(a) + jnp.asarray(e, a.dtype), part, identity)

    def carried_one(turn, state):
        return combine(
            state, jax.tree.map(lambda a: lax.dynamic_index_in_dim(a, turn, 0, False), gathered)
        )

    return lax.fori_loop(0, place, carried_one, state)


def entering(array, axis, join, neutral):
    count = lax.axis_size(axis)
    place = lax.axis_index(axis)
    ahead = count - 1 - place
    gathered = jax.tree.map(
        lambda a, kind: lax.all_gather(a.astype(kind), axis),
        array,
        jax.tree.map(lambda a: jnp.bfloat16 if a.dtype == jnp.float32 else a.dtype, array),
    )
    state = jax.tree.map(lambda a, e: jnp.zeros_like(a) + jnp.asarray(e, a.dtype), array, neutral)

    def entering_one(turn, state):
        source = count - 1 - turn
        return join(
            state,
            jax.tree.map(
                lambda a, own: lax.dynamic_index_in_dim(a, source, 0, False).astype(own.dtype),
                gathered,
                array,
            ),
        )

    return lax.fori_loop(0, ahead, entering_one, state)


def batched_product(matrix_one, matrix_two):
    return jnp.einsum("...ij,...jk->...ik", matrix_one, matrix_two, precision=HIGHEST)


def compose_pair(earlier, later):
    return (batched_product(later[0], earlier[0]), batched_product(later[0], earlier[1]) + later[1])


def root_norm(features, gain):
    return (
        features
        * lax.rsqrt(jnp.mean(features * features, axis=-1, keepdims=True) + EPS_NORM)
        * gain
    )


def split_blocks(tensor_in, block_count):
    dims_in = tensor_in.shape
    tensor_in = tensor_in.reshape(
        (dims_in[0], block_count, dims_in[1] // block_count) + dims_in[2:]
    )
    return jnp.moveaxis(tensor_in, 1, 0)


def join_blocks(tensor_in):
    block_count, head_count, block_size, head_dim = tensor_in.shape
    return tensor_in.transpose(0, 2, 1, 3).reshape(block_count * block_size, head_count, head_dim)


def lower_solve(matrix, right_side):
    return jax.scipy.linalg.solve_triangular(matrix, right_side, lower=True)


def prepare(
    mixed_in,
    prev_rim,
    beta_pre,
    decay_pre,
    conv_weight,
    decay_log,
    decay_bias,
    valid_mask,
    block_count,
):
    token_count = mixed_in.shape[0]
    head_count = decay_log.shape[0]
    step_count = beta_pre.shape[1] // head_count
    padded = jnp.concatenate([prev_rim, mixed_in], axis=0)
    summed = padded[0:token_count] * conv_weight[0]
    for offset in range(1, conv_weight.shape[0]):
        summed = summed + padded[offset : offset + token_count] * conv_weight[offset]
    active = jax.nn.silu(summed)
    inner_width = active.shape[1] // (1 + 2 * step_count)
    head_dim = inner_width // head_count
    query_rows = active[:, :inner_width].reshape(token_count, head_count, head_dim)
    key_rows = active[:, inner_width : inner_width * (1 + step_count)].reshape(
        token_count, step_count, head_count, head_dim
    )
    value_rows = active[:, inner_width * (1 + step_count) :].reshape(
        token_count, step_count, head_count, head_dim
    )
    query_rows = (
        query_rows
        * lax.rsqrt(jnp.sum(query_rows * query_rows, axis=-1, keepdims=True) + EPS_KEY)
        * head_dim ** (-0.5)
    )
    key_rows = key_rows * lax.rsqrt(jnp.sum(key_rows * key_rows, axis=-1, keepdims=True) + EPS_KEY)
    beta_rows = (
        jax.nn.sigmoid(beta_pre).reshape(token_count, step_count, head_count)
        * valid_mask[:, None, None]
    )
    log_decay = -jnp.exp(decay_log) * jax.nn.softplus(decay_pre + decay_bias) * valid_mask[:, None]
    log_decay = jnp.concatenate(
        [log_decay[:, None, :], jnp.zeros((token_count, step_count - 1, head_count), jnp.float32)],
        axis=1,
    )
    pseudo_count = token_count * step_count
    key_rows = key_rows.transpose(2, 0, 1, 3).reshape(head_count, pseudo_count, head_dim)
    value_rows = value_rows.transpose(2, 0, 1, 3).reshape(head_count, pseudo_count, head_dim)
    beta_rows = beta_rows.transpose(2, 0, 1).reshape(head_count, pseudo_count)
    log_decay = log_decay.transpose(2, 0, 1).reshape(head_count, pseudo_count)
    query_rows = query_rows.transpose(1, 0, 2)
    return (
        split_blocks(query_rows, block_count),
        split_blocks(key_rows, block_count),
        split_blocks(value_rows, block_count),
        split_blocks(beta_rows, block_count),
        split_blocks(log_decay, block_count),
    )


def group_summary(key_rows, value_rows, beta_rows, log_decay):
    pseudo_count = key_rows.shape[1]
    head_dim = key_rows.shape[2]
    cum_decay = jnp.cumsum(log_decay, axis=1)
    row_place = lax.broadcasted_iota(jnp.int32, (pseudo_count, pseudo_count), 0)
    col_place = lax.broadcasted_iota(jnp.int32, (pseudo_count, pseudo_count), 1)
    strict = row_place > col_place
    spread = cum_decay[:, :, None] - cum_decay[:, None, :]
    pair_decay = jnp.where(strict, jnp.exp(jnp.where(strict, spread, 0.0)), 0.0)
    key_gram = jnp.einsum("hid,hjd->hij", key_rows, key_rows, precision=HIGHEST)
    system = (
        jnp.eye(pseudo_count, dtype=jnp.float32) + beta_rows[:, :, None] * pair_decay * key_gram
    )
    right_side = jnp.concatenate(
        [
            (beta_rows * jnp.exp(cum_decay))[:, :, None] * key_rows,
            beta_rows[:, :, None] * value_rows,
        ],
        axis=2,
    )
    solved = jax.vmap(lower_solve)(system, right_side)
    key_solve = solved[:, :, :head_dim]
    pseudo_values = solved[:, :, head_dim:]
    last_decay = cum_decay[:, -1]
    carry_keys = jnp.exp(last_decay[:, None] - cum_decay)[:, :, None] * key_rows
    transition = jnp.exp(last_decay)[:, None, None] * jnp.eye(
        head_dim, dtype=jnp.float32
    ) - jnp.einsum("hcd,hce->hde", carry_keys, key_solve, precision=HIGHEST)
    injected = jnp.einsum("hcd,hce->hde", carry_keys, pseudo_values, precision=HIGHEST)
    return (cum_decay, key_solve, pseudo_values, transition, injected)


def group_output(query_rows, key_rows, cum_decay, key_solve, pseudo_values, carried):
    token_count = query_rows.shape[1]
    pseudo_count = key_rows.shape[1]
    step_count = pseudo_count // token_count
    picked = cum_decay[:, step_count - 1 :: step_count]
    out_place = (
        lax.broadcasted_iota(jnp.int32, (token_count, pseudo_count), 0) * step_count
        + step_count
        - 1
    )
    col_place = lax.broadcasted_iota(jnp.int32, (token_count, pseudo_count), 1)
    visible = col_place <= out_place
    spread = picked[:, :, None] - cum_decay[:, None, :]
    weights = jnp.where(visible, jnp.exp(jnp.where(visible, spread, 0.0)), 0.0) * jnp.einsum(
        "htd,hjd->htj", query_rows, key_rows, precision=HIGHEST
    )
    fresh_values = pseudo_values - jnp.einsum("hcd,hde->hce", key_solve, carried, precision=HIGHEST)
    return jnp.exp(picked)[:, :, None] * jnp.einsum(
        "htd,hde->hte", query_rows, carried, precision=HIGHEST
    ) + jnp.einsum("htj,hje->hte", weights, fresh_values, precision=HIGHEST)


def device_summary(key_rows, value_rows, beta_rows, log_decay):
    cum_decay, key_solve, pseudo_values, transition, injected = jax.vmap(group_summary)(
        key_rows, value_rows, beta_rows, log_decay
    )
    head_dim = key_rows.shape[-1]
    start = (
        jnp.broadcast_to(jnp.eye(head_dim, dtype=jnp.float32), transition.shape[1:]),
        jnp.zeros(injected.shape[1:], jnp.float32),
    )

    def compose_step(carried, group_in):
        return (compose_pair(carried, group_in), None)

    whole, unused = lax.scan(compose_step, start, (transition, injected))
    return (cum_decay, key_solve, pseudo_values, transition, injected, whole[0], whole[1])


def device_outputs(
    query_rows, key_rows, cum_decay, key_solve, pseudo_values, transition, injected, start
):

    def advance(carried, group_in):
        query_block, key_block, cum_block, solve_block, pseudo_block, trans_block, inject_block = (
            group_in
        )
        produced = group_output(
            query_block, key_block, cum_block, solve_block, pseudo_block, carried
        )
        return (batched_product(trans_block, carried) + inject_block, produced)

    ending, group_outs = lax.scan(
        advance,
        start,
        (query_rows, key_rows, cum_decay, key_solve, pseudo_values, transition, injected),
    )
    return group_outs


def gated_norm(mixed_out, out_gate, head_gain, valid_mask):
    token_count, head_count, head_dim = mixed_out.shape
    normed = (
        mixed_out
        * lax.rsqrt(jnp.mean(mixed_out * mixed_out, axis=-1, keepdims=True) + EPS_HEAD)
        * head_gain
    )
    gated = (
        normed
        * jax.nn.silu(out_gate.reshape(token_count, head_count, head_dim))
        * valid_mask[:, None, None]
    )
    return gated.reshape(token_count, head_count * head_dim)


def project(left_side, matrix):
    return jnp.dot(left_side, matrix, preferred_element_type=jnp.float32)


def outer_sum(left_side, right_side):
    return lax.dot_general(
        left_side, right_side, (((0,), (0,)), ((), ())), preferred_element_type=jnp.float32
    )


def back_project(left_side, matrix):
    return lax.dot_general(
        left_side, matrix, (((1,), (1,)), ((), ())), preferred_element_type=jnp.float32
    )


def vector_slice(vector):
    return vector[:, None]


def split_columns(matrix, widths):
    pieces = []
    offset = 0
    for width in widths:
        pieces.append(matrix[:, offset : offset + width])
        offset = offset + width
    return pieces


def on_device(
    block_input,
    valid_length,
    query_weight,
    key_weight,
    value_weight,
    beta_weight,
    decay_weight,
    gate_weight,
    out_weight,
    ffn_gate_weight,
    ffn_up_weight,
    ffn_down_weight,
    norm_gain,
    ffn_norm_gain,
    head_norm_gain,
    decay_log,
    decay_bias,
    conv_weight,
    output_grad,
):
    gathered = (
        lax.all_gather(query_weight, ("seq", "rows"), axis=0, tiled=True),
        lax.all_gather(key_weight, ("seq", "rows"), axis=0, tiled=True),
        lax.all_gather(value_weight, ("seq", "rows"), axis=0, tiled=True),
        lax.all_gather(beta_weight, ("seq", "rows"), axis=0, tiled=True),
        lax.all_gather(decay_weight, ("seq", "rows"), axis=0, tiled=True),
        lax.all_gather(gate_weight, ("seq", "rows"), axis=0, tiled=True),
        lax.all_gather(out_weight, ("seq", "rows"), axis=0, tiled=True),
        lax.all_gather(ffn_gate_weight, ("seq", "rows"), axis=0, tiled=True),
        lax.all_gather(ffn_up_weight, ("seq", "rows"), axis=0, tiled=True),
        lax.all_gather(ffn_down_weight, ("seq", "rows"), axis=0, tiled=True),
        lax.all_gather(norm_gain, ("seq", "rows"), axis=0, tiled=True),
        lax.all_gather(ffn_norm_gain, ("seq", "rows"), axis=0, tiled=True),
    )
    (
        full_query,
        full_key,
        full_value,
        full_beta,
        full_decay,
        full_gate,
        full_out,
        full_ffn_gate,
        full_ffn_up,
        full_ffn_down,
        gain_first,
        gain_second,
    ) = gathered
    rows_here, tokens_here, model_width = block_input.shape
    total_rows = rows_here * tokens_here
    block_count = tokens_here // GROUP
    rim_size = conv_weight.shape[0] - 1
    tokens = block_input.astype(jnp.float32).reshape(total_rows, model_width)
    positions = lax.axis_index("seq") * tokens_here + lax.broadcasted_iota(
        jnp.int32, (rows_here, tokens_here), 1
    )
    valid_mask = (positions < valid_length[:, None]).astype(jnp.float32)
    normed, norm_first_back = jax.vjp(root_norm, tokens, gain_first.astype(jnp.float32))
    normed_low = normed.astype(jnp.bfloat16)
    mixed_in = jnp.concatenate(
        [
            project(normed_low, full_query),
            project(normed_low, full_key),
            project(normed_low, full_value),
        ],
        axis=1,
    )
    mixed_rows = mixed_in.reshape(rows_here, tokens_here, -1)
    beta_pre = project(normed_low, full_beta).reshape(rows_here, tokens_here, -1)
    decay_pre = project(normed_low, full_decay).reshape(rows_here, tokens_here, -1)
    gate_pre = project(normed_low, full_gate).reshape(rows_here, tokens_here, -1)
    prev_rim = passed_along(mixed_rows[:, tokens_here - rim_size :, :], "seq", 1)

    def prep_rows(mixed_part, rim_part, beta_part, decay_part, conv_part, log_part, bias_part):

        def prep_per_row(mixed_row, rim_row, beta_row, decay_row, mask_row):
            return prepare(
                mixed_row,
                rim_row,
                beta_row,
                decay_row,
                conv_part,
                log_part,
                bias_part,
                mask_row,
                block_count,
            )

        return jax.vmap(prep_per_row)(mixed_part, rim_part, beta_part, decay_part, valid_mask)

    prepared, prep_back = jax.vjp(
        prep_rows, mixed_rows, prev_rim, beta_pre, decay_pre, conv_weight, decay_log, decay_bias
    )
    query_rows, key_rows, value_rows, beta_rows, log_decay = prepared
    summary, summary_back = jax.vjp(
        jax.vmap(device_summary), key_rows, value_rows, beta_rows, log_decay
    )
    cum_decay, key_solve, pseudo_values, transition, injected, whole_trans, whole_inject = summary
    eye_rows = jnp.broadcast_to(
        jnp.eye(whole_trans.shape[-1], dtype=jnp.float32), whole_trans.shape
    )
    zero_rows = jnp.zeros(whole_inject.shape, jnp.float32)
    prefix = carried_in((whole_trans, whole_inject), "seq", compose_pair, (eye_rows, zero_rows))
    state_in = prefix[1]
    group_outs, outputs_back = jax.vjp(
        jax.vmap(device_outputs),
        query_rows,
        key_rows,
        cum_decay,
        key_solve,
        pseudo_values,
        transition,
        injected,
        state_in,
    )

    def final_rows(outs_part, gate_part, gain_part):

        def final_per_row(out_row, gate_row, mask_row):
            return gated_norm(join_blocks(out_row), gate_row, gain_part, mask_row)

        return jax.vmap(final_per_row)(outs_part, gate_part, valid_mask)

    gated, final_back = jax.vjp(final_rows, group_outs, gate_pre, head_norm_gain)
    mixed_low = gated.reshape(total_rows, -1).astype(jnp.bfloat16)
    second = tokens + back_project(mixed_low, full_out)
    normed_two, norm_second_back = jax.vjp(root_norm, second, gain_second.astype(jnp.float32))
    normed_two_low = normed_two.astype(jnp.bfloat16)
    gate_act = project(normed_two_low, full_ffn_gate)
    up_act = project(normed_two_low, full_ffn_up)
    hidden = (jax.nn.silu(gate_act) * up_act).astype(jnp.bfloat16)
    result = (
        (second + back_project(hidden, full_ffn_down))
        .astype(jnp.bfloat16)
        .reshape(rows_here, tokens_here, model_width)
    )
    grad_branch = output_grad.reshape(total_rows, model_width)
    grad_out = grad_branch.astype(jnp.float32)
    grad_hidden = project(grad_branch, full_ffn_down)
    sigmoid_gate = jax.nn.sigmoid(gate_act)
    grad_gate_low = (
        grad_hidden * up_act * sigmoid_gate * (1.0 + gate_act * (1.0 - sigmoid_gate))
    ).astype(jnp.bfloat16)
    grad_up_low = (grad_hidden * gate_act * sigmoid_gate).astype(jnp.bfloat16)
    grad_normed_two = back_project(grad_gate_low, full_ffn_gate) + back_project(
        grad_up_low, full_ffn_up
    )
    grad_second_norm, grad_gain_second = norm_second_back(grad_normed_two)
    grad_second = grad_out + grad_second_norm
    ffn_widths = [full_ffn_gate.shape[1], full_ffn_up.shape[1], full_ffn_down.shape[1], 1]
    grad_mixed_low = grad_second.astype(jnp.bfloat16)
    grad_gated = project(grad_mixed_low, full_out).reshape(rows_here, tokens_here, -1)
    grad_group_outs, grad_gate_pre, grad_head_gain = final_back(grad_gated)
    (
        grad_query_rows,
        grad_keys_late,
        grad_cum,
        grad_solve,
        grad_pseudo,
        grad_trans,
        grad_inject,
        grad_state,
    ) = outputs_back(grad_group_outs)
    adjoint = entering(
        (jnp.swapaxes(whole_trans, -1, -2), grad_state), "seq", compose_pair, (eye_rows, zero_rows)
    )
    later_adjoint = adjoint[1]
    grad_whole_trans = jnp.einsum("rhik,rhjk->rhij", later_adjoint, state_in, precision=HIGHEST)
    grad_keys_early, grad_value_rows, grad_beta_rows, grad_log_decay = summary_back(
        (
            grad_cum,
            grad_solve,
            grad_pseudo,
            grad_trans,
            grad_inject,
            grad_whole_trans,
            later_adjoint,
        )
    )
    (
        grad_mixed_rows,
        grad_rim,
        grad_beta_pre,
        grad_decay_pre,
        grad_conv,
        grad_decay_log,
        grad_decay_bias,
    ) = prep_back(
        (
            grad_query_rows,
            grad_keys_early + grad_keys_late,
            grad_value_rows,
            grad_beta_rows,
            grad_log_decay,
        )
    )
    returned = passed_along(grad_rim.astype(jnp.bfloat16), "seq", -1).astype(grad_rim.dtype)
    cut_at = tokens_here - rim_size
    grad_mixed_rows = jnp.concatenate(
        [grad_mixed_rows[:, :cut_at, :], grad_mixed_rows[:, cut_at:, :] + returned], axis=1
    )
    grad_mixed_in = grad_mixed_rows.reshape(total_rows, -1)
    query_width = full_query.shape[1]
    key_width = full_key.shape[1]
    grad_query_low = grad_mixed_in[:, :query_width].astype(jnp.bfloat16)
    grad_key_low = grad_mixed_in[:, query_width : query_width + key_width].astype(jnp.bfloat16)
    grad_value_low = grad_mixed_in[:, query_width + key_width :].astype(jnp.bfloat16)
    grad_beta_low = grad_beta_pre.reshape(total_rows, -1).astype(jnp.bfloat16)
    grad_decay_low = grad_decay_pre.reshape(total_rows, -1).astype(jnp.bfloat16)
    grad_gate_pre_low = grad_gate_pre.reshape(total_rows, -1).astype(jnp.bfloat16)
    grad_normed = (
        back_project(grad_query_low, full_query)
        + back_project(grad_key_low, full_key)
        + back_project(grad_value_low, full_value)
    )
    grad_normed = (
        grad_normed
        + back_project(grad_beta_low, full_beta)
        + back_project(grad_decay_low, full_decay)
        + back_project(grad_gate_pre_low, full_gate)
    )
    grad_tokens, grad_gain_first = norm_first_back(grad_normed)
    grad_input = (grad_second + grad_tokens).reshape(rows_here, tokens_here, model_width)
    mixer_widths = [
        full_query.shape[1],
        full_key.shape[1],
        full_value.shape[1],
        full_beta.shape[1],
        full_decay.shape[1],
        full_gate.shape[1],
        full_out.shape[1],
        1,
    ]
    small = lax.psum((grad_head_gain, grad_decay_log, grad_decay_bias, grad_conv), ("seq", "rows"))
    both_summed = lax.psum_scatter(
        jnp.concatenate(
            [
                jnp.concatenate(
                    [
                        outer_sum(normed_low, grad_query_low),
                        outer_sum(normed_low, grad_key_low),
                        outer_sum(normed_low, grad_value_low),
                        outer_sum(normed_low, grad_beta_low),
                        outer_sum(normed_low, grad_decay_low),
                        outer_sum(normed_low, grad_gate_pre_low),
                        outer_sum(grad_mixed_low, mixed_low),
                        vector_slice(grad_gain_first),
                    ],
                    axis=1,
                ),
                jnp.concatenate(
                    [
                        outer_sum(normed_two_low, grad_gate_low),
                        outer_sum(normed_two_low, grad_up_low),
                        outer_sum(grad_branch, hidden),
                        vector_slice(grad_gain_second),
                    ],
                    axis=1,
                ),
            ],
            axis=1,
        ),
        ("seq", "rows"),
        scatter_dimension=0,
        tiled=True,
    )
    mixer_columns = sum(mixer_widths)
    mixer_summed = both_summed[:, :mixer_columns]
    ffn_summed = both_summed[:, mixer_columns:]
    mixer_parts = split_columns(mixer_summed, mixer_widths)
    ffn_parts = split_columns(ffn_summed, ffn_widths)
    return (
        result,
        grad_input,
        mixer_parts[0],
        mixer_parts[1],
        mixer_parts[2],
        mixer_parts[3],
        mixer_parts[4],
        mixer_parts[5],
        mixer_parts[6],
        ffn_parts[0],
        ffn_parts[1],
        ffn_parts[2],
        mixer_parts[7][:, 0],
        ffn_parts[3][:, 0],
        small[0],
        small[1],
        small[2],
        small[3],
    )


def solution(mesh):
    placed = (
        P("rows", "seq", None),
        P("rows"),
        P(("seq", "rows"), None),
        P(("seq", "rows"), None),
        P(("seq", "rows"), None),
        P(("seq", "rows"), None),
        P(("seq", "rows"), None),
        P(("seq", "rows"), None),
        P(("seq", "rows"), None),
        P(("seq", "rows"), None),
        P(("seq", "rows"), None),
        P(("seq", "rows"), None),
        P(("seq", "rows")),
        P(("seq", "rows")),
        P(),
        P(),
        P(),
        P(),
        P("rows", "seq", None),
    )
    return jax.shard_map(
        on_device,
        mesh=mesh,
        in_specs=placed,
        out_specs=(
            P("rows", "seq", None),
            P("rows", "seq", None),
            P(("seq", "rows"), None),
            P(("seq", "rows"), None),
            P(("seq", "rows"), None),
            P(("seq", "rows"), None),
            P(("seq", "rows"), None),
            P(("seq", "rows"), None),
            P(("seq", "rows"), None),
            P(("seq", "rows"), None),
            P(("seq", "rows"), None),
            P(("seq", "rows"), None),
            P(("seq", "rows")),
            P(("seq", "rows")),
            P(),
            P(),
            P(),
            P(),
        ),
        check_vma=False,
    )
```

profile of v0, /device:TPU:0, one launch (start us, length us, event | category | flops | bytes accessed | tf_op | source)
XLA Modules:
  0.0 2158.9 jit_solution(14012925499877476795)
XLA Ops:
  11.8 42.1 %all-reduce.19 = (bf16[1024]{0:T(1024)(128)(2,1)S(1)}, bf16[1024]{0:T(1024)(128)(2,1)S(1)}) all-reduce(bf16[1024]{0:T(1024)(128)(2,1)S(1)} %dynamic-update-slice, bf16[1024]{0:T(1024)(128)(2,1)S(1)} %dynamic-update-slice.1), channel_id=1, replica_groups=mesh['seq'=4,'rows'=8] {'seq','rows'}, use_global_device_ids=true, to_apply=%add.16 | all-reduce | flops 2048 | bytes 8192
  53.9 40.9 %all-gather.4 = bf16[32,32,8]{1,2,0:T(8,128)(2,1)S(1)} all-gather(bf16[1,32,8]{1,2,0:T(8,128)(2,1)} %bitcast.1057), channel_id=1, replica_groups=mesh['seq'=4,'rows'=8] {'seq','rows'}, dimensions={0}, use_global_device_ids=true | all-gather | bytes 16896 | tf_op jit(solution)/shard_map/all_gather | solution.py:312
  94.9 37.6 %all-gather.5 = bf16[32,32,16]{1,2,0:T(8,128)(2,1)S(1)} all-gather(bf16[1,32,16]{1,2,0:T(8,128)(2,1)} %bitcast.1056), channel_id=1, replica_groups=mesh['seq'=4,'rows'=8] {'seq','rows'}, dimensions={0}, use_global_device_ids=true | all-gather | bytes 33792 | tf_op jit(solution)/shard_map/all_gather | solution.py:311
  146.4 52.0 %all-gather.23.cloned.1.call-done = bf16[1024,2048]{1,0:T(8,128)(2,1)} async-done(((bf16[32,2048]{1,0:T(8,128)(2,1)}), bf16[1024,2048]{1,0:T(8,128)(2,1)}) %all-gather.23.cloned.1.call-update) | async-done | bytes 4194320 | tf_op jit(solution)/shard_map/all_gather | solution.py:310
  207.9 5.3 fusion.135
  221.4 4.6 fusion.158
  229.6 316.0 %custom-call.10 = f32[1,4,8,1,128,128]{4,5,3,2,1,0:T(8,128)} custom-call(f32[1,4,8,1,128,128]{5,4,3,2,1,0:T(8,128)} %select_bitcast_fusion), custom_call_target="InvertDiagBlocksLowerTriangular" | custom-call | tf_op jit(solution)/shard_map/jvp(vmap(vmap(vmap(jit(_solve_triangular)))))/triangular_solve | solution.py:89
  553.7 5.5 fusion.196
  559.2 6.0 fusion.190
  569.3 21.9 %while.127 = (s32[]{:T(128)}, f32[1,8,128,128]{3,2,1,0:T(8,128)S(1)}, f32[1,8,128,128]{3,2,1,0:T(8,128)}, f32[4,1,8,128,128]{4,3,2,1,0:T(8,128)}, f32[4,1,8,128,...) while((s32[]{:T(128)}, ...), condition=%wide.region_4.5_spmd, body=%wide.region_3.4_spmd.sunk | while | flops 402784256 | bytes 16254081 | solution.py:217
  609.5 4.7 slice_bitcast_fusion.3
  614.3 13.0 all-gather.37.cloned.1.call-done
  627.3 37.0 %all-gather.35.cloned.1.call-done = f32[4,8,128,128]{3,2,1,0:T(8,128)} async-done(((f32[1,8,128,128]{3,2,1,0:T(8,128)}), f32[4,8,128,128]{3,2,1,0:T(8,128)}) %all-gather.35.cloned.1.call-update) | async-done | bytes 2097168 | tf_op jit(solution)/shard_map/all_gather | solution.py:23
  668.4 57.3 %while.131 = (s32[]{:T(128)}, f32[1,8,128,128]{3,2,1,0:T(8,128)}, f32[4,1,8,64,128]{4,3,2,1,0:T(8,128)}, f32[4,1,8,64,128]{4,3,2,1,0:T(8,128)}, f32[4,1,8,64,128...) while((s32[]{:T(128)}, f32[1,8,128,128]{3,2,1,0:T(8,128)}, ...), condition=%wide.region_9.10_spmd.clone.clone, body=%wide.region_8.9_spmd.clone.clone.sunk | while | flops 705757184 | bytes 11625177 | solution.py:234
  736.1 46.0 %all-gather.27.cloned.1.call-done = bf16[1024,1024]{1,0:T(8,128)(2,1)} async-done(((bf16[32,1024]{1,0:T(8,128)(2,1)}), bf16[1024,1024]{1,0:T(8,128)(2,1)}) %all-gather.27.cloned.1.call-update) | async-done | bytes 2097168 | tf_op jit(solution)/shard_map/all_gather | solution.py:314
  785.6 65.5 %all-gather.31.cloned.1.call-done = bf16[1024,2816]{1,0:T(8,128)(2,1)} async-done(((bf16[32,2816]{1,0:T(8,128)(2,1)}), bf16[1024,2816]{1,0:T(8,128)(2,1)}) %all-gather.31.cloned.1.call-update) | async-done | bytes 5767184 | tf_op jit(solution)/shard_map/all_gather | solution.py:316
  851.1 5.9 fusion.362
  856.9 63.3 %all-gather.29.cloned.1.call-done = bf16[1024,2816]{1,0:T(8,128)(2,1)} async-done(((bf16[32,2816]{1,0:T(8,128)(2,1)}), bf16[1024,2816]{1,0:T(8,128)(2,1)}) %all-gather.29.cloned.1.call-update) | async-done | bytes 5767184 | tf_op jit(solution)/shard_map/all_gather | solution.py:315
  920.3 5.9 fusion.361
  926.1 63.2 %all-gather.33.cloned.1.call-done = bf16[1024,2816]{1,0:T(8,128)(2,1)} async-done(((bf16[32,2816]{1,0:T(8,128)(2,1)}), bf16[1024,2816]{1,0:T(8,128)(2,1)}) %all-gather.33.cloned.1.call-update) | async-done | bytes 5767184 | tf_op jit(solution)/shard_map/all_gather | solution.py:317
  989.3 8.1 multiply_convert_fusion
  999.4 4.7 multiply_reduce_fusion.9
  1021.4 101.2 %while.132 = (s32[]{:T(128)}, f32[1,8,128,128]{3,2,1,0:T(8,128)S(1)}, f32[4,1,8,64,128]{4,3,0,2,1:T(8,128)}, f32[4,1,8,128,128]{4,3,2,1,0:T(8,128)}, f32[4,1,8,1...) while((s32[]{:T(128)}, ...), condition=%wide.region_18.19_spmd.clone.clone, body=%wide.region_14.18_spmd.clone.clone.sunk | while | flops 1410663424 | bytes 30732652 | solution.py:234
  1128.2 6.0 fusion.366
  1145.6 5.9 fusion.365
  1151.6 5.9 convolution_bitcast_fusion.7
  1160.1 4.6 while.129
  1170.9 38.5 %while.130 = (s32[]{:T(128)}, f32[1,8,128,128]{3,2,1,0:T(8,128)}, f32[1,8,128,128]{3,2,1,0:T(8,128)S(1)}, f32[4,1,8,128,128]{3,4,2,1,0:T(8,128)}, f32[4,1,8,128,...) while((s32[]{:T(128)}, f32[1,8,128,128]{3,2,1,0:T(8,128)}, ...), condition=%wide.region_22.23_spmd, body=%wide.region_21.22_spmd.sunk | while | flops 805437440 | bytes 18351260 | solution.py:217
  1209.5 5.2 fusion.160
  1214.8 4.8 bitcast_add_fusion.1
  1223.7 6.3 fusion.139
  1230.1 4.3 fusion.144
  1234.4 4.5 fusion.205
  1246.5 8.6 fusion.227
  1265.8 5.0 reduce_window_sum.26
  1280.1 5.0 fusion.154
  1285.1 7.5 fusion.152
  1298.7 4.3 add_add_fusion
  1306.0 15.8 multiply_reduce_fusion.3
  1321.8 11.0 broadcast_multiply_fusion
  1332.9 8.2 pad_add_fusion
  1350.1 4.7 fusion.279
  1354.8 4.6 fusion.275
  1366.9 71.4 %concatenate.42 = f32[1024,15642]{1,0:T(8,128)} concatenate(f32[1024,1024]{1,0:T(8,128)} %fusion.291, f32[1024,2048]{1,0:T(8,128)} %fusion.279, f32[1024,2048]{1,0:T(8,128)} %fusion.275, f32[1024,16]{1,0:T(8,128)S(1)} %fusion.308, f32[1024,8]{1,0:T(8,128)S(1)} %fusion.306, f32[1024,1024]{1,0:T(8,128)} %fusion.332, f32[1024,1024]{1,0:T(8,128)} %fusion.302, f32[1024,1]{1,0:T(8,128)S(1)} %copy.501, ...), dimensions={1} | concatenate | bytes 128139264 | tf_op jit(solution)/shard_map/concatenate | solution.py:522
  1439.6 5.6 fusion.225
  1445.9 39.4 %all-reduce.18 = (f32[128]{0:T(128)}, f32[8]{0:T(128)}, f32[8]{0:T(128)}) all-reduce(f32[128]{0:T(128)S(1)} %copy-done.110, f32[8]{0:T(128)S(1)} %negate_multiply_fusion, f32[8]{0:T(128)S(1)} %get-tuple-element.2007), channel_id=1, replica_groups=mesh['seq'=4,'rows'=8] {'seq','rows'}, use_global_device_ids=true, to_apply=%region_39.40 | all-reduce | flops 144 | bytes 1152 | tf_op jit(solution)/shard_map/psum | solution.py:520
  1488.0 536.5 %reduce-scatter.2.cloned.1.call-done = f32[32,15642]{1,0:T(8,128)} async-done(((f32[1024,15642]{1,0:T(8,128)}), f32[32,15642]{1,0:T(8,128)}) %reduce-scatter.2.cloned.1.call-update) | async-done | bytes 2002192 | tf_op jit(solution)/shard_map/reduce_scatter | solution.py:521
  2033.0 117.7 %all-reduce.22.cloned.1.call-done = f32[4,5120]{1,0:T(4,128)} async-done(((f32[4,5120]{1,0:T(4,128)}), f32[4,5120]{1,0:T(4,128)}) %all-reduce.22.cloned.1.call-update) | async-done | bytes 81936 | tf_op jit(solution)/shard_map/psum | solution.py:520
  (646 shorter events, 425.4 us)
Async XLA Ops:
  7.2 128.4 %copy-start.2 = (bf16[1,256,1024]{2,1,0:T(8,128)(2,1)S(1)}, bf16[1,256,1024]{2,1,0:T(8,128)(2,1)}, u32[]{:S(2)}) copy-start(bf16[1,256,1024]{2,1,0:T(8,128)(2,1)} %param.31) | copy-start | bytes 1572868
  7.2 128.4 %copy-start.115 = (f32[8]{0:T(128)S(1)}, f32[8]{0:T(128)}, u32[]{:S(2)}) copy-start(f32[8]{0:T(128)} %param.46) | copy-start | bytes 100
  7.2 128.4 %copy-start.114 = (f32[8]{0:T(128)S(1)}, f32[8]{0:T(128)}, u32[]{:S(2)}) copy-start(f32[8]{0:T(128)} %param.47) | copy-start | bytes 100
  7.2 132.2 %all-gather.19.cloned.1.call-start = ((), (), s32[]{:S(2)}) async-start(), calls=%async_computation.1 | async-start | bytes 2162688 | tf_op jit(solution)/shard_map/all_gather | solution.py:308
  8.0 134.8 %all-gather.21.cloned.1.call-start = ((), (), s32[]{:S(2)}) async-start(), calls=%async_computation.2 | async-start | bytes 4325376 | tf_op jit(solution)/shard_map/all_gather | solution.py:309
  8.7 189.7 %all-gather.23.cloned.1.call-start = ((), (), s32[]{:S(2)}) async-start(), calls=%async_computation.3 | async-start | bytes 4325376 | tf_op jit(solution)/shard_map/all_gather | solution.py:310
  9.4 617.9 %all-gather.37.cloned.1.call-start = ((), (), s32[]{:S(2)}) async-start(), calls=%async_computation.12 | async-start | bytes 2621440 | tf_op jit(solution)/shard_map/all_gather | solution.py:23
  94.9 43.6 %copy-start.97 = (bf16[1024,8]{0,1:T(8,128)(2,1)}, bf16[1024,8]{0,1:T(8,128)(2,1)S(1)}, u32[]{:S(2)}) copy-start(bf16[1024,8]{0,1:T(8,128)(2,1)S(1)} %reshape.1714) | copy-start | bytes 49156
  139.0 408.5 %copy-start.88 = (f32[4,8,128]{2,1,0:T(8,128)}, f32[4,8,128]{2,1,0:T(8,128)S(1)}, u32[]{:S(2)}) copy-start(f32[4,8,128]{2,1,0:T(8,128)S(1)} %copy.426) | copy-start | bytes 49156
  139.2 408.4 %copy-start.73 = (f32[4,8,128]{2,1,0:T(8,128)}, f32[4,8,128]{2,1,0:T(8,128)S(1)}, u32[]{:S(2)}) copy-start(f32[4,8,128]{2,1,0:T(8,128)S(1)} %copy.423) | copy-start | bytes 49156
  139.2 457.0 %copy-start.101 = (f32[4,8]{1,0:T(4,128)}, f32[4,8]{1,0:T(4,128)S(1)}, u32[]{:S(2)}) copy-start(f32[4,8]{1,0:T(4,128)S(1)} %slice_bitcast_fusion.7) | copy-start | bytes 388
  139.4 68.5 %copy-start.78 = (f32[1,5120]{1,0:T(1,128)}, f32[1,5120]{1,0:T(1,128)S(1)}, u32[]{:S(2)}) copy-start(f32[1,5120]{1,0:T(1,128)S(1)} %get-tuple-element.2056) | copy-start | bytes 61444
  139.4 68.5 %copy-start.80 = (f32[1,5120]{1,0:T(1,128)}, f32[1,5120]{1,0:T(1,128)S(1)}, u32[]{:S(2)}) copy-start(f32[1,5120]{1,0:T(1,128)S(1)} %get-tuple-element.2057) | copy-start | bytes 61444
  139.4 68.5 %copy-start.82 = (f32[1,5120]{1,0:T(1,128)}, f32[1,5120]{1,0:T(1,128)S(1)}, u32[]{:S(2)}) copy-start(f32[1,5120]{1,0:T(1,128)S(1)} %get-tuple-element.2058) | copy-start | bytes 61444
  139.4 68.5 %copy-start.84 = (f32[1,5120]{1,0:T(1,128)}, f32[1,5120]{1,0:T(1,128)S(1)}, u32[]{:S(2)}) copy-start(f32[1,5120]{1,0:T(1,128)S(1)} %get-tuple-element.2059) | copy-start | bytes 61444
  146.4 61.5 %copy-start.17 = (f32[256,2048]{1,0:T(8,128)}, f32[256,2048]{1,0:T(8,128)S(1)}, u32[]{:S(2)}) copy-start(f32[256,2048]{1,0:T(8,128)S(1)} %fusion.342) | copy-start | bytes 6291460
  202.6 10.6 copy-start.5
  202.6 5.3 collective-permute-start
  206.3 19.7 copy-start.90
  206.3 19.7 copy-start.92
  591.2 73.2 %all-gather.35.cloned.1.call-start = ((), (), s32[]{:S(2)}) async-start(), calls=%async_computation.11 | async-start | bytes 2621440 | tf_op jit(solution)/shard_map/all_gather | solution.py:23
  592.0 138.3 %all-gather.25.cloned.1.call-start = ((), (), s32[]{:S(2)}) async-start(), calls=%async_computation.4 | async-start | bytes 2162688 | tf_op jit(solution)/shard_map/all_gather | solution.py:313
  592.5 189.5 %all-gather.27.cloned.1.call-start = ((), (), s32[]{:S(2)}) async-start(), calls=%async_computation.5 | async-start | bytes 2162688 | tf_op jit(solution)/shard_map/all_gather | solution.py:314
  593.3 257.8 %all-gather.31.cloned.1.call-start = ((), (), s32[]{:S(2)}) async-start(), calls=%async_computation.7 | async-start | bytes 5947392 | tf_op jit(solution)/shard_map/all_gather | solution.py:316
  594.0 326.2 %all-gather.29.cloned.1.call-start = ((), (), s32[]{:S(2)}) async-start(), calls=%async_computation.6 | async-start | bytes 5947392 | tf_op jit(solution)/shard_map/all_gather | solution.py:315
  594.8 394.5 %all-gather.33.cloned.1.call-start = ((), (), s32[]{:S(2)}) async-start(), calls=%async_computation.8 | async-start | bytes 5947392 | tf_op jit(solution)/shard_map/all_gather | solution.py:317
  595.4 562.1 %all-gather.39.cloned.1.call-start = ((), (), s32[]{:S(2)}) async-start(), calls=%async_computation.13 | async-start | bytes 1310720 | tf_op jit(solution)/shard_map/all_gather | solution.py:39
  614.3 545.8 %all-gather.41.cloned.1.call-start = ((), (), s32[]{:S(2)}) async-start(), calls=%async_computation.14 | async-start | bytes 1310720 | tf_op jit(solution)/shard_map/all_gather | solution.py:39
  733.9 50.6 %copy-start.61 = (bf16[256,1024]{1,0:T(8,128)(2,1)}, bf16[256,1024]{1,0:T(8,128)(2,1)S(1)}, u32[]{:S(2)}) copy-start(bf16[256,1024]{1,0:T(8,128)(2,1)S(1)} %get-tuple-element.2063) | copy-start | bytes 1572868
  785.6 134.7 %copy-start.45 = (bf16[256,1024]{1,0:T(8,128)(2,1)}, bf16[256,1024]{1,0:T(8,128)(2,1)S(1)}, u32[]{:S(2)}) copy-start(bf16[256,1024]{1,0:T(8,128)(2,1)S(1)} %multiply_convert_fusion.3) | copy-start | bytes 1572868
  989.3 8.1 copy-start.111
  1134.2 890.2 %reduce-scatter.2.cloned.1.call-start = ((), (), s32[]{:S(2)}) async-start(), calls=%async_computation.9 | async-start | bytes 66502656 | tf_op jit(solution)/shard_map/reduce_scatter | solution.py:521
  1246.5 15.6 copy-start.52
  1246.5 15.6 copy-start.50
  1246.5 15.6 copy-start.72
  1260.5 10.5 copy-start.104
  1260.5 10.5 copy-start.109
  1262.1 10.5 copy-start.100
  1306.0 15.8 copy-start.79
  1306.0 15.8 copy-start.81
  1306.0 15.8 copy-start.83
  1306.0 15.8 copy-start.85
  1341.1 5.9 collective-permute-start.1
  1438.4 7.5 copy-start.110
  1438.4 46.9 %copy-start.106 = (f32[256]{0:T(256)S(1)}, f32[256]{0:T(256)}, u32[]{:S(2)}) copy-start(f32[256]{0:T(256)} %copy-done.105) | copy-start | bytes 3076
  1438.4 46.9 %copy-start.35 = (f32[256,1024]{1,0:T(8,128)S(1)}, f32[256,1024]{1,0:T(8,128)}, u32[]{:S(2)}) copy-start(f32[256,1024]{1,0:T(8,128)} %copy-done.34) | copy-start | bytes 3145732
  1438.4 712.2 %all-reduce.22.cloned.1.call-start = ((), (), s32[]{:S(2)}) async-start(), calls=%async_computation.10 | async-start | bytes 163840 | tf_op jit(solution)/shard_map/psum | solution.py:520
  2024.4 7.9 slice-start
  (101 other events, 365.9 us)
Sparse Core Ops, SparseCore 0:
  11.0 59.3 all-gather.18
  73.4 61.0 all-gather.20
  137.5 60.8 all-gather.22
  591.3 35.9 all-gather.36
  629.0 35.2 all-gather.34
  667.2 56.4 all-gather.24
  726.7 55.3 all-gather.26
  784.9 66.1 all-gather.30
  853.9 66.2 all-gather.28
  923.0 66.2 all-gather.32
  991.7 25.5 all-gather.38
  1134.3 25.6 all-gather.40
  1438.5 585.9 reduce-scatter.1
  2031.4 119.2 all-reduce.21
where the time goes:
time: 2170 us; the launch traced here: 2160 us
  waiting for transfers between devices  1010 us (47%)
  other arithmetic  407 us (19%)
  matrix products  359 us (17%)
  local copies, waits for them, and re-layouts  202 us (9%)
  blocking collectives  160 us (7%)
    reduce_scatter x1, waiting for transfers between devices, on_device(): lax.psum_scatter(jnp.concatenate([jnp.concatenate([outer_sum(normed_low,...  536 us
    another operation x2, other arithmetic, lower_solve(): return jax.scipy.linalg.solve_triangular(matrix, right_side, lower=True)  318 us
    psum x1, waiting for transfers between devices, on_device(): lax.psum((grad_head_gain, grad_decay_log, grad_decay_bias, grad_conv), ('...  118 us
    dot_general x39, matrix products, batched_product(): jnp.einsum('...ij,...jk->...ik', matrix_one, matrix_two, precision=HIGHEST)  72.9 us
    concatenate x1, local copies, waits for them, and re-layouts, on_device(): jnp.concatenate([jnp.concatenate([outer_sum(normed_low, grad_query_low),...  71.4 us
    all_gather x1, waiting for transfers between devices, on_device(): lax.all_gather(ffn_up_weight, ('seq', 'rows'), axis=0, tiled=True)  65.5 us
    all_gather x1, waiting for transfers between devices, on_device(): lax.all_gather(ffn_gate_weight, ('seq', 'rows'), axis=0, tiled=True)  63.3 us
    all_gather x1, waiting for transfers between devices, on_device(): lax.all_gather(ffn_down_weight, ('seq', 'rows'), axis=0, tiled=True)  63.2 us
  transfers between devices with their start and end apart: 16, of which 12 were waited for; matrix products, arithmetic and copies ran while one was open for 14% of the time, Pallas kernels for 0%

commit v1 on v0

v1 whole, which is shorter than its diff:
```python
import functools

import jax
import jax.numpy as jnp
from jax import lax
from jax.experimental import pallas as pl
from jax.experimental.pallas import tpu as pltpu
from jax.sharding import PartitionSpec as P

GROUP = 64
EPS_NORM = 1e-06
EPS_KEY = 1e-06
EPS_HEAD = 1e-05
LOW = jnp.bfloat16
F32 = jnp.float32
HIGHEST = lax.Precision.HIGHEST
BOTH = ("seq", "rows")

FORMS = {
    "nn": (((1,), (0,)), ((), ())),
    "nt": (((1,), (1,)), ((), ())),
    "tn": (((0,), (0,)), ((), ())),
}


def split_low(a):
    high = a.astype(LOW)
    return high, (a - high.astype(F32)).astype(LOW)


def mm(a, b, form):
    a_axis = 0 if form == "tn" else 1
    b_axis = 1 if form == "nt" else 0
    a_two = jnp.concatenate(split_low(a), axis=a_axis)
    b_high, b_low = split_low(b)
    b_two = jnp.concatenate([b_high, b_low], axis=1 - b_axis)
    b_two = jnp.concatenate([b_two, b_two], axis=b_axis)
    out = lax.dot_general(a_two, b_two, FORMS[form], preferred_element_type=F32)
    half = out.shape[1] // 2
    return out[:, :half] + out[:, half:]


def mm_low(a, b, form):
    return lax.dot_general(a.astype(LOW), b.astype(LOW), FORMS[form], preferred_element_type=F32)


def mm_high(a, b, form):
    return lax.dot_general(a, b, FORMS[form], precision=HIGHEST, preferred_element_type=F32)


def row_dot(a, b):
    return jnp.sum(a * b, axis=1, keepdims=True)


def place(shape, axis):
    return lax.broadcasted_iota(jnp.int32, shape, axis)


def level_table():
    time = 2 * (jnp.arange(2 * GROUP) % GROUP) + jnp.arange(2 * GROUP) // GROUP
    row, col = time[:, None], time[None, :]
    differ = row ^ col
    level = sum((differ >= 2**m).astype(jnp.int32) for m in range(1, 7))
    return jnp.where(row > col, level, -1)


def inverses(systems, level):
    size = level.shape[0]
    eye = (place((size, size), 0) == place((size, size), 1)).astype(F32)
    found = [eye - jnp.where(level == 0, a, 0.0) for a in systems]
    for m in range(1, 7):
        inner = [mm(jnp.where(level == m, a, 0.0), t, "nn") for a, t in zip(systems, found)]
        found = [t - mm(t, s, "nn") for t, s in zip(found, inner)]
    return found


def conv_active(pad_ref, taps_ref, first, count):
    cols = slice(first, first + 128)
    summed = 0.0
    for back in range(4):
        summed = summed + pad_ref[pl.ds(8 - back, count), cols] * taps_ref[3 - back : 4 - back, cols]
    return summed


def silu(x):
    return x * jax.nn.sigmoid(x)


def softplus(x):
    return jnp.maximum(x, 0.0) + jnp.log1p(jnp.exp(-jnp.abs(x)))


def cum_decays(log_decay):
    tril = (place((GROUP, GROUP), 0) >= place((GROUP, GROUP), 1)).astype(F32)
    across = (place((GROUP, 2 * GROUP), 0) <= place((GROUP, 2 * GROUP), 1) % GROUP).astype(F32)
    return mm_high(tril, log_decay, "nn"), mm_high(log_decay, across, "tn")


def twice(a):
    return jnp.concatenate([a, a], axis=0)


def group_setup(level, beta, cum, across, head, heads):
    lane = 2 * heads + head
    c = cum[:, lane : lane + 1]
    row = across[lane : lane + 1, :]
    c_two = twice(c)
    end = c[GROUP - 1 : GROUP, :]
    b = jnp.concatenate([beta[:, head : head + 1], beta[:, heads + head : heads + head + 1]], axis=0)
    strict = level >= 0
    pair = jnp.where(strict, jnp.exp(jnp.where(strict, c_two - row, 0.0)), 0.0)
    seen = place((GROUP, 2 * GROUP), 1) % GROUP <= place((GROUP, 2 * GROUP), 0)
    view = jnp.where(seen, jnp.exp(jnp.where(seen, c - row, 0.0)), 0.0)
    return c, c_two, end, b, pair, view


def forward_kernel(
    heads, length_ref, mixed_ref, halo_ref, gate_ref, taps_ref, small_ref, level_ref,
    out_ref, raw_ref, solve_ref, fresh_ref, state_ref, carried, padded,
):
    step = pl.program_id(0)
    count = mixed_ref.shape[0]
    groups = count // GROUP
    wide = heads * 128

    @pl.when(step == 0)
    def _():
        carried[...] = jnp.zeros_like(carried)

    padded[0:8, :] = jnp.where(step > 0, halo_ref[:, : 5 * wide], 0.0)
    padded[8 : 8 + count, :] = mixed_ref[:, : 5 * wide]
    valid = (step * count + place((count, 1), 0) < length_ref[0]).astype(F32)
    level = level_ref[...]
    tail = mixed_ref[:, 5 * wide :]
    beta = jax.nn.sigmoid(tail) * valid
    log_decay = small_ref[0:1, :] * softplus(tail + small_ref[1:2, :]) * valid

    def active(slot, head):
        return silu(conv_active(padded, taps_ref, slot * wide + head * 128, count))

    def unit(x):
        return x * lax.rsqrt(row_dot(x, x) + EPS_KEY)

    queries = [unit(active(0, h)) * 128**-0.5 for h in range(heads)]
    keys = [[unit(active(1 + j, h)) for j in range(2)] for h in range(heads)]
    values = [[active(3 + j, h) for j in range(2)] for h in range(heads)]
    work = []
    for g in range(groups):
        rows = slice(g * GROUP, (g + 1) * GROUP)
        cum, across = cum_decays(log_decay[rows])
        for h in range(heads):
            key = jnp.concatenate([keys[h][0][rows], keys[h][1][rows]], axis=0)
            value = jnp.concatenate([values[h][0][rows], values[h][1][rows]], axis=0)
            c, c_two, end, b, pair, view = group_setup(level, beta[rows], cum, across, h, heads)
            gram = mm(key, key, "nt")
            work.append((g, h, rows, key, value, c, c_two, end, b, view, b * pair * gram))
    solves = inverses([w[-1] for w in work], level)
    raws = [[None] * groups for _ in range(heads)]
    ready = []
    for (g, h, rows, key, value, c, c_two, end, b, view, _), solve in zip(work, solves):
        solve_ref[g, h] = solve
        query = queries[h][rows]
        weights = view * mm(query, key, "nt")
        key_solve = mm(solve, b * jnp.exp(c_two) * key, "nn")
        pseudo = mm(solve, b * value, "nn")
        ready.append((query, weights, key_solve, pseudo))
    for (g, h, rows, key, value, c, c_two, end, b, view, _), made in zip(work, ready):
        query, weights, key_solve, pseudo = made
        state = carried[h]
        state_ref[g, h] = state
        fresh = pseudo - mm(key_solve, state, "nn")
        fresh_ref[g, h] = fresh
        carried[h] = jnp.exp(end) * state + mm(jnp.exp(end - c_two) * key, fresh, "tn")
        raws[h][g] = jnp.exp(c) * mm(query, state, "nn") + mm(weights, fresh, "nn")
    for h in range(heads):
        cols = slice(h * 128, (h + 1) * 128)
        raw = jnp.concatenate(raws[h], axis=0)
        raw_ref[:, cols] = raw
        scale = lax.rsqrt(jnp.mean(raw * raw, axis=1, keepdims=True) + EPS_HEAD)
        gated = raw * scale * small_ref[2:3, :] * silu(gate_ref[:, cols]) * valid
        out_ref[:, cols] = gated.astype(LOW)


def backward_kernel(
    heads, length_ref, mixed_ref, halo_ref, gate_ref, raw_ref, grad_ref, taps_ref, small_ref, level_ref,
    solve_ref, fresh_ref, state_ref,
    grad_mixed_ref, grad_gate_ref, grad_taps_ref, grad_small_ref,
    carried, padded, spread,
):
    step = pl.program_id(0)
    block = pl.num_programs(0) - 1 - step
    count = mixed_ref.shape[0]
    groups = count // GROUP
    wide = heads * 128

    @pl.when(step == 0)
    def _():
        carried[...] = jnp.zeros_like(carried)
        spread[...] = jnp.zeros_like(spread)
        grad_taps_ref[...] = jnp.zeros_like(grad_taps_ref)
        grad_small_ref[...] = jnp.zeros_like(grad_small_ref)

    spread[count : count + 8, :] = spread[0:8, :]
    padded[0:8, :] = jnp.where(block > 0, halo_ref[:, : 5 * wide], 0.0)
    padded[8 : 8 + count, :] = mixed_ref[:, : 5 * wide]
    valid = (block * count + place((count, 1), 0) < length_ref[0]).astype(F32)
    level = level_ref[...]
    strict = level >= 0
    tail = mixed_ref[:, 5 * wide :]
    sigmoid_tail = jax.nn.sigmoid(tail)
    beta = sigmoid_tail * valid
    log_decay = small_ref[0:1, :] * softplus(tail + small_ref[1:2, :]) * valid
    lanes = place((1, 128), 1)

    grad_raws = []
    for h in range(heads):
        cols = slice(h * 128, (h + 1) * 128)
        raw, gate = raw_ref[:, cols], gate_ref[:, cols]
        grad = grad_ref[:, cols] * valid
        sig = jax.nn.sigmoid(gate)
        scale = lax.rsqrt(jnp.mean(raw * raw, axis=1, keepdims=True) + EPS_HEAD)
        shaped = raw * scale
        gain = small_ref[2:3, :]
        grad_gate_ref[:, cols] = (grad * shaped * gain * sig * (1.0 + gate * (1.0 - sig))).astype(LOW)
        grad_normed = grad * gate * sig
        grad_small_ref[2:3, :] += jnp.sum(grad_normed * shaped, axis=0, keepdims=True)
        grad_shaped = grad_normed * gain
        grad_raws.append(scale * (grad_shaped - shaped * jnp.mean(grad_shaped * shaped, axis=1, keepdims=True)))

    def summed(slot, head):
        return conv_active(padded, taps_ref, slot * wide + head * 128, count)

    def unit(x):
        return x * lax.rsqrt(row_dot(x, x) + EPS_KEY)

    queries = [unit(silu(summed(0, h))) * 128**-0.5 for h in range(heads)]
    keys = [[unit(silu(summed(1 + j, h))) for j in range(2)] for h in range(heads)]
    values = [[silu(summed(3 + j, h)) for j in range(2)] for h in range(heads)]
    work = []
    for g in reversed(range(groups)):
        rows = slice(g * GROUP, (g + 1) * GROUP)
        cum, across = cum_decays(log_decay[rows])
        for h in range(heads):
            key = jnp.concatenate([keys[h][0][rows], keys[h][1][rows]], axis=0)
            value = jnp.concatenate([values[h][0][rows], values[h][1][rows]], axis=0)
            c, c_two, end, b, pair, view = group_setup(level, beta[rows], cum, across, h, heads)
            query, grad_raw = queries[h][rows], grad_raws[h][rows]
            scores = view * mm(query, key, "nt")
            late = mm(scores, grad_raw, "tn")
            grad_scores = view * mm(grad_raw, fresh_ref[g, h], "nt")
            work.append((g, h, rows, key, value, c, c_two, end, b, pair, query, grad_raw, late, grad_scores))
    grad_parts = [[[None] * groups for _ in range(5)] for _ in range(heads)]
    grad_betas, grad_cums = [0.0] * groups, [0.0] * groups
    for (g, h, rows, key, value, c, c_two, end, b, pair, query, grad_raw, late, grad_scores) in work:
        state, fresh, solve = state_ref[g, h], fresh_ref[g, h], solve_ref[g, h]
        grad_state = carried[h]
        grow, fade, all_fade = jnp.exp(c_two), jnp.exp(end - c_two), jnp.exp(end)
        grad_seen = jnp.exp(c) * grad_raw
        grad_fresh = late + mm(fade * key, grad_state, "nn")
        adjoint = mm(solve, grad_fresh, "tn")
        carried[h] = (
            all_fade * grad_state
            + mm(query, grad_seen, "tn")
            - mm(b * grow * key, adjoint, "tn")
        )
        grad_query = mm(grad_seen, state, "nt") + mm(grad_scores, key, "nn")
        part_one = mm(grad_scores, query, "tn")
        part_two = fade * mm(fresh, grad_state, "nt")
        part_three = -mm(adjoint, state, "nt")
        coupled = jnp.where(strict, -mm(adjoint, fresh, "nt"), 0.0) * pair
        part_four = mm(coupled, key, "nn")
        part_five = mm(b * coupled, key, "tn")
        grad_key = part_one + part_two + b * grow * part_three + b * part_four + part_five
        grad_value = b * adjoint
        through = grow * row_dot(part_three, key)
        pulled = row_dot(part_four, key)
        grad_b = row_dot(adjoint, value) + through + pulled
        ends = row_dot(part_two, key)
        grad_c = b * (through + pulled) - ends - row_dot(part_one + part_five, key)
        grad_c = row_dot(query, grad_query) + grad_c[:GROUP] + grad_c[GROUP:]
        grad_end = jnp.sum(ends) + jnp.sum(all_fade * grad_state * state)
        grad_c = grad_c + jnp.where(place((GROUP, 1), 0) == GROUP - 1, grad_end, 0.0)
        grad_cums[g] = grad_cums[g] + jnp.where(lanes == 2 * heads + h, grad_c, 0.0)
        for j in range(2):
            half = slice(j * GROUP, (j + 1) * GROUP)
            grad_betas[g] = grad_betas[g] + jnp.where(lanes == j * heads + h, grad_b[half], 0.0)
            grad_parts[h][1 + j][g] = grad_key[half]
            grad_parts[h][3 + j][g] = grad_value[half]
        grad_parts[h][0][g] = grad_query
    triu = (place((GROUP, GROUP), 0) <= place((GROUP, GROUP), 1)).astype(F32)
    grad_log = jnp.concatenate([mm_high(triu, x, "nn") for x in grad_cums], axis=0)
    grad_beta = jnp.concatenate(grad_betas, axis=0)
    grad_decay = grad_log * small_ref[0:1, :] * valid * jax.nn.sigmoid(tail + small_ref[1:2, :])
    grad_mixed_ref[:, 5 * wide :] = (
        grad_beta * beta * (1.0 - sigmoid_tail) + grad_decay
    ).astype(LOW)
    grad_small_ref[0:1, :] += jnp.sum(grad_log * log_decay, axis=0, keepdims=True)
    grad_small_ref[1:2, :] += jnp.sum(grad_decay, axis=0, keepdims=True)

    for h in range(heads):
        for slot in range(5):
            cols = slice(slot * wide + h * 128, slot * wide + (h + 1) * 128)
            grad = jnp.concatenate(grad_parts[h][slot], axis=0)
            pre = summed(slot, h)
            sig = jax.nn.sigmoid(pre)
            if slot < 3:
                act = pre * sig
                scale = lax.rsqrt(row_dot(act, act) + EPS_KEY)
                shaped = act * scale
                if slot == 0:
                    grad = grad * 128**-0.5
                grad = scale * (grad - shaped * row_dot(grad, shaped))
            grad = grad * sig * (1.0 + pre * (1.0 - sig))
            spread[0:count, cols] = grad
            back = 0.0
            for ahead in range(4):
                back = back + spread[pl.ds(ahead, count), cols] * taps_ref[3 - ahead : 4 - ahead, cols]
            grad_mixed_ref[:, cols] = back.astype(LOW)
            for tap in range(4):
                grad_taps_ref[tap : tap + 1, cols] += jnp.sum(
                    grad * padded[pl.ds(5 + tap, count), cols], axis=0, keepdims=True
                )


def step_tokens(tokens):
    return min(128, tokens)


def block_specs(heads, count, order):
    wide = heads * 128
    all_wide = 5 * wide + 128
    whole = lambda *shape: pl.BlockSpec(shape, lambda i: (0,) * len(shape))
    return dict(
        length=pl.BlockSpec(memory_space=pltpu.SMEM),
        mixed=pl.BlockSpec((count, all_wide), lambda i: (order(i), 0)),
        halo=pl.BlockSpec((8, all_wide), lambda i: (jnp.maximum(order(i) * (count // 8) - 1, 0), 0)),
        head=pl.BlockSpec((count, wide), lambda i: (order(i), 0)),
        taps=whole(8, 5 * wide),
        small=whole(8, 128),
        level=whole(2 * GROUP, 2 * GROUP),
        kept=pl.BlockSpec((count // GROUP, heads, 128, 128), lambda i: (order(i), 0, 0, 0)),
    )


VMEM_BYTES = 56 * 2**20


def mixer_forward(heads, length, mixed, gate, taps, small, level):
    tokens = mixed.shape[0]
    count = step_tokens(tokens)
    steps = tokens // count
    wide = heads * 128
    s = block_specs(heads, count, lambda i: i)
    kept = jax.ShapeDtypeStruct((tokens // GROUP, heads, 128, 128), F32)
    return pl.pallas_call(
        functools.partial(forward_kernel, heads),
        grid=(steps,),
        in_specs=[s["length"], s["mixed"], s["halo"], s["head"], s["taps"], s["small"], s["level"]],
        out_specs=[s["head"], s["head"], s["kept"], s["kept"], s["kept"]],
        out_shape=[
            jax.ShapeDtypeStruct((tokens, wide), LOW),
            jax.ShapeDtypeStruct((tokens, wide), F32),
            kept, kept, kept,
        ],
        scratch_shapes=[pltpu.VMEM((heads, 128, 128), F32), pltpu.VMEM((count + 8, 5 * wide), F32)],
        compiler_params=pltpu.CompilerParams(vmem_limit_bytes=VMEM_BYTES),
        cost_estimate=pl.CostEstimate(
            flops=tokens * heads * 40_000_00, bytes_accessed=tokens * heads * 10_000, transcendentals=0
        ),
        name="mixer_forward",
    )(length, mixed, mixed, gate, taps, small, level)


def mixer_backward(heads, length, mixed, gate, raw, grad, taps, small, level, solve, fresh, state):
    tokens = mixed.shape[0]
    count = step_tokens(tokens)
    steps = tokens // count
    wide = heads * 128
    s = block_specs(heads, count, lambda i: steps - 1 - i)
    return pl.pallas_call(
        functools.partial(backward_kernel, heads),
        grid=(steps,),
        in_specs=[
            s["length"], s["mixed"], s["halo"], s["head"], s["head"], s["head"], s["taps"], s["small"], s["level"],
            s["kept"], s["kept"], s["kept"],
        ],
        out_specs=[s["mixed"], s["head"], s["taps"], s["small"]],
        out_shape=[
            jax.ShapeDtypeStruct(mixed.shape, LOW),
            jax.ShapeDtypeStruct((tokens, wide), LOW),
            jax.ShapeDtypeStruct((8, 5 * wide), F32),
            jax.ShapeDtypeStruct((8, 128), F32),
        ],
        scratch_shapes=[
            pltpu.VMEM((heads, 128, 128), F32),
            pltpu.VMEM((count + 8, 5 * wide), F32),
            pltpu.VMEM((count + 8, 5 * wide), F32),
        ],
        compiler_params=pltpu.CompilerParams(vmem_limit_bytes=VMEM_BYTES),
        cost_estimate=pl.CostEstimate(
            flops=tokens * heads * 60_000_00, bytes_accessed=tokens * heads * 10_000, transcendentals=0
        ),
        name="mixer_backward",
    )(length, mixed, mixed, gate, raw, grad, taps, small, level, solve, fresh, state)


def swap(array, axis, bits):
    return lax.ppermute(array, axis, [(i, i ^ bits) for i in range(lax.axis_size(axis))])


def on_square(axis):
    return lax.axis_size(axis) == 4


def power_of_two(axis):
    return lax.axis_size(axis) & (lax.axis_size(axis) - 1) == 0


def block_at(array, index, size):
    return lax.dynamic_slice_in_dim(array, index * size, size, 0)


def put(array, block, start):
    return lax.dynamic_update_slice(array, block, (start,) + (0,) * (array.ndim - 1))


def gather_tokens(array):
    if not on_square("seq"):
        return lax.all_gather(array, "seq", axis=0, tiled=True)
    me = lax.axis_index("seq")
    size = array.shape[0]
    half = size // 2
    beside, below = swap(array, "seq", 1), swap(array, "seq", 2)
    far_one = swap(below[:half], "seq", 1)
    far_two = swap(beside[half:], "seq", 2)
    out = jnp.zeros((4 * size,) + array.shape[1:], array.dtype)
    out = put(out, array, me * size)
    out = put(out, beside, (me ^ 1) * size)
    out = put(out, below, (me ^ 2) * size)
    out = put(out, far_one, (me ^ 3) * size)
    return put(out, far_two, (me ^ 3) * size + half)


def scatter_sum(array):
    count = lax.axis_size("seq")
    size = array.shape[0] // count
    if not on_square("seq"):
        return lax.psum_scatter(array.astype(LOW), "seq", scatter_dimension=0, tiled=True).astype(F32)
    me = lax.axis_index("seq")
    half = array.shape[1] // 2
    parts = []
    for cols, first, second in ((slice(0, half), 1, 2), (slice(half, None), 2, 1)):
        part = array[:, cols].reshape(count, size, half)

        def block(index):
            return lax.dynamic_index_in_dim(part, index, 0, False)

        near = swap(block(me ^ first).astype(LOW), "seq", first)
        sent = swap(block(me ^ first ^ second).astype(LOW), "seq", first)
        onward = (block(me ^ second) + sent.astype(F32)).astype(LOW)
        own = block(me) + near.astype(F32)
        parts.append((own, swap(onward, "seq", second)))
    return jnp.concatenate([own + got.astype(F32) for own, got in parts], axis=1)


def exchange(blocks):
    if not on_square("seq"):
        return lax.all_to_all(blocks, "seq", 0, 0, tiled=True)
    me = lax.axis_index("seq")
    out = blocks
    for bits in (3, 1, 2):
        sent = lax.dynamic_index_in_dim(blocks, me ^ bits, 0, True)
        out = put(out, swap(sent, "seq", bits), me ^ bits)
    return out


def sum_over_rows(array):
    if not power_of_two("rows"):
        return lax.psum(array, "rows")
    bits = 1
    while bits < lax.axis_size("rows"):
        array = array + swap(array, "rows", bits)
        bits *= 2
    return array


def gather_small(array):
    if not power_of_two("seq"):
        return lax.all_gather(array, "seq")
    count = lax.axis_size("seq")
    me = lax.axis_index("seq")
    out = put(jnp.zeros((count,) + array.shape, array.dtype), array[None], me)
    bits = 1
    while bits < count:
        out = out + swap(out, "seq", bits)
        bits *= 2
    return out


def gather_weights(blocks):
    mine = exchange(blocks)
    whole = lax.all_gather(mine, "rows", axis=0)
    rows, count, size, width = whole.shape
    return whole.transpose(1, 0, 2, 3).reshape(count * rows * size, width)


def scatter_weights(grad):
    count, rows = lax.axis_size("seq"), lax.axis_size("rows")
    size = grad.shape[0] // (count * rows)
    width = grad.shape[1]
    grad = grad.astype(LOW).reshape(count, rows, size, width).transpose(1, 0, 2, 3)
    summed = lax.psum_scatter(grad.reshape(-1, width), "rows", scatter_dimension=0, tiled=True)
    return exchange(summed.reshape(count, size, width))


def project(left, right):
    return jnp.dot(left, right, preferred_element_type=F32)


def outer_sum(left, right):
    return lax.dot_general(left, right, FORMS["tn"], preferred_element_type=F32)


def back_project(left, right):
    return lax.dot_general(left, right, FORMS["nt"], preferred_element_type=F32)


def norm_scale(features):
    return lax.rsqrt(jnp.mean(features * features, axis=-1, keepdims=True) + EPS_NORM)


def norm_back(features, scale, grad):
    return scale * grad - features * scale**3 * jnp.mean(grad * features, axis=-1, keepdims=True)


def on_device(
    block_input, valid_length, query_weight, key_weight, value_weight, beta_weight, decay_weight, gate_weight,
    out_weight, ffn_gate_weight, ffn_up_weight, ffn_down_weight, norm_gain, ffn_norm_gain, head_norm_gain,
    decay_log, decay_bias, conv_weight, output_grad,
):
    count = lax.axis_size("seq")
    me = lax.axis_index("seq")
    rows_here, tokens_here, model_width = block_input.shape
    share = query_weight.shape[0]
    head_count = decay_log.shape[0]
    heads = max(1, head_count // count)
    blocks = head_count // heads
    copies = count // blocks
    block = me // copies
    wide = heads * 128
    hidden = ffn_gate_weight.shape[1] // count
    all_wide = 5 * wide + 128

    def cut(weight, pieces):
        width = weight.shape[1] // (pieces * blocks)
        out = weight.reshape(share, pieces, blocks, width).transpose(2, 0, 1, 3)
        return jnp.repeat(out.reshape(blocks, share, pieces * width), copies, axis=0)

    def cut_hidden(weight):
        return weight.reshape(share, count, hidden).transpose(1, 0, 2)

    def gain_column(gain):
        return jnp.broadcast_to(gain[None, :, None], (count, share, 1))

    tail = jnp.concatenate(
        [cut(beta_weight, 2), cut(decay_weight, 1), gain_column(norm_gain), gain_column(ffn_norm_gain)], axis=2
    )
    tail = jnp.pad(tail, ((0, 0), (0, 0), (0, 128 - tail.shape[2])))
    first_pack = jnp.concatenate([cut(query_weight, 1), cut(key_weight, 2), cut(value_weight, 2), tail], axis=2)
    later_pack = jnp.concatenate(
        [cut(gate_weight, 1), cut(out_weight, 1), cut_hidden(ffn_gate_weight), cut_hidden(ffn_up_weight),
         cut_hidden(ffn_down_weight)], axis=2,
    )
    mixed_weight = gather_weights(first_pack)
    own = block_input.reshape(tokens_here, model_width)
    everyone = gather_tokens(own)
    later_weight = gather_weights(later_pack)
    gate_matrix = later_weight[:, :wide]
    out_matrix = later_weight[:, wide : 2 * wide]
    ffn_in = later_weight[:, 2 * wide : 2 * wide + 2 * hidden]
    ffn_down = later_weight[:, 2 * wide + 2 * hidden :]
    gain_first = mixed_weight[:, 5 * wide + 3 * heads].astype(F32)
    gain_second = mixed_weight[:, 5 * wide + 3 * heads + 1].astype(F32)
    grad_branch = gather_tokens(output_grad.reshape(tokens_here, model_width))

    def block_lanes(vector, first):
        mine = lax.dynamic_slice_in_dim(vector, block * heads, heads)
        return jnp.zeros((128,), F32).at[first : first + heads].set(mine)

    small = jnp.zeros((8, 128), F32)
    small = small.at[0].set(block_lanes(-jnp.exp(decay_log), 2 * heads))
    small = small.at[1].set(block_lanes(decay_bias, 2 * heads))
    small = small.at[2].set(head_norm_gain)
    taps = conv_weight.reshape(conv_weight.shape[0], 5, blocks, wide)
    taps = lax.dynamic_index_in_dim(taps, block, 2, False).reshape(conv_weight.shape[0], 5 * wide)
    taps = jnp.pad(taps, ((0, 8 - taps.shape[0]), (0, 0)))
    level = level_table()

    tokens_all = everyone.astype(F32)
    scale_all = norm_scale(tokens_all)
    shaped_all = tokens_all * scale_all
    normed = (shaped_all * gain_first).astype(LOW)
    mixed = project(normed, mixed_weight)
    gate_pre = project(normed, gate_matrix)
    gated, raw, solve, fresh, state = mixer_forward(heads, valid_length, mixed, gate_pre, taps, small, level)
    keep = (me % copies == 0).astype(F32)

    def once(array):
        return array if copies == 1 else array * keep.astype(array.dtype)

    tokens = own.astype(F32)
    second = tokens + scatter_sum(once(back_project(gated, out_matrix)))
    scale_second = norm_scale(second)
    normed_two = gather_tokens((second * scale_second * gain_second).astype(LOW))
    acts = project(normed_two, ffn_in)
    gate_act, up_act = acts[:, :hidden], acts[:, hidden:]
    sig = jax.nn.sigmoid(gate_act)
    hidden_low = (gate_act * sig * up_act).astype(LOW)
    result = second + scatter_sum(back_project(hidden_low, ffn_down))
    result = result.astype(LOW).reshape(block_input.shape)

    grad_hidden = project(grad_branch, ffn_down)
    grad_acts = jnp.concatenate(
        [grad_hidden * up_act * sig * (1.0 + gate_act * (1.0 - sig)), grad_hidden * gate_act * sig], axis=1
    ).astype(LOW)
    grad_normed_two = scatter_sum(back_project(grad_acts, ffn_in))
    grad_second = output_grad.reshape(tokens_here, model_width).astype(F32) + norm_back(
        second, scale_second, grad_normed_two * gain_second
    )
    grad_gain_second = jnp.sum(grad_normed_two * second * scale_second, axis=0)
    grad_mixed_low = gather_tokens(grad_second.astype(LOW))
    grad_gated = project(grad_mixed_low, out_matrix)
    ffn_grads = scatter_weights(
        jnp.concatenate([outer_sum(normed_two, grad_acts), outer_sum(grad_branch, hidden_low)], axis=1)
    )
    grad_pre, grad_gate, grad_taps, grad_small = mixer_backward(
        heads, valid_length, mixed, gate_pre, raw, grad_gated, taps, small, level, solve, fresh, state
    )
    grad_pre, grad_gate = once(grad_pre), once(grad_gate)
    pooled = jnp.concatenate([grad_taps[:4], jnp.pad(grad_small[:4], ((0, 0), (0, 5 * wide - 128)))], axis=0)
    pooled = gather_small(sum_over_rows(once(pooled)))

    late_grads = scatter_weights(
        jnp.concatenate([outer_sum(normed, grad_gate), once(outer_sum(grad_mixed_low, gated))], axis=1)
    )
    grad_normed = back_project(grad_pre, mixed_weight) + back_project(grad_gate, gate_matrix)
    grad_gain_first = jnp.sum(grad_normed * shaped_all, axis=0)
    mixed_grads = outer_sum(normed, grad_pre)
    first_gain = 5 * wide + 3 * heads
    mixed_grads = jnp.concatenate(
        [mixed_grads[:, :first_gain], grad_gain_first[:, None], grad_gain_second[:, None],
         jnp.zeros((model_width, all_wide - first_gain - 2), F32)], axis=1,
    )
    mixed_grads = scatter_weights(mixed_grads).astype(F32)
    grad_normed = scatter_sum(grad_normed)
    scale = norm_scale(tokens)
    grad_input = grad_second + norm_back(tokens, scale, grad_normed * gain_first)
    grad_input = grad_input.reshape(block_input.shape)

    def join(grads, pieces):
        grads = grads[::copies].astype(F32)
        width = grads.shape[2] // pieces
        return grads.reshape(blocks, share, pieces, width).transpose(1, 2, 0, 3).reshape(share, -1)

    def join_hidden(grads):
        return grads.astype(F32).transpose(1, 0, 2).reshape(share, -1)

    tail = mixed_grads[:, :, 5 * wide :]
    by_block = pooled[::copies]
    grad_conv = by_block[:, :4].reshape(blocks, 4, 5, wide).transpose(1, 2, 0, 3).reshape(4, -1)
    return (
        result,
        grad_input,
        join(mixed_grads[:, :, :wide], 1),
        join(mixed_grads[:, :, wide : 3 * wide], 2),
        join(mixed_grads[:, :, 3 * wide : 5 * wide], 2),
        join(tail[:, :, : 2 * heads], 2),
        join(tail[:, :, 2 * heads : 3 * heads], 1),
        join(late_grads[:, :, :wide], 1),
        join(late_grads[:, :, wide:], 1),
        join_hidden(ffn_grads[:, :, :hidden]),
        join_hidden(ffn_grads[:, :, hidden : 2 * hidden]),
        join_hidden(ffn_grads[:, :, 2 * hidden :]),
        jnp.sum(tail[:, :, 3 * heads], axis=0),
        jnp.sum(tail[:, :, 3 * heads + 1], axis=0),
        jnp.sum(by_block[:, 6, :128], axis=0),
        by_block[:, 4, 2 * heads : 3 * heads].reshape(-1),
        by_block[:, 5, 2 * heads : 3 * heads].reshape(-1),
        grad_conv,
    )


def solution(mesh):
    tokens, weight, vector, whole = P("rows", "seq", None), P(BOTH, None), P(BOTH), P()
    return jax.shard_map(
        on_device,
        mesh=mesh,
        in_specs=(tokens, P("rows")) + (weight,) * 10 + (vector,) * 2 + (whole,) * 4 + (tokens,),
        out_specs=(tokens, tokens) + (weight,) * 10 + (vector,) * 2 + (whole,) * 4,
        check_vma=False,
    )
```

time: 2170 us -> 510 us (0.24)
  waiting for transfers between devices: 1010 us -> 177 us
  other arithmetic: 407 us -> 19.2 us
  matrix products: 359 us -> 56.1 us
  blocking collectives: 160 us -> 0 us
  local copies, waits for them, and re-layouts: 202 us -> 87 us
  Pallas kernels: 0 us -> 81.3 us
  starting transfers between devices: 5.47 us -> 65.8 us
    reduce_scatter x1 -> x3, waiting for transfers between devices: 536 us -> 0.06 us  [scatter_weights(): lax.psum_scatter(grad.reshape(-1, width), 'rows', scatter_dimension=0, ti...]
    another operation x11 -> x0, other arithmetic: 325 us -> none  [the longest x2 318 us: lower_solve(): return jax.scipy.linalg.solve_triangular(matrix, right_side, lower=True)]
    all_gather x12 -> x2, waiting for transfers between devices: 342 us -> 35.7 us  [gather_weights(): whole = lax.all_gather(mine, 'rows', axis=0)]
    dot_general x128 -> x15, matrix products: 342 us -> 56.1 us  [the longest x5 19.6 us: outer_sum(): return lax.dot_general(left, right, FORMS['tn'], preferred_element_type=F32)]
    ppermute x2 -> x60, waiting for transfers between devices: 5.2 us -> 142 us  [swap(): lax.ppermute(array, axis, [(i, i ^ bits) for i in range(lax.axis_size(axi...]
    psum x1 -> x0, waiting for transfers between devices: 118 us -> none  [on_device(): lax.psum((grad_head_gain, grad_decay_log, grad_decay_bias, grad_conv), ('...]
    pallas_call x0 -> x2, Pallas kernels: none -> 81.3 us  [the longest x1 47.3 us: mixer_backward(): pl.pallas_call(functools.partial(backward_kernel, heads), grid=(steps,),...]
    all_gather x2 -> x0, blocking collectives: 78.4 us -> none  [the longest x1 40.9 us: on_device(): lax.all_gather(decay_weight, ('seq', 'rows'), axis=0, tiled=True)]
  transfers between devices with their start and end apart: 16 -> 65, of which waited for: 12 -> 40; matrix products, arithmetic and copies ran while one was open for 14% -> 23% of each run, Pallas kernels for 0% -> 0%
where the time goes in v1:
time: 510 us; the launch traced here: 503 us
  waiting for transfers between devices  177 us (35%)
  local copies, waits for them, and re-layouts  87 us (17%)
  Pallas kernels  81.3 us (16%)
  starting transfers between devices  65.8 us (13%)
  matrix products  56.1 us (11%)
  other arithmetic  19.2 us (4%)
  between operations  16.3 us (3%)
    ppermute x60, waiting for transfers between devices, swap(): lax.ppermute(array, axis, [(i, i ^ bits) for i in range(lax.axis_size(axi...  142 us
    ppermute x60, starting transfers between devices, swap(): lax.ppermute(array, axis, [(i, i ^ bits) for i in range(lax.axis_size(axi...  65.5 us
    pallas_call x1, Pallas kernels, mixer_backward(): pl.pallas_call(functools.partial(backward_kernel, heads), grid=(steps,),...  47.3 us
    all_gather x2, waiting for transfers between devices, gather_weights(): whole = lax.all_gather(mine, 'rows', axis=0)  35.7 us
    pallas_call x1, Pallas kernels, mixer_forward(): pl.pallas_call(functools.partial(forward_kernel, heads), grid=(steps,), i...  34 us
    dot_general x5, matrix products, outer_sum(): return lax.dot_general(left, right, FORMS['tn'], preferred_element_type=F32)  19.6 us
    dot_general x5, matrix products, back_project(): return lax.dot_general(left, right, FORMS['nt'], preferred_element_type=F32)  19.2 us
    dot_general x5, matrix products, project(): return jnp.dot(left, right, preferred_element_type=F32)  17.3 us
  transfers between devices with their start and end apart: 65, of which 40 were waited for; matrix products, arithmetic and copies ran while one was open for 23% of the time, Pallas kernels for 0%

profile of v1, /device:TPU:0, one launch (start us, length us, event | category | flops | bytes accessed | tf_op | source)
XLA Modules:
  0.0 503.0 jit_solution(17186177144977077806)
XLA Ops:
  13.5 3.0 collective-permute-start.6
  18.1 5.3 %collective-permute-done.4 = bf16[1,32,1408]{2,1,0:T(8,128)(2,1)S(1)} collective-permute-done((bf16[1,32,1408]{2,1,0:T(8,128)(2,1)S(1)}, bf16[1,32,1408]{2,1,0:T(8,128)(2,1)S(1)}, u32[]{:S(2)}, u32[]{:S(2)}) %collective-permute-start.4) | collective-permute-done | bytes 90144 | tf_op jit(solution)/shard_map/ppermute | solution.py:408
  31.8 8.4 %collective-permute-done.7 = bf16[1,32,2624]{2,0,1:T(2,128)(2,1)S(1)} collective-permute-done((bf16[1,32,2624]{2,0,1:T(2,128)(2,1)S(1)}, bf16[1,32,2624]{2,0,1:T(2,128)(2,1)S(1)}, u32[]{:S(2)}, u32[]{:S(2)}) %collective-permute-start.7) | collective-permute-done | bytes 167968 | tf_op jit(solution)/shard_map/ppermute | solution.py:408
  52.9 10.0 %collective-permute-done.1 = bf16[256,1024]{1,0:T(8,128)(2,1)} collective-permute-done((bf16[256,1024]{1,0:T(8,128)(2,1)S(1)}, bf16[256,1024]{1,0:T(8,128)(2,1)}, u32[]{:S(2)}, u32[]{:S(2)}) %collective-permute-start.1) | collective-permute-done | bytes 524320 | tf_op jit(solution)/shard_map/ppermute | solution.py:408
  71.2 3.2 collective-permute-done.3
  75.0 2.3 copy.144
  78.9 5.7 %fusion.77.mixed_ref.halo_ref = f32[1024,1408]{1,0:T(8,128)} fusion(bf16[1024,1408]{1,0:T(8,128)(2,1)S(1)} %bitcast.332, bf16[1024,1024]{1,0:T(8,128)(2,1)S(1)} %constant_dynamic-update-slice_fusion.24, f32[1024]{0:T(1024)S(1)} %get-tuple-element.96, f32[1024]{0:T(1024)S(1)} %add_rsqrt_fusion), kind=kOutput, calls=%fused_computation.229 | convolution fusion | flops 2956984320 | bytes 10756096 | tf_op jit(solution)/shard_map/dot_general | solution.py:517
  84.6 35.7 %all-gather.5.cloned.1.call-done = bf16[8,4,32,2624]{3,2,1,0:T(8,128)(2,1)} async-done(((bf16[1,4,32,2624]{3,2,1,0:T(8,128)(2,1)}), bf16[8,4,32,2624]{3,2,1,0:T(8,128)(2,1)}) %all-gather.5.cloned.1.call-update) | async-done | bytes 5373968 | tf_op jit(solution)/shard_map/all_gather | solution.py:502
  120.2 3.0 copy.149
  127.4 34.0 %mixer_forward.1 = (bf16[1024,256]{1,0:T(8,128)(2,1)}, f32[1024,256]{1,0:T(8,128)}, f32[16,2,128,128]{3,2,1,0:T(8,128)}, f32[16,2,128,128]{3,2,1,0:T(8,128)}, f32[16,2,128,128]{3,2,1,0:T(8,128)}) custom-call(s32[1]{0:T(128)S(6)} %copy.225.length_ref, f32[1024,1408]{1,0:T(8,128)} %fusion.77.mixed_ref.halo_ref, f32[1024,1408]{1,0:T(8,128)} %fusion.77.mixed_ref.halo_ref, ...), custom_call_target="tpu_custom_call" | custom-call | flops 8192000000 | bytes 20480000 | tf_op jit(solution)/shard_map/mixer_forward/pallas_call | solution.py:355
  171.1 4.3 collective-permute-done.14
  180.4 6.3 %collective-permute-done.27 = bf16[256,1024]{1,0:T(8,128)(2,1)} collective-permute-done((bf16[256,1024]{1,0:T(8,128)(2,1)S(1)}, bf16[256,1024]{1,0:T(8,128)(2,1)}, u32[]{:S(2)}, u32[]{:S(2)}) %collective-permute-start.27) | collective-permute-done | bytes 524320 | tf_op jit(solution)/shard_map/ppermute | solution.py:408
  189.1 3.1 collective-permute-done.13
  204.3 2.9 collective-permute-done.28
  207.3 8.1 %collective-permute-done.17 = bf16[256,1024]{1,0:T(8,128)(2,1)S(1)} collective-permute-done((bf16[256,1024]{1,0:T(8,128)(2,1)S(1)}, bf16[256,1024]{1,0:T(8,128)(2,1)S(1)}, u32[]{:S(2)}, u32[]{:S(2)}) %collective-permute-start.17) | collective-permute-done | bytes 524320 | tf_op jit(solution)/shard_map/ppermute | solution.py:408
  216.0 3.1 collective-permute-done.29
  223.0 2.7 collective-permute-done.19
  227.1 3.4 fusion.7
  230.5 4.7 multiply_convert_fusion.1
  235.2 3.4 fusion.5
  242.2 6.3 %collective-permute-done.34 = bf16[256,512]{1,0:T(8,128)(2,1)S(1)} collective-permute-done((bf16[256,512]{1,0:T(8,128)(2,1)S(1)}, bf16[256,512]{1,0:T(8,128)(2,1)S(1)}, u32[]{:S(2)}, u32[]{:S(2)}) %collective-permute-start.34) | collective-permute-done | bytes 262176 | tf_op jit(solution)/shard_map/ppermute | solution.py:408
  253.3 2.4 collective-permute-done.35
  255.8 3.7 collective-permute-done.30
  261.9 10.8 %collective-permute-done.37 = bf16[256,1024]{1,0:T(8,128)(2,1)S(1)} collective-permute-done((bf16[256,1024]{1,0:T(8,128)(2,1)S(1)}, bf16[256,1024]{1,0:T(8,128)(2,1)S(1)}, u32[]{:S(2)}, u32[]{:S(2)}) %collective-permute-start.37) | collective-permute-done | bytes 524320 | tf_op jit(solution)/shard_map/ppermute | solution.py:408
  274.9 4.2 collective-permute-done.38
  282.6 47.3 %mixer_backward.1 = (bf16[1024,1408]{1,0:T(8,128)(2,1)}, bf16[1024,256]{1,0:T(8,128)(2,1)}, f32[8,1280]{1,0:T(8,128)}, f32[8,128]{1,0:T(8,128)}) custom-call(s32[1]{0:T(128)S(6)} %copy.225.length_ref, f32[1024,1408]{1,0:T(8,128)} %fusion.77.mixed_ref.halo_ref, f32[1024,1408]{1,0:T(8,128)} %fusion.77.mixed_ref.halo_ref, f32[1024,256]{1,0:T(8,128)} %fusion.47.gate_ref, ...), custom_call_target="tpu_custom_call" | custom-call | flops 12288000000 | bytes 20480000 | tf_op jit(solution)/shard_map/mixer_backward/pallas_call | solution.py:380
  333.6 5.8 %fusion.74 = bf16[1024,1408]{0,1:T(8,128)(2,1)S(1)} fusion(bf16[1024,1408]{1,0:T(8,128)(2,1)} %get-tuple-element.92, bf16[1024,1024]{1,0:T(8,128)(2,1)} %copy-done.1, f32[1024]{0:T(1024)S(1)} %get-tuple-element.96, f32[1024]{0:T(1024)S(1)} %add_rsqrt_fusion), kind=kOutput, calls=%fused_computation.228 | convolution fusion | flops 2956984320 | bytes 7872512 | tf_op jit(solution)/shard_map/dot_general | solution.py:521
  341.2 4.7 copy.153
  345.9 6.3 %fusion.84 = f32[1024,1024]{1,0:T(8,128)S(1)} fusion(bf16[1024,1408]{1,0:T(8,128)(2,1)} %get-tuple-element.92, bf16[1024,1408]{1,0:T(8,128)(2,1)} %bitcast.333), kind=kOutput, calls=%fused_computation.235 | convolution fusion | flops 2952790016 | bytes 9961472 | tf_op jit(solution)/shard_map/dot_general | solution.py:525
  352.2 3.8 fusion.3
  356.5 5.9 %concatenate.128 = bf16[4,8,32,1408]{3,2,1,0:T(8,128)(2,1)} concatenate(bf16[4,8,32,1286]{3,2,1,0:T(8,128)(2,1)} %bitcast.284, bf16[4,8,32,1]{3,2,1,0:T(8,128)(2,1)S(1)} %concatenate.136, bf16[4,8,32,1]{3,2,1,0:T(8,128)(2,1)S(1)} %concatenate.137, bf16[4,8,32,120]{3,2,1,0:T(8,128)(2,1)S(1)} %broadcast_in_dim.17), dimensions={3} | concatenate | bytes 5767168 | tf_op jit(solution)/shard_map/concatenate | solution.py:650
  362.4 3.7 copy.156
  366.2 4.9 convolution_convert_fusion.1
  371.1 2.6 copy.167
  373.6 6.1 %convolution_convert_fusion = bf16[1024,1408]{1,0:T(8,128)(2,1)S(1)} fusion(bf16[1024,1024]{1,0:T(8,128)(2,1)} %copy-done.14, bf16[1024,704]{1,0:T(8,128)(2,1)} %copy-done.33, bf16[1024,704]{1,0:T(8,128)(2,1)} %copy-done.32), kind=kOutput, calls=%fused_computation.9 | convolution fusion | flops 2959998976 | bytes 7864320 | tf_op jit(solution)/shard_map/dot_general | solution.py:521
  380.2 2.5 copy.176
  382.7 3.7 fusion.11
  391.3 2.7 collective-permute-done.24
  396.9 3.7 collective-permute-done.25
  414.5 4.3 collective-permute-done.44
  420.3 8.0 %collective-permute-done.58 = f32[4,8,1280]{2,1,0:T(8,128)S(1)} collective-permute-done((f32[4,8,1280]{2,1,0:T(8,128)S(1)}, f32[4,8,1280]{2,1,0:T(8,128)S(1)}, u32[]{:S(2)}, u32[]{:S(2)}) %collective-permute-start.58) | collective-permute-done | bytes 163872 | tf_op jit(solution)/shard_map/ppermute | solution.py:408
  431.2 2.5 collective-permute-done.59
  442.3 3.3 collective-permute-done.49
  447.9 2.9 fusion.15
  454.6 3.8 collective-permute-done.46
  465.2 3.2 collective-permute-done.48
  473.8 4.3 collective-permute-done.52
  487.9 4.3 collective-permute-done.54
  (363 shorter events, 166.4 us)
Async XLA Ops:
  7.2 67.8 %all-gather.3.cloned.1.call-start = ((), (), s32[]{:S(2)}) async-start(), calls=%async_computation.3 | async-start | bytes 3244032 | tf_op jit(solution)/shard_map/all_gather | solution.py:502
  13.5 10.0 %collective-permute-start.6 = (bf16[1,32,1408]{2,1,0:T(8,128)(2,1)S(1)}, bf16[1,32,1408]{2,1,0:T(8,128)(2,1)S(1)}, u32[]{:S(2)}, u32[]{:S(2)}) collective-permute-start(bf16[1,32,1408]{2,1,0:T(8,128)(2,1)S(1)} %get-tuple-element.150), channel_id=1, source_target_pairs={{0,16},{8,24},{16,0},{24,8},{1,17},{9,25},{17,1},{25,9},{2,18},{10... | collective-permute-start | bytes 270344 | tf_op jit(solution)/shard_map/ppermute | solution.py:408
  16.5 6.9 %collective-permute-start.5 = (bf16[1,32,1408]{2,1,0:T(8,128)(2,1)S(1)}, bf16[1,32,1408]{2,1,0:T(8,128)(2,1)S(1)}, u32[]{:S(2)}, u32[]{:S(2)}) collective-permute-start(bf16[1,32,1408]{2,1,0:T(8,128)(2,1)S(1)} %get-tuple-element.151), channel_id=1, source_target_pairs={{0,8},{8,0},{16,24},{24,16},{1,9},{9,1},{17,25},{25,17},{2,10},{10... | collective-permute-start | bytes 270344 | tf_op jit(solution)/shard_map/ppermute | solution.py:408
  24.3 95.9 %all-gather.5.cloned.1.call-start = ((), (), s32[]{:S(2)}) async-start(), calls=%async_computation.4 | async-start | bytes 6193152 | tf_op jit(solution)/shard_map/all_gather | solution.py:502
  28.3 12.0 %collective-permute-start.7 = (bf16[1,32,2624]{2,0,1:T(2,128)(2,1)S(1)}, bf16[1,32,2624]{2,0,1:T(2,128)(2,1)S(1)}, u32[]{:S(2)}, u32[]{:S(2)}) collective-permute-start(bf16[1,32,2624]{2,0,1:T(2,128)(2,1)S(1)} %get-tuple-element.138), channel_id=1, source_target_pairs={{0,24},{8,16},{16,8},{24,0},{1,25},{9,17},{17,9},{25,1},{2,26},{10... | collective-permute-start | bytes 503816 | tf_op jit(solution)/shard_map/ppermute | solution.py:408
  29.8 14.7 %collective-permute-start.8 = (bf16[1,32,2624]{2,0,1:T(2,128)(2,1)S(1)}, bf16[1,32,2624]{2,0,1:T(2,128)(2,1)S(1)}, u32[]{:S(2)}, u32[]{:S(2)}) collective-permute-start(bf16[1,32,2624]{2,0,1:T(2,128)(2,1)S(1)} %get-tuple-element.137), channel_id=1, source_target_pairs={{0,8},{8,0},{16,24},{24,16},{1,9},{9,1},{17,25},{25,17},{2,10},{10... | collective-permute-start | bytes 503816 | tf_op jit(solution)/shard_map/ppermute | solution.py:408
  30.5 16.0 %collective-permute-start.9 = (bf16[1,32,2624]{2,0,1:T(2,128)(2,1)S(1)}, bf16[1,32,2624]{2,0,1:T(2,128)(2,1)S(1)}, u32[]{:S(2)}, u32[]{:S(2)}) collective-permute-start(bf16[1,32,2624]{2,0,1:T(2,128)(2,1)S(1)} %get-tuple-element.136), channel_id=1, source_target_pairs={{0,16},{8,24},{16,0},{24,8},{1,17},{9,25},{17,1},{25,9},{2,18},{10... | collective-permute-start | bytes 503816 | tf_op jit(solution)/shard_map/ppermute | solution.py:408
  49.6 390.4 %reduce-scatter.6.cloned.1.call-start = ((), (), s32[]{:S(2)}) async-start(), calls=%async_computation.6 | async-start | bytes 1179648 | tf_op jit(solution)/shard_map/reduce_scatter | solution.py:512
  49.7 18.2 %collective-permute-start = (bf16[256,1024]{1,0:T(8,128)(2,1)S(1)}, bf16[256,1024]{1,0:T(8,128)(2,1)S(1)}, u32[]{:S(2)}, u32[]{:S(2)}) collective-permute-start(bf16[256,1024]{1,0:T(8,128)(2,1)S(1)} %bitcast.275), channel_id=1, source_target_pairs={{0,8},{8,0},{16,24},{24,16},{1,9},{9,1},{17,25},{25,17},{2,10},{10... | collective-permute-start | bytes 1572872 | tf_op jit(solution)/shard_map/ppermute | solution.py:408
  50.8 12.1 %collective-permute-start.1 = (bf16[256,1024]{1,0:T(8,128)(2,1)S(1)}, bf16[256,1024]{1,0:T(8,128)(2,1)}, u32[]{:S(2)}, u32[]{:S(2)}) collective-permute-start(bf16[256,1024]{1,0:T(8,128)(2,1)S(1)} %bitcast.276), channel_id=1, source_target_pairs={{0,16},{8,24},{16,0},{24,8},{1,17},{9,25},{17,1},{25,9},{2,18},{10... | collective-permute-start | bytes 1572872 | tf_op jit(solution)/shard_map/ppermute | solution.py:408
  64.6 6.6 %collective-permute-start.2 = (bf16[128,1024]{1,0:T(8,128)(2,1)}, bf16[128,1024]{1,0:T(8,128)(2,1)S(1)}, u32[]{:S(2)}, u32[]{:S(2)}) collective-permute-start(bf16[128,1024]{1,0:T(8,128)(2,1)} %slice.244), channel_id=1, source_target_pairs={{0,8},{8,0},{16,24},{24,16},{1,9},{9,1},{17,25},{25,17},{2,10},{10... | collective-permute-start | bytes 786440 | tf_op jit(solution)/shard_map/ppermute | solution.py:408
  166.0 9.5 %collective-permute-start.14 = (bf16[256,512]{1,0:T(8,128)(2,1)}, bf16[256,512]{1,0:T(8,128)(2,1)}, u32[]{:S(2)}, u32[]{:S(2)}) collective-permute-start(bf16[256,512]{1,0:T(8,128)(2,1)} %get-tuple-element.135), channel_id=1, source_target_pairs={{0,16},{8,24},{16,0},{24,8},{1,17},{9,25},{17,1},{25,9},{2,18},{10... | collective-permute-start | bytes 786440 | tf_op jit(solution)/shard_map/ppermute | solution.py:408
  167.5 19.2 %collective-permute-start.27 = (bf16[256,1024]{1,0:T(8,128)(2,1)S(1)}, bf16[256,1024]{1,0:T(8,128)(2,1)}, u32[]{:S(2)}, u32[]{:S(2)}) collective-permute-start(bf16[256,1024]{1,0:T(8,128)(2,1)S(1)} %bitcast.326), channel_id=1, source_target_pairs={{0,16},{8,24},{16,0},{24,8},{1,17},{9,25},{17,1},{25,9},{2,18},{10... | collective-permute-start | bytes 1572872 | tf_op jit(solution)/shard_map/ppermute | solution.py:408
  168.1 10.6 %collective-permute-start.11 = (bf16[256,512]{1,0:T(8,128)(2,1)S(1)}, bf16[256,512]{1,0:T(8,128)(2,1)S(1)}, u32[]{:S(2)}, u32[]{:S(2)}) collective-permute-start(bf16[256,512]{1,0:T(8,128)(2,1)S(1)} %get-tuple-element.133), channel_id=1, source_target_pairs={{0,8},{8,0},{16,24},{24,16},{1,9},{9,1},{17,25},{25,17},{2,10},{10... | collective-permute-start | bytes 786440 | tf_op jit(solution)/shard_map/ppermute | solution.py:408
  169.6 22.6 %collective-permute-start.13 = (bf16[256,512]{1,0:T(8,128)(2,1)S(1)}, bf16[256,512]{1,0:T(8,128)(2,1)S(1)}, u32[]{:S(2)}, u32[]{:S(2)}) collective-permute-start(bf16[256,512]{1,0:T(8,128)(2,1)S(1)} %get-tuple-element.134), channel_id=1, source_target_pairs={{0,16},{8,24},{16,0},{24,8},{1,17},{9,25},{17,1},{25,9},{2,18},{10... | collective-permute-start | bytes 786440 | tf_op jit(solution)/shard_map/ppermute | solution.py:408
  176.6 17.0 %collective-permute-start.15 = (bf16[256,512]{1,0:T(8,128)(2,1)S(1)}, bf16[256,512]{1,0:T(8,128)(2,1)S(1)}, u32[]{:S(2)}, u32[]{:S(2)}) collective-permute-start(bf16[256,512]{1,0:T(8,128)(2,1)S(1)} %fusion.38), channel_id=1, source_target_pairs={{0,8},{8,0},{16,24},{24,16},{1,9},{9,1},{17,25},{25,17},{2,10},{10... | collective-permute-start | bytes 786440 | tf_op jit(solution)/shard_map/ppermute | solution.py:408
  178.2 16.6 %collective-permute-start.10 = (bf16[256,512]{1,0:T(8,128)(2,1)S(1)}, bf16[256,512]{1,0:T(8,128)(2,1)S(1)}, u32[]{:S(2)}, u32[]{:S(2)}) collective-permute-start(bf16[256,512]{1,0:T(8,128)(2,1)S(1)} %get-tuple-element.132), channel_id=1, source_target_pairs={{0,8},{8,0},{16,24},{24,16},{1,9},{9,1},{17,25},{25,17},{2,10},{10... | collective-permute-start | bytes 786440 | tf_op jit(solution)/shard_map/ppermute | solution.py:408
  178.8 18.3 %collective-permute-start.12 = (bf16[256,512]{1,0:T(8,128)(2,1)S(1)}, bf16[256,512]{1,0:T(8,128)(2,1)S(1)}, u32[]{:S(2)}, u32[]{:S(2)}) collective-permute-start(bf16[256,512]{1,0:T(8,128)(2,1)S(1)} %fusion.40), channel_id=1, source_target_pairs={{0,16},{8,24},{16,0},{24,8},{1,17},{9,25},{17,1},{25,9},{2,18},{10... | collective-permute-start | bytes 786440 | tf_op jit(solution)/shard_map/ppermute | solution.py:408
  186.6 15.6 %collective-permute-start.26 = (bf16[256,1024]{1,0:T(8,128)(2,1)S(1)}, bf16[256,1024]{1,0:T(8,128)(2,1)S(1)}, u32[]{:S(2)}, u32[]{:S(2)}) collective-permute-start(bf16[256,1024]{1,0:T(8,128)(2,1)S(1)} %bitcast.327), channel_id=1, source_target_pairs={{0,8},{8,0},{16,24},{24,16},{1,9},{9,1},{17,25},{25,17},{2,10},{10... | collective-permute-start | bytes 1572872 | tf_op jit(solution)/shard_map/ppermute | solution.py:408
  192.2 15.1 %collective-permute-start.28 = (bf16[128,1024]{1,0:T(8,128)(2,1)S(1)}, bf16[128,1024]{1,0:T(8,128)(2,1)S(1)}, u32[]{:S(2)}, u32[]{:S(2)}) collective-permute-start(bf16[128,1024]{1,0:T(8,128)(2,1)S(1)} %slice.260), channel_id=1, source_target_pairs={{0,8},{8,0},{16,24},{24,16},{1,9},{9,1},{17,25},{25,17},{2,10},{10... | collective-permute-start | bytes 786440 | tf_op jit(solution)/shard_map/ppermute | solution.py:408
  198.9 20.2 %collective-permute-start.16 = (bf16[256,1024]{1,0:T(8,128)(2,1)S(1)}, bf16[256,1024]{1,0:T(8,128)(2,1)S(1)}, u32[]{:S(2)}, u32[]{:S(2)}) collective-permute-start(bf16[256,1024]{1,0:T(8,128)(2,1)S(1)} %get-tuple-element.108), channel_id=1, source_target_pairs={{0,8},{8,0},{16,24},{24,16},{1,9},{9,1},{17,25},{25,17},{2,10},{10... | collective-permute-start | bytes 1572872 | tf_op jit(solution)/shard_map/ppermute | solution.py:408
  200.5 14.9 %collective-permute-start.17 = (bf16[256,1024]{1,0:T(8,128)(2,1)S(1)}, bf16[256,1024]{1,0:T(8,128)(2,1)S(1)}, u32[]{:S(2)}, u32[]{:S(2)}) collective-permute-start(bf16[256,1024]{1,0:T(8,128)(2,1)S(1)} %get-tuple-element.108), channel_id=1, source_target_pairs={{0,16},{8,24},{16,0},{24,8},{1,17},{9,25},{17,1},{25,9},{2,18},{10... | collective-permute-start | bytes 1572872 | tf_op jit(solution)/shard_map/ppermute | solution.py:408
  202.3 16.8 %collective-permute-start.29 = (bf16[128,1024]{1,0:T(8,128)(2,1)S(1)}, bf16[128,1024]{1,0:T(8,128)(2,1)S(1)}, u32[]{:S(2)}, u32[]{:S(2)}) collective-permute-start(bf16[128,1024]{1,0:T(8,128)(2,1)S(1)} %slice.261), channel_id=1, source_target_pairs={{0,16},{8,24},{16,0},{24,8},{1,17},{9,25},{17,1},{25,9},{2,18},{10... | collective-permute-start | bytes 786440 | tf_op jit(solution)/shard_map/ppermute | solution.py:408
  215.4 7.6 %collective-permute-start.18 = (bf16[128,1024]{1,0:T(8,128)(2,1)S(1)}, bf16[128,1024]{1,0:T(8,128)(2,1)S(1)}, u32[]{:S(2)}, u32[]{:S(2)}) collective-permute-start(bf16[128,1024]{1,0:T(8,128)(2,1)S(1)} %slice.252), channel_id=1, source_target_pairs={{0,8},{8,0},{16,24},{24,16},{1,9},{9,1},{17,25},{25,17},{2,10},{10... | collective-permute-start | bytes 786440 | tf_op jit(solution)/shard_map/ppermute | solution.py:408
  219.2 6.5 %collective-permute-start.19 = (bf16[128,1024]{1,0:T(8,128)(2,1)S(1)}, bf16[128,1024]{1,0:T(8,128)(2,1)S(1)}, u32[]{:S(2)}, u32[]{:S(2)}) collective-permute-start(bf16[128,1024]{1,0:T(8,128)(2,1)S(1)} %slice.253), channel_id=1, source_target_pairs={{0,16},{8,24},{16,0},{24,8},{1,17},{9,25},{17,1},{25,9},{2,18},{10... | collective-permute-start | bytes 786440 | tf_op jit(solution)/shard_map/ppermute | solution.py:408
  239.2 9.3 %collective-permute-start.34 = (bf16[256,512]{1,0:T(8,128)(2,1)S(1)}, bf16[256,512]{1,0:T(8,128)(2,1)S(1)}, u32[]{:S(2)}, u32[]{:S(2)}) collective-permute-start(bf16[256,512]{1,0:T(8,128)(2,1)S(1)} %get-tuple-element.127), channel_id=1, source_target_pairs={{0,16},{8,24},{16,0},{24,8},{1,17},{9,25},{17,1},{25,9},{2,18},{10... | collective-permute-start | bytes 786440 | tf_op jit(solution)/shard_map/ppermute | solution.py:408
  240.8 9.9 %collective-permute-start.31 = (bf16[256,512]{1,0:T(8,128)(2,1)S(1)}, bf16[256,512]{1,0:T(8,128)(2,1)S(1)}, u32[]{:S(2)}, u32[]{:S(2)}) collective-permute-start(bf16[256,512]{1,0:T(8,128)(2,1)S(1)} %get-tuple-element.125), channel_id=1, source_target_pairs={{0,8},{8,0},{16,24},{24,16},{1,9},{9,1},{17,25},{25,17},{2,10},{10... | collective-permute-start | bytes 786440 | tf_op jit(solution)/shard_map/ppermute | solution.py:408
  241.7 11.6 %collective-permute-start.33 = (bf16[256,512]{1,0:T(8,128)(2,1)S(1)}, bf16[256,512]{1,0:T(8,128)(2,1)S(1)}, u32[]{:S(2)}, u32[]{:S(2)}) collective-permute-start(bf16[256,512]{1,0:T(8,128)(2,1)S(1)} %get-tuple-element.126), channel_id=1, source_target_pairs={{0,16},{8,24},{16,0},{24,8},{1,17},{9,25},{17,1},{25,9},{2,18},{10... | collective-permute-start | bytes 786440 | tf_op jit(solution)/shard_map/ppermute | solution.py:408
  248.6 7.0 %collective-permute-start.35 = (bf16[256,512]{1,0:T(8,128)(2,1)S(1)}, bf16[256,512]{1,0:T(8,128)(2,1)S(1)}, u32[]{:S(2)}, u32[]{:S(2)}) collective-permute-start(bf16[256,512]{1,0:T(8,128)(2,1)S(1)} %fusion.28), channel_id=1, source_target_pairs={{0,8},{8,0},{16,24},{24,16},{1,9},{9,1},{17,25},{25,17},{2,10},{10... | collective-permute-start | bytes 786440 | tf_op jit(solution)/shard_map/ppermute | solution.py:408
  249.5 9.9 %collective-permute-start.30 = (bf16[256,512]{1,0:T(8,128)(2,1)S(1)}, bf16[256,512]{1,0:T(8,128)(2,1)S(1)}, u32[]{:S(2)}, u32[]{:S(2)}) collective-permute-start(bf16[256,512]{1,0:T(8,128)(2,1)S(1)} %get-tuple-element.124), channel_id=1, source_target_pairs={{0,8},{8,0},{16,24},{24,16},{1,9},{9,1},{17,25},{25,17},{2,10},{10... | collective-permute-start | bytes 786440 | tf_op jit(solution)/shard_map/ppermute | solution.py:408
  250.8 8.6 %collective-permute-start.32 = (bf16[256,512]{1,0:T(8,128)(2,1)S(1)}, bf16[256,512]{1,0:T(8,128)(2,1)S(1)}, u32[]{:S(2)}, u32[]{:S(2)}) collective-permute-start(bf16[256,512]{1,0:T(8,128)(2,1)S(1)} %fusion.30), channel_id=1, source_target_pairs={{0,16},{8,24},{16,0},{24,8},{1,17},{9,25},{17,1},{25,9},{2,18},{10... | collective-permute-start | bytes 786440 | tf_op jit(solution)/shard_map/ppermute | solution.py:408
  260.6 12.1 %collective-permute-start.37 = (bf16[256,1024]{1,0:T(8,128)(2,1)S(1)}, bf16[256,1024]{1,0:T(8,128)(2,1)S(1)}, u32[]{:S(2)}, u32[]{:S(2)}) collective-permute-start(bf16[256,1024]{1,0:T(8,128)(2,1)S(1)} %get-tuple-element.106), channel_id=1, source_target_pairs={{0,16},{8,24},{16,0},{24,8},{1,17},{9,25},{17,1},{25,9},{2,18},{10... | collective-permute-start | bytes 1572872 | tf_op jit(solution)/shard_map/ppermute | solution.py:408
  260.8 12.8 %collective-permute-start.36 = (bf16[256,1024]{1,0:T(8,128)(2,1)S(1)}, bf16[256,1024]{1,0:T(8,128)(2,1)S(1)}, u32[]{:S(2)}, u32[]{:S(2)}) collective-permute-start(bf16[256,1024]{1,0:T(8,128)(2,1)S(1)} %get-tuple-element.106), channel_id=1, source_target_pairs={{0,8},{8,0},{16,24},{24,16},{1,9},{9,1},{17,25},{25,17},{2,10},{10... | collective-permute-start | bytes 1572872 | tf_op jit(solution)/shard_map/ppermute | solution.py:408
  333.1 118.9 %reduce-scatter.4.cloned.1.call-start = ((), (), s32[]{:S(2)}) async-start(), calls=%async_computation.5 | async-start | bytes 3244032 | tf_op jit(solution)/shard_map/reduce_scatter | solution.py:512
  366.2 105.0 %reduce-scatter.8.cloned.1.call-start = ((), (), s32[]{:S(2)}) async-start(), calls=%async_computation.7 | async-start | bytes 5013504 | tf_op jit(solution)/shard_map/reduce_scatter | solution.py:512
  387.1 7.0 %collective-permute-start.24 = (bf16[256,512]{1,0:T(8,128)(2,1)S(1)}, bf16[256,512]{1,0:T(8,128)(2,1)S(1)}, u32[]{:S(2)}, u32[]{:S(2)}) collective-permute-start(bf16[256,512]{1,0:T(8,128)(2,1)S(1)} %get-tuple-element.131), channel_id=1, source_target_pairs={{0,16},{8,24},{16,0},{24,8},{1,17},{9,25},{17,1},{25,9},{2,18},{10... | collective-permute-start | bytes 786440 | tf_op jit(solution)/shard_map/ppermute | solution.py:408
  388.3 7.2 %collective-permute-start.21 = (bf16[256,512]{1,0:T(8,128)(2,1)S(1)}, bf16[256,512]{1,0:T(8,128)(2,1)S(1)}, u32[]{:S(2)}, u32[]{:S(2)}) collective-permute-start(bf16[256,512]{1,0:T(8,128)(2,1)S(1)} %get-tuple-element.129), channel_id=1, source_target_pairs={{0,8},{8,0},{16,24},{24,16},{1,9},{9,1},{17,25},{25,17},{2,10},{10... | collective-permute-start | bytes 786440 | tf_op jit(solution)/shard_map/ppermute | solution.py:408
  389.2 7.6 %collective-permute-start.23 = (bf16[256,512]{1,0:T(8,128)(2,1)S(1)}, bf16[256,512]{1,0:T(8,128)(2,1)S(1)}, u32[]{:S(2)}, u32[]{:S(2)}) collective-permute-start(bf16[256,512]{1,0:T(8,128)(2,1)S(1)} %get-tuple-element.130), channel_id=1, source_target_pairs={{0,16},{8,24},{16,0},{24,8},{1,17},{9,25},{17,1},{25,9},{2,18},{10... | collective-permute-start | bytes 786440 | tf_op jit(solution)/shard_map/ppermute | solution.py:408
  390.5 10.2 %collective-permute-start.20 = (bf16[256,512]{1,0:T(8,128)(2,1)S(1)}, bf16[256,512]{1,0:T(8,128)(2,1)S(1)}, u32[]{:S(2)}, u32[]{:S(2)}) collective-permute-start(bf16[256,512]{1,0:T(8,128)(2,1)S(1)} %get-tuple-element.128), channel_id=1, source_target_pairs={{0,8},{8,0},{16,24},{24,16},{1,9},{9,1},{17,25},{25,17},{2,10},{10... | collective-permute-start | bytes 786440 | tf_op jit(solution)/shard_map/ppermute | solution.py:408
  394.1 6.4 %collective-permute-start.25 = (bf16[256,512]{1,0:T(8,128)(2,1)S(1)}, bf16[256,512]{1,0:T(8,128)(2,1)S(1)}, u32[]{:S(2)}, u32[]{:S(2)}) collective-permute-start(bf16[256,512]{1,0:T(8,128)(2,1)S(1)} %fusion.32), channel_id=1, source_target_pairs={{0,8},{8,0},{16,24},{24,16},{1,9},{9,1},{17,25},{25,17},{2,10},{10... | collective-permute-start | bytes 786440 | tf_op jit(solution)/shard_map/ppermute | solution.py:408
  404.7 31.6 %collective-permute-start.43 = (bf16[256,512]{1,0:T(8,128)(2,1)S(1)}, bf16[256,512]{1,0:T(8,128)(2,1)}, u32[]{:S(2)}, u32[]{:S(2)}) collective-permute-start(bf16[256,512]{1,0:T(8,128)(2,1)S(1)} %get-tuple-element.122), channel_id=1, source_target_pairs={{0,16},{8,24},{16,0},{24,8},{1,17},{9,25},{17,1},{25,9},{2,18},{10... | collective-permute-start | bytes 786440 | tf_op jit(solution)/shard_map/ppermute | solution.py:408
  405.5 13.3 %collective-permute-start.44 = (bf16[256,512]{1,0:T(8,128)(2,1)S(1)}, bf16[256,512]{1,0:T(8,128)(2,1)S(1)}, u32[]{:S(2)}, u32[]{:S(2)}) collective-permute-start(bf16[256,512]{1,0:T(8,128)(2,1)S(1)} %get-tuple-element.123), channel_id=1, source_target_pairs={{0,16},{8,24},{16,0},{24,8},{1,17},{9,25},{17,1},{25,9},{2,18},{10... | collective-permute-start | bytes 786440 | tf_op jit(solution)/shard_map/ppermute | solution.py:408
  409.8 27.8 %collective-permute-start.40 = (bf16[256,512]{1,0:T(8,128)(2,1)S(1)}, bf16[256,512]{1,0:T(8,128)(2,1)}, u32[]{:S(2)}, u32[]{:S(2)}) collective-permute-start(bf16[256,512]{1,0:T(8,128)(2,1)S(1)} %get-tuple-element.120), channel_id=1, source_target_pairs={{0,8},{8,0},{16,24},{24,16},{1,9},{9,1},{17,25},{25,17},{2,10},{10... | collective-permute-start | bytes 786440 | tf_op jit(solution)/shard_map/ppermute | solution.py:408
  410.7 18.4 %collective-permute-start.41 = (bf16[256,512]{1,0:T(8,128)(2,1)S(1)}, bf16[256,512]{1,0:T(8,128)(2,1)S(1)}, u32[]{:S(2)}, u32[]{:S(2)}) collective-permute-start(bf16[256,512]{1,0:T(8,128)(2,1)S(1)} %get-tuple-element.121), channel_id=1, source_target_pairs={{0,8},{8,0},{16,24},{24,16},{1,9},{9,1},{17,25},{25,17},{2,10},{10... | collective-permute-start | bytes 786440 | tf_op jit(solution)/shard_map/ppermute | solution.py:408
  413.8 14.4 %collective-permute-start.58 = (f32[4,8,1280]{2,1,0:T(8,128)S(1)}, f32[4,8,1280]{2,1,0:T(8,128)S(1)}, u32[]{:S(2)}, u32[]{:S(2)}) collective-permute-start(f32[4,8,1280]{2,1,0:T(8,128)S(1)} %bitcast_dynamic-update-slice_fusion.3), channel_id=1, source_target_pairs={{0,8},{8,0},{16,24},{24,16},{1,9},{9,1},{17,25},{25,17},{2,10},{10... | collective-permute-start | bytes 491528 | tf_op jit(solution)/shard_map/ppermute | solution.py:408
  419.5 16.8 %collective-permute-start.45 = (bf16[256,512]{1,0:T(8,128)(2,1)}, bf16[256,512]{1,0:T(8,128)(2,1)}, u32[]{:S(2)}, u32[]{:S(2)}) collective-permute-start(bf16[256,512]{1,0:T(8,128)(2,1)} %fusion.24), channel_id=1, source_target_pairs={{0,8},{8,0},{16,24},{24,16},{1,9},{9,1},{17,25},{25,17},{2,10},{10... | collective-permute-start | bytes 786440 | tf_op jit(solution)/shard_map/ppermute | solution.py:408
  430.0 7.7 %collective-permute-start.42 = (bf16[256,512]{1,0:T(8,128)(2,1)}, bf16[256,512]{1,0:T(8,128)(2,1)}, u32[]{:S(2)}, u32[]{:S(2)}) collective-permute-start(bf16[256,512]{1,0:T(8,128)(2,1)} %fusion.26), channel_id=1, source_target_pairs={{0,16},{8,24},{16,0},{24,8},{1,17},{9,25},{17,1},{25,9},{2,18},{10... | collective-permute-start | bytes 786440 | tf_op jit(solution)/shard_map/ppermute | solution.py:408
  479.7 8.1 %collective-permute-start.53 = (bf16[1,32,2112]{2,1,0:T(8,128)(2,1)S(1)}, bf16[1,32,2112]{2,1,0:T(8,128)(2,1)S(1)}, u32[]{:S(2)}, u32[]{:S(2)}) collective-permute-start(bf16[1,32,2112]{2,1,0:T(8,128)(2,1)S(1)} %get-tuple-element.143), channel_id=1, source_target_pairs={{0,8},{8,0},{16,24},{24,16},{1,9},{9,1},{17,25},{25,17},{2,10},{10... | collective-permute-start | bytes 405512 | tf_op jit(solution)/shard_map/ppermute | solution.py:408
  (53 other events, 528.2 us)
Sparse Core Ops, SparseCore 0:
  24.4 36.4 all-gather.2
  63.1 57.0 all-gather.4
  333.2 29.9 reduce-scatter.5
  366.3 36.3 reduce-scatter.3
  404.9 51.8 reduce-scatter.7

commit v2 on v1

v2 whole, which is shorter than its diff:
```python
import functools

import jax
import jax.numpy as jnp
from jax import lax
from jax.experimental import pallas as pl
from jax.experimental.pallas import tpu as pltpu
from jax.sharding import PartitionSpec as P

GROUP = 64
EPS_NORM = 1e-06
EPS_KEY = 1e-06
EPS_HEAD = 1e-05
LOW = jnp.bfloat16
F32 = jnp.float32
HIGHEST = lax.Precision.HIGHEST
BOTH = ("seq", "rows")

FORMS = {
    "nn": (((1,), (0,)), ((), ())),
    "nt": (((1,), (1,)), ((), ())),
    "tn": (((0,), (0,)), ((), ())),
}


def split_low(a):
    high = a.astype(LOW)
    return high, (a - high.astype(F32)).astype(LOW)


def mm(a, b, form):
    a_axis = 0 if form == "tn" else 1
    b_axis = 1 if form == "nt" else 0
    a_two = jnp.concatenate(split_low(a), axis=a_axis)
    b_high, b_low = split_low(b)
    b_two = jnp.concatenate([b_high, b_low], axis=1 - b_axis)
    b_two = jnp.concatenate([b_two, b_two], axis=b_axis)
    out = lax.dot_general(a_two, b_two, FORMS[form], preferred_element_type=F32)
    half = out.shape[1] // 2
    return out[:, :half] + out[:, half:]


def mm_low(a, b, form):
    return lax.dot_general(a.astype(LOW), b.astype(LOW), FORMS[form], preferred_element_type=F32)


def mm_high(a, b, form):
    return lax.dot_general(a, b, FORMS[form], precision=HIGHEST, preferred_element_type=F32)


def row_dot(a, b):
    return jnp.sum(a * b, axis=1, keepdims=True)


def place(shape, axis):
    return lax.broadcasted_iota(jnp.int32, shape, axis)


def level_table():
    time = 2 * (jnp.arange(2 * GROUP) % GROUP) + jnp.arange(2 * GROUP) // GROUP
    row, col = time[:, None], time[None, :]
    differ = row ^ col
    level = sum((differ >= 2**m).astype(jnp.int32) for m in range(1, 7))
    return jnp.where(row > col, level, -1)


def inverses(systems, level):
    size = level.shape[0]
    eye = (place((size, size), 0) == place((size, size), 1)).astype(F32)
    found = [eye - jnp.where(level == 0, a, 0.0) for a in systems]
    for m in range(1, 7):
        inner = [mm(jnp.where(level == m, a, 0.0), t, "nn") for a, t in zip(systems, found)]
        found = [t - mm(t, s, "nn") for t, s in zip(found, inner)]
    return found


def conv_active(pad_ref, taps_ref, first, count):
    cols = slice(first, first + 128)
    summed = 0.0
    for back in range(4):
        summed = summed + pad_ref[pl.ds(8 - back, count), cols] * taps_ref[3 - back : 4 - back, cols]
    return summed


def silu(x):
    return x * jax.nn.sigmoid(x)


def softplus(x):
    return jnp.maximum(x, 0.0) + jnp.log1p(jnp.exp(-jnp.abs(x)))


def cum_decays(log_decay):
    tril = (place((GROUP, GROUP), 0) >= place((GROUP, GROUP), 1)).astype(F32)
    across = (place((GROUP, 2 * GROUP), 0) <= place((GROUP, 2 * GROUP), 1) % GROUP).astype(F32)
    return mm_high(tril, log_decay, "nn"), mm_high(log_decay, across, "tn")


def twice(a):
    return jnp.concatenate([a, a], axis=0)


def group_setup(level, beta, cum, across, head, heads):
    lane = 2 * heads + head
    c = cum[:, lane : lane + 1]
    row = across[lane : lane + 1, :]
    c_two = twice(c)
    end = c[GROUP - 1 : GROUP, :]
    b = jnp.concatenate([beta[:, head : head + 1], beta[:, heads + head : heads + head + 1]], axis=0)
    strict = level >= 0
    pair = jnp.where(strict, jnp.exp(jnp.where(strict, c_two - row, 0.0)), 0.0)
    seen = place((GROUP, 2 * GROUP), 1) % GROUP <= place((GROUP, 2 * GROUP), 0)
    view = jnp.where(seen, jnp.exp(jnp.where(seen, c - row, 0.0)), 0.0)
    return c, c_two, end, b, pair, view


def forward_kernel(
    heads, first, info_ref, mixed_ref, halo_ref, taps_ref, small_ref, level_ref, start_ref,
    out_ref, raw_ref, solve_ref, fresh_ref, state_ref, end_ref, carried, padded,
):
    step = pl.program_id(0)
    count = mixed_ref.shape[0]
    block = step + first // count
    groups = count // GROUP
    wide = heads * 128

    @pl.when(step == 0)
    def _():
        carried[...] = start_ref[...]

    padded[0:8, :] = jnp.where(block > 0, halo_ref[:, : 5 * wide], 0.0)
    padded[8 : 8 + count, :] = mixed_ref[:, : 5 * wide]
    valid = (block * count + place((count, 1), 0) < info_ref[0]).astype(F32)
    level = level_ref[...]
    tail = mixed_ref[:, 6 * wide :]
    beta = jax.nn.sigmoid(tail) * valid
    log_decay = small_ref[0:1, :] * softplus(tail + small_ref[1:2, :]) * valid

    def active(slot, head):
        return silu(conv_active(padded, taps_ref, slot * wide + head * 128, count))

    def unit(x):
        return x * lax.rsqrt(row_dot(x, x) + EPS_KEY)

    queries = [unit(active(0, h)) * 128**-0.5 for h in range(heads)]
    keys = [[unit(active(1 + j, h)) for j in range(2)] for h in range(heads)]
    values = [[active(3 + j, h) for j in range(2)] for h in range(heads)]
    work = []
    for g in range(groups):
        rows = slice(g * GROUP, (g + 1) * GROUP)
        cum, across = cum_decays(log_decay[rows])
        for h in range(heads):
            key = jnp.concatenate([keys[h][0][rows], keys[h][1][rows]], axis=0)
            value = jnp.concatenate([values[h][0][rows], values[h][1][rows]], axis=0)
            c, c_two, end, b, pair, view = group_setup(level, beta[rows], cum, across, h, heads)
            gram = mm(key, key, "nt")
            work.append((g, h, rows, key, value, c, c_two, end, b, view, b * pair * gram))
    solves = inverses([w[-1] for w in work], level)
    raws = [[None] * groups for _ in range(heads)]
    ready = []
    for (g, h, rows, key, value, c, c_two, end, b, view, _), solve in zip(work, solves):
        solve_ref[g, h] = solve
        query = queries[h][rows]
        weights = view * mm(query, key, "nt")
        key_solve = mm(solve, b * jnp.exp(c_two) * key, "nn")
        pseudo = mm(solve, b * value, "nn")
        ready.append((query, weights, key_solve, pseudo))
    for (g, h, rows, key, value, c, c_two, end, b, view, _), made in zip(work, ready):
        query, weights, key_solve, pseudo = made
        state = carried[h]
        state_ref[g, h] = state
        fresh = pseudo - mm(key_solve, state, "nn")
        fresh_ref[g, h] = fresh
        carried[h] = jnp.exp(end) * state + mm(jnp.exp(end - c_two) * key, fresh, "tn")
        raws[h][g] = jnp.exp(c) * mm(query, state, "nn") + mm(weights, fresh, "nn")
    for h in range(heads):
        cols = slice(h * 128, (h + 1) * 128)
        raw = jnp.concatenate(raws[h], axis=0)
        raw_ref[:, cols] = raw
        scale = lax.rsqrt(jnp.mean(raw * raw, axis=1, keepdims=True) + EPS_HEAD)
        gated = raw * scale * small_ref[2:3, :] * silu(mixed_ref[:, 5 * wide + h * 128 : 5 * wide + (h + 1) * 128]) * valid
        out_ref[:, cols] = gated.astype(LOW)
    end_ref[...] = carried[...]


def backward_kernel(
    heads, first, info_ref, mixed_ref, halo_ref, raw_ref, grad_ref, taps_ref, small_ref, level_ref,
    solve_ref, fresh_ref, state_ref, start_ref, rim_ref,
    grad_mixed_ref, grad_taps_ref, grad_small_ref, end_ref, last_rim_ref,
    carried, padded, spread,
):
    step = pl.program_id(0)
    count = mixed_ref.shape[0]
    block = pl.num_programs(0) - 1 - step + first // count
    groups = count // GROUP
    wide = heads * 128

    @pl.when(step == 0)
    def _():
        carried[...] = start_ref[...]
        spread[0:8, :] = rim_ref[...]
        grad_taps_ref[...] = jnp.zeros_like(grad_taps_ref)
        grad_small_ref[...] = jnp.zeros_like(grad_small_ref)

    spread[count : count + 8, :] = spread[0:8, :]
    padded[0:8, :] = jnp.where(block > 0, halo_ref[:, : 5 * wide], 0.0)
    padded[8 : 8 + count, :] = mixed_ref[:, : 5 * wide]
    valid = (block * count + place((count, 1), 0) < info_ref[0]).astype(F32)
    level = level_ref[...]
    strict = level >= 0
    tail = mixed_ref[:, 6 * wide :]
    sigmoid_tail = jax.nn.sigmoid(tail)
    beta = sigmoid_tail * valid
    log_decay = small_ref[0:1, :] * softplus(tail + small_ref[1:2, :]) * valid
    lanes = place((1, 128), 1)

    grad_raws = []
    for h in range(heads):
        cols = slice(h * 128, (h + 1) * 128)
        gate_cols = slice(5 * wide + h * 128, 5 * wide + (h + 1) * 128)
        raw, gate = raw_ref[:, cols], mixed_ref[:, gate_cols]
        grad = grad_ref[:, cols] * valid
        sig = jax.nn.sigmoid(gate)
        scale = lax.rsqrt(jnp.mean(raw * raw, axis=1, keepdims=True) + EPS_HEAD)
        shaped = raw * scale
        gain = small_ref[2:3, :]
        grad_mixed_ref[:, gate_cols] = (grad * shaped * gain * sig * (1.0 + gate * (1.0 - sig))).astype(LOW)
        grad_normed = grad * gate * sig
        grad_small_ref[2:3, :] += jnp.sum(grad_normed * shaped, axis=0, keepdims=True)
        grad_shaped = grad_normed * gain
        grad_raws.append(scale * (grad_shaped - shaped * jnp.mean(grad_shaped * shaped, axis=1, keepdims=True)))

    def summed(slot, head):
        return conv_active(padded, taps_ref, slot * wide + head * 128, count)

    def unit(x):
        return x * lax.rsqrt(row_dot(x, x) + EPS_KEY)

    queries = [unit(silu(summed(0, h))) * 128**-0.5 for h in range(heads)]
    keys = [[unit(silu(summed(1 + j, h))) for j in range(2)] for h in range(heads)]
    values = [[silu(summed(3 + j, h)) for j in range(2)] for h in range(heads)]
    work = []
    for g in reversed(range(groups)):
        rows = slice(g * GROUP, (g + 1) * GROUP)
        cum, across = cum_decays(log_decay[rows])
        for h in range(heads):
            key = jnp.concatenate([keys[h][0][rows], keys[h][1][rows]], axis=0)
            value = jnp.concatenate([values[h][0][rows], values[h][1][rows]], axis=0)
            c, c_two, end, b, pair, view = group_setup(level, beta[rows], cum, across, h, heads)
            query, grad_raw = queries[h][rows], grad_raws[h][rows]
            scores = view * mm(query, key, "nt")
            late = mm(scores, grad_raw, "tn")
            grad_scores = view * mm(grad_raw, fresh_ref[g, h], "nt")
            work.append((g, h, rows, key, value, c, c_two, end, b, pair, query, grad_raw, late, grad_scores))
    grad_parts = [[[None] * groups for _ in range(5)] for _ in range(heads)]
    grad_betas, grad_cums = [0.0] * groups, [0.0] * groups
    for (g, h, rows, key, value, c, c_two, end, b, pair, query, grad_raw, late, grad_scores) in work:
        state, fresh, solve = state_ref[g, h], fresh_ref[g, h], solve_ref[g, h]
        grad_state = carried[h]
        grow, fade, all_fade = jnp.exp(c_two), jnp.exp(end - c_two), jnp.exp(end)
        grad_seen = jnp.exp(c) * grad_raw
        grad_fresh = late + mm(fade * key, grad_state, "nn")
        adjoint = mm(solve, grad_fresh, "tn")
        carried[h] = (
            all_fade * grad_state
            + mm(query, grad_seen, "tn")
            - mm(b * grow * key, adjoint, "tn")
        )
        grad_query = mm(grad_seen, state, "nt") + mm(grad_scores, key, "nn")
        part_one = mm(grad_scores, query, "tn")
        part_two = fade * mm(fresh, grad_state, "nt")
        part_three = -mm(adjoint, state, "nt")
        coupled = jnp.where(strict, -mm(adjoint, fresh, "nt"), 0.0) * pair
        part_four = mm(coupled, key, "nn")
        part_five = mm(b * coupled, key, "tn")
        grad_key = part_one + part_two + b * grow * part_three + b * part_four + part_five
        grad_value = b * adjoint
        through = grow * row_dot(part_three, key)
        pulled = row_dot(part_four, key)
        grad_b = row_dot(adjoint, value) + through + pulled
        ends = row_dot(part_two, key)
        grad_c = b * (through + pulled) - ends - row_dot(part_one + part_five, key)
        grad_c = row_dot(query, grad_query) + grad_c[:GROUP] + grad_c[GROUP:]
        grad_end = jnp.sum(ends) + jnp.sum(all_fade * grad_state * state)
        grad_c = grad_c + jnp.where(place((GROUP, 1), 0) == GROUP - 1, grad_end, 0.0)
        grad_cums[g] = grad_cums[g] + jnp.where(lanes == 2 * heads + h, grad_c, 0.0)
        for j in range(2):
            half = slice(j * GROUP, (j + 1) * GROUP)
            grad_betas[g] = grad_betas[g] + jnp.where(lanes == j * heads + h, grad_b[half], 0.0)
            grad_parts[h][1 + j][g] = grad_key[half]
            grad_parts[h][3 + j][g] = grad_value[half]
        grad_parts[h][0][g] = grad_query
    triu = (place((GROUP, GROUP), 0) <= place((GROUP, GROUP), 1)).astype(F32)
    grad_log = jnp.concatenate([mm_high(triu, x, "nn") for x in grad_cums], axis=0)
    grad_beta = jnp.concatenate(grad_betas, axis=0)
    grad_decay = grad_log * small_ref[0:1, :] * valid * jax.nn.sigmoid(tail + small_ref[1:2, :])
    grad_mixed_ref[:, 6 * wide :] = (
        grad_beta * beta * (1.0 - sigmoid_tail) + grad_decay
    ).astype(LOW)
    grad_small_ref[0:1, :] += jnp.sum(grad_log * log_decay, axis=0, keepdims=True)
    grad_small_ref[1:2, :] += jnp.sum(grad_decay, axis=0, keepdims=True)

    for h in range(heads):
        for slot in range(5):
            cols = slice(slot * wide + h * 128, slot * wide + (h + 1) * 128)
            grad = jnp.concatenate(grad_parts[h][slot], axis=0)
            pre = summed(slot, h)
            sig = jax.nn.sigmoid(pre)
            if slot < 3:
                act = pre * sig
                scale = lax.rsqrt(row_dot(act, act) + EPS_KEY)
                shaped = act * scale
                if slot == 0:
                    grad = grad * 128**-0.5
                grad = scale * (grad - shaped * row_dot(grad, shaped))
            grad = grad * sig * (1.0 + pre * (1.0 - sig))
            spread[0:count, cols] = grad
            back = 0.0
            for ahead in range(4):
                back = back + spread[pl.ds(ahead, count), cols] * taps_ref[3 - ahead : 4 - ahead, cols]
            grad_mixed_ref[:, cols] = back.astype(LOW)
            for tap in range(4):
                grad_taps_ref[tap : tap + 1, cols] += jnp.sum(
                    grad * padded[pl.ds(5 + tap, count), cols], axis=0, keepdims=True
                )
    end_ref[...] = carried[...]
    last_rim_ref[...] = spread[0:8, :]


def step_tokens(tokens):
    return min(128, tokens)


def block_specs(heads, count, first, per, order):
    wide = heads * 128
    all_wide = 6 * wide + 128
    skip, per = first // count, max(per // count, 1)

    def moved(i, info):
        return ((i // per) ^ info[1]) * per + i % per

    whole = lambda *shape: pl.BlockSpec(shape, lambda i, info: (0,) * len(shape))
    return dict(
        mixed=pl.BlockSpec((count, all_wide), lambda i, info: (order(i) + skip, 0)),
        halo=pl.BlockSpec(
            (8, all_wide), lambda i, info: (jnp.maximum((order(i) + skip) * (count // 8) - 1, 0), 0)
        ),
        mixed_part=pl.BlockSpec((count, all_wide), lambda i, info: (order(i), 0)),
        head=pl.BlockSpec((count, wide), lambda i, info: (order(i), 0)),
        moved_head=pl.BlockSpec((count, wide), lambda i, info: (moved(order(i), info), 0)),
        taps=whole(8, 5 * wide),
        small=whole(8, 128),
        level=whole(2 * GROUP, 2 * GROUP),
        state=whole(heads, 128, 128),
        kept=pl.BlockSpec((count // GROUP, heads, 128, 128), lambda i, info: (order(i), 0, 0, 0)),
    )


VMEM_BYTES = 56 * 2**20


def mixer_forward(heads, first, tokens, info, mixed, taps, small, level, start):
    count = step_tokens(tokens)
    steps = tokens // count
    wide = heads * 128
    s = block_specs(heads, count, first, count, lambda i: i)
    kept = jax.ShapeDtypeStruct((tokens // GROUP, heads, 128, 128), F32)
    return pl.pallas_call(
        functools.partial(forward_kernel, heads, first),
        grid_spec=pltpu.PrefetchScalarGridSpec(
            num_scalar_prefetch=1,
            grid=(steps,),
            in_specs=[s["mixed"], s["halo"], s["taps"], s["small"], s["level"], s["state"]],
            out_specs=[s["head"], s["head"], s["kept"], s["kept"], s["kept"], s["state"]],
            scratch_shapes=[pltpu.VMEM((heads, 128, 128), F32), pltpu.VMEM((count + 8, 5 * wide), F32)],
        ),
        out_shape=[
            jax.ShapeDtypeStruct((tokens, wide), LOW),
            jax.ShapeDtypeStruct((tokens, wide), F32),
            kept, kept, kept,
            jax.ShapeDtypeStruct(start.shape, F32),
        ],
        compiler_params=pltpu.CompilerParams(vmem_limit_bytes=VMEM_BYTES),
        cost_estimate=pl.CostEstimate(
            flops=tokens * heads * (4_000_000 if first == 0 else 18_000_000), bytes_accessed=tokens * heads * 10_000, transcendentals=0
        ),
        name="mixer_forward",
    )(info, mixed, mixed, taps, small, level, start)


def mixer_backward(
    heads, first, tokens, per, info, mixed, raw, grad, taps, small, level, solve, fresh, state, start, rim
):
    count = step_tokens(tokens)
    steps = tokens // count
    wide = heads * 128
    s = block_specs(heads, count, first, per, lambda i: steps - 1 - i)
    return pl.pallas_call(
        functools.partial(backward_kernel, heads, first),
        grid_spec=pltpu.PrefetchScalarGridSpec(
            num_scalar_prefetch=1,
            grid=(steps,),
            in_specs=[
                s["mixed"], s["halo"], s["head"], s["moved_head"], s["taps"], s["small"], s["level"],
                s["kept"], s["kept"], s["kept"], s["state"], s["taps"],
            ],
            out_specs=[s["mixed_part"], s["taps"], s["small"], s["state"], s["taps"]],
            scratch_shapes=[
                pltpu.VMEM((heads, 128, 128), F32),
                pltpu.VMEM((count + 8, 5 * wide), F32),
                pltpu.VMEM((count + 8, 5 * wide), F32),
            ],
        ),
        out_shape=[
            jax.ShapeDtypeStruct((tokens, mixed.shape[1]), LOW),
            jax.ShapeDtypeStruct((8, 5 * wide), F32),
            jax.ShapeDtypeStruct((8, 128), F32),
            jax.ShapeDtypeStruct(start.shape, F32),
            jax.ShapeDtypeStruct(rim.shape, F32),
        ],
        compiler_params=pltpu.CompilerParams(vmem_limit_bytes=VMEM_BYTES),
        cost_estimate=pl.CostEstimate(
            flops=tokens * heads * 26_000_000, bytes_accessed=tokens * heads * 10_000, transcendentals=0
        ),
        name="mixer_backward",
    )(info, mixed, mixed, raw, grad, taps, small, level, solve, fresh, state, start, rim)


def swap(array, axis, bits):
    return lax.ppermute(array, axis, [(i, i ^ bits) for i in range(lax.axis_size(axis))])


def on_square():
    return lax.axis_size("seq") == 4


def power_of_two(axis):
    return lax.axis_size(axis) & (lax.axis_size(axis) - 1) == 0


def after(array, *others):
    return lax.optimization_barrier((array,) + others)[0]


def spread_out(array):
    if not on_square():
        whole = lax.all_gather(array, "seq")
        return [whole[i] for i in range(whole.shape[0])]
    far, beside, below = (swap(array, "seq", bits) for bits in (3, 1, 2))
    return [array, beside, below, far]


def in_place_order(blocks):
    if not on_square():
        return jnp.concatenate(blocks, axis=0)
    me = lax.axis_index("seq")
    size = blocks[0].shape[0]
    out = jnp.zeros((len(blocks) * size,) + blocks[0].shape[1:], blocks[0].dtype)
    for bits, block in enumerate(blocks):
        out = lax.dynamic_update_slice(out, block, ((me ^ bits) * size, 0))
    return out


def row_block(array, index):
    size = array.shape[0] // lax.axis_size("seq")
    return lax.dynamic_slice_in_dim(array, index * size, size, 0)


def to_send(array):
    if not on_square():
        return [array.astype(LOW)]
    me = lax.axis_index("seq")
    return [row_block(array, me ^ bits).astype(LOW) for bits in (3, 1, 2)]


def send(blocks):
    if not on_square():
        return [lax.psum_scatter(blocks[0], "seq", scatter_dimension=0, tiled=True)]
    return [swap(block, "seq", bits) for bits, block in zip((3, 1, 2), blocks)]


def total(array, got):
    if not on_square():
        return got[0].astype(F32)
    return row_block(array, lax.axis_index("seq")) + sum(block.astype(F32) for block in got)


def exchange(blocks):
    if not on_square():
        return lax.all_to_all(blocks, "seq", 0, 0, tiled=True)
    me = lax.axis_index("seq")
    others = (3, 1, 2)
    sends = lax.optimization_barrier(tuple(lax.dynamic_index_in_dim(blocks, me ^ bits, 0, True) for bits in others))
    got = lax.optimization_barrier(tuple(swap(block, "seq", bits) for bits, block in zip(others, sends)))
    out = blocks
    for bits, block in zip(others, got):
        out = lax.dynamic_update_slice(out, block, (me ^ bits, 0, 0))
    return out


def sum_over(array, axis):
    if not power_of_two(axis):
        return lax.psum(array, axis)
    bits = 1
    while bits < lax.axis_size(axis):
        array = array + swap(array, axis, bits)
        bits *= 2
    return array


def gather_rows(mine):
    whole = lax.all_gather(mine, "rows", axis=0)
    rows, count, size, width = whole.shape
    return whole.transpose(1, 0, 2, 3).reshape(count * rows * size, width)


def by_rows(grad):
    count, rows = lax.axis_size("seq"), lax.axis_size("rows")
    size = grad.shape[0] // (count * rows)
    grad = grad.astype(LOW).reshape(count, rows, size, grad.shape[1])
    return grad.transpose(1, 0, 2, 3).reshape(-1, grad.shape[3])


def sum_rows(grad):
    count = lax.axis_size("seq")
    summed = lax.psum_scatter(grad, "rows", scatter_dimension=0, tiled=True)
    return summed.reshape(count, -1, grad.shape[1])


def project(left, right):
    return jnp.dot(left, right, preferred_element_type=F32)


def outer_sum(left, right):
    return lax.dot_general(left, right, FORMS["tn"], preferred_element_type=F32)


def back_project(left, right):
    return lax.dot_general(left, right, FORMS["nt"], preferred_element_type=F32)


def norm_scale(features):
    return lax.rsqrt(jnp.mean(features * features, axis=-1, keepdims=True) + EPS_NORM)


def norm_back(features, scale, grad):
    return scale * grad - features * scale**3 * jnp.mean(grad * features, axis=-1, keepdims=True)


def on_device(
    block_input, valid_length, query_weight, key_weight, value_weight, beta_weight, decay_weight, gate_weight,
    out_weight, ffn_gate_weight, ffn_up_weight, ffn_down_weight, norm_gain, ffn_norm_gain, head_norm_gain,
    decay_log, decay_bias, conv_weight, output_grad,
):
    count = lax.axis_size("seq")
    me = lax.axis_index("seq")
    rows_here, tokens_here, model_width = block_input.shape
    share = query_weight.shape[0]
    head_count = decay_log.shape[0]
    heads = max(1, head_count // count)
    blocks = head_count // heads
    copies = count // blocks
    block = me // copies
    wide = heads * 128
    hidden = ffn_gate_weight.shape[1] // count

    def cut(weight, pieces, at):
        width = weight.shape[1] // (pieces * blocks)
        at = at // copies
        return [
            weight[:, (p * blocks + at) * width : (p * blocks + at + 1) * width] for p in range(pieces)
        ]

    def cut_hidden(weight, at):
        return [weight[:, at * hidden : (at + 1) * hidden]]

    gains = jnp.stack([norm_gain, ffn_norm_gain], axis=1)

    def tail_of(at):
        parts = cut(beta_weight, 2, at) + cut(decay_weight, 1, at) + [gains]
        return parts + [jnp.zeros((share, 128 - 3 * heads - 2), LOW)]

    def first_of(at):
        parts = cut(query_weight, 1, at) + cut(key_weight, 2, at) + cut(value_weight, 2, at)
        return jnp.concatenate(parts + cut(gate_weight, 1, at) + tail_of(at), axis=1)

    def rest_of(at):
        order = [at ^ bits for bits in range(count)] if on_square() else range(0, count, copies)
        parts = sum((cut(out_weight, 1, other) for other in order), [])
        parts += cut_hidden(ffn_gate_weight, at) + cut_hidden(ffn_up_weight, at) + cut_hidden(ffn_down_weight, at)
        return jnp.concatenate(parts, axis=1)

    def pack(part):
        return jnp.stack([part(at) for at in range(count)])

    first_share = exchange(pack(first_of))
    mixed_weight = gather_rows(first_share)
    own = after(block_input.reshape(tokens_here, model_width), first_share)
    everyone = in_place_order(spread_out(own))
    rest_pack, everyone = lax.optimization_barrier((pack(rest_of), everyone))
    rest_share = exchange(rest_pack)
    rest_weight = gather_rows(rest_share)
    out_all = rest_weight[:, : blocks * wide]
    ffn_in = rest_weight[:, blocks * wide : blocks * wide + 2 * hidden]
    ffn_down = rest_weight[:, blocks * wide + 2 * hidden :]
    if on_square():
        out_own = out_all[:, :wide]
    else:
        out_own = lax.dynamic_slice_in_dim(out_all, block * wide, wide, 1)
    gain_first = mixed_weight[:, 6 * wide + 3 * heads].astype(F32)
    gain_second = mixed_weight[:, 6 * wide + 3 * heads + 1].astype(F32)

    def block_lanes(vector, first):
        mine = lax.dynamic_slice_in_dim(vector, block * heads, heads)
        return jnp.pad(mine, (first, 128 - first - heads))

    small = jnp.stack([block_lanes(-jnp.exp(decay_log), 2 * heads), block_lanes(decay_bias, 2 * heads), head_norm_gain])
    small = jnp.pad(small, ((0, 5), (0, 0)))
    taps = [
        lax.dynamic_slice_in_dim(conv_weight, (slot * blocks + block) * wide, wide, 1) for slot in range(5)
    ]
    taps = jnp.pad(jnp.concatenate(taps, axis=1), ((0, 8 - conv_weight.shape[0]), (0, 0)))
    level = level_table()
    info = jnp.stack([valid_length[0], me if on_square() else jnp.int32(0)])

    length = count * tokens_here
    part = length // 2
    tie = lax.optimization_barrier

    tokens_all = everyone.astype(F32)
    normed = (tokens_all * norm_scale(tokens_all) * gain_first).astype(LOW)
    mixed = project(normed, mixed_weight)
    mixed, own_grad = tie((mixed, output_grad.reshape(tokens_here, model_width)))
    grads_got = spread_out(own_grad)
    zero_state = jnp.zeros((heads, 128, 128), F32)
    gated_a, *kept_a, end = mixer_forward(heads, 0, part, info, mixed, taps, small, level, zero_state)
    end, grads_got, everyone_late = tie((end, grads_got, everyone))
    gated_got_a = spread_out(gated_a)
    gated_b, *kept_b, end = mixer_forward(heads, part, part, info, mixed, taps, small, level, end)
    gated_b, gated_got_a = tie((gated_b, gated_got_a))
    gated_got_b = spread_out(gated_b)
    grad_branch = in_place_order(grads_got)

    def feed_forward(index, gated_got, got=None):
        rows = slice(index * part, (index + 1) * part)
        gated_all = jnp.concatenate(gated_got[:: 1 if on_square() else copies], axis=1)
        second = everyone_late[rows].astype(F32) + back_project(gated_all, out_all)
        normed_two = (second * norm_scale(second) * gain_second).astype(LOW)
        if got is not None:
            normed_two, got = tie((normed_two, got))
        acts = project(normed_two, ffn_in)
        gate_act, up_act = acts[:, :hidden], acts[:, hidden:]
        sig = jax.nn.sigmoid(gate_act)
        hidden_low = (gate_act * sig * up_act).astype(LOW)
        grad_hidden = project(grad_branch[rows], ffn_down)
        grad_acts = [grad_hidden * up_act * sig * (1.0 + gate_act * (1.0 - sig)), grad_hidden * gate_act * sig]
        grad_acts = jnp.concatenate(grad_acts, axis=1).astype(LOW)
        return second, normed_two, hidden_low, grad_acts, back_project(grad_acts, ffn_in), got

    def second_back(index, second, partial, got):
        grad = total(partial, got) * gain_second
        second = row_block(second, me)
        out_grad = row_block(grad_branch[index * part : (index + 1) * part], me)
        return (out_grad.astype(F32) + norm_back(second, norm_scale(second), grad)).astype(LOW)

    second_a, normed_two_a, hidden_a, grad_acts_a, partial_a, _ = feed_forward(0, gated_got_a)
    sends_a, gated_got_b = tie((to_send(partial_a), gated_got_b))
    got_a = send(sends_a)
    second_b, normed_two_b, hidden_b, grad_acts_b, partial_b, got_a = feed_forward(1, gated_got_b, got_a)
    sends_b, hidden_b, grad_acts_b = tie((to_send(partial_b), hidden_b, grad_acts_b))
    got_b = send(sends_b)

    join_parts = lambda a, b: jnp.concatenate([a, b], axis=0)
    normed_two, hidden_low = join_parts(normed_two_a, normed_two_b), join_parts(hidden_a, hidden_b)
    grad_acts = join_parts(grad_acts_a, grad_acts_b)
    early_in = outer_sum(normed_two, grad_acts).astype(LOW)
    early_down = outer_sum(grad_branch, hidden_low).astype(LOW)
    grad_second_a = second_back(0, second_a, partial_a, got_a)
    got_b, early_in, early_down, grad_second_a = tie((got_b, early_in, early_down, grad_second_a))
    grads_two_b = spread_out(second_back(1, second_b, partial_b, got_b))
    early = by_rows(jnp.concatenate([early_in, early_down], axis=1))
    down = back_project(hidden_low, ffn_down)
    down_sends = to_send(down)
    grads_two_b, early, down_sends, grad_second_a = tie((grads_two_b, early, down_sends, grad_second_a))
    early = sum_rows(early)
    grads_two_a = spread_out(grad_second_a)

    grad_gated = project(jnp.concatenate(grads_two_b, axis=0), out_own)
    rim = jnp.zeros((8, 5 * wide), F32)
    grad_pre_b, taps_b, small_b, end, rim = mixer_backward(
        heads, part, part, part // count, info, mixed, kept_b[0], grad_gated, taps, small, level, *kept_b[1:],
        zero_state, rim,
    )
    end, grads_two_a, down_sends = tie((end, grads_two_a, down_sends))
    down_got = send(down_sends)
    grad_gated = project(jnp.concatenate(grads_two_a, axis=0), out_own)
    grad_second = join_parts(in_place_order(grads_two_a), in_place_order(grads_two_b))

    def once(array):
        return array if copies == 1 else array * (me % copies == 0).astype(array.dtype)

    grad_pre_a, taps_a, small_a, end, rim = mixer_backward(
        heads, 0, part, part // count, info, mixed, kept_a[0], grad_gated, taps, small, level, *kept_a[1:], end, rim
    )
    grad_pre = once(join_parts(grad_pre_a, grad_pre_b))
    out_grad = once(outer_sum(grad_second, join_parts(gated_a, gated_b)).astype(LOW))
    late = by_rows(jnp.concatenate([outer_sum(normed, grad_pre).astype(LOW), out_grad], axis=1))
    grad_taps, grad_small = taps_a + taps_b, small_a + small_b
    grad_pre, late, down_got, early, grad_taps, grad_small = tie(
        (grad_pre, late, down_got, early, grad_taps, grad_small)
    )
    late = sum_rows(late)
    grad_normed = back_project(grad_pre, mixed_weight)
    grad_normed_got = send(to_send(grad_normed))

    def at_block(vector, first, width):
        mine = once(vector[first : first + width])
        return lax.dynamic_update_slice(jnp.zeros((blocks * width,), F32), mine, (block * width,))

    flat = [once(grad_small[2]), at_block(grad_small[0], 2 * heads, heads), at_block(grad_small[1], 2 * heads, heads)]
    flat = jnp.concatenate(flat)
    taps_wide = 5 * wide
    flat = jnp.pad(flat, (0, -flat.shape[0] % taps_wide)).reshape(-1, taps_wide)
    pooled = sum_over(jnp.concatenate([once(grad_taps[:4]), flat], axis=0), "rows")
    by_place = lax.dynamic_update_slice(jnp.zeros((blocks, 4, taps_wide), F32), pooled[None, :4], (block, 0, 0))
    pooled = sum_over(jnp.concatenate([by_place.reshape(-1, taps_wide), pooled[4:]], axis=0), "seq")
    ends = [128, 128 + head_count, 128 + 2 * head_count]

    second = row_block(join_parts(second_a, second_b), me)
    result = (second + total(down, down_got)).astype(LOW).reshape(block_input.shape)
    tokens = own.astype(F32)
    grad_tokens = norm_back(tokens, norm_scale(tokens), total(grad_normed, grad_normed_got) * gain_first)
    grad_input = row_block(grad_second, me).astype(F32) + grad_tokens
    grad_input = grad_input.reshape(block_input.shape)

    def join(grads, first, pieces, width, every=copies):
        return jnp.concatenate(
            [
                grads[b, :, first + p * width : first + (p + 1) * width]
                for p in range(pieces)
                for b in range(0, count, every)
            ],
            axis=1,
        ).astype(F32)

    early = exchange(early)
    late, early, result, grad_input, pooled = tie((late, early, result, grad_input, pooled))
    late = exchange(late)
    flat = pooled[4 * blocks :].reshape(-1)
    grad_conv = pooled[: 4 * blocks].reshape(blocks, 4, taps_wide)
    grad_conv = jnp.concatenate(
        [grad_conv[b, :, slot * wide : (slot + 1) * wide] for slot in range(5) for b in range(blocks)], axis=1
    )
    grad_query = join(late, 0, 1, wide)
    grad_key = join(late, wide, 2, wide)
    grad_value = join(late, 3 * wide, 2, wide)
    grad_beta = join(late, 6 * wide, 2, heads)
    grad_decay = join(late, 6 * wide + 2 * heads, 1, heads)
    grad_gate = join(late, 5 * wide, 1, wide)
    grad_ffn_gate = join(early, 0, 1, hidden, 1)
    grad_ffn_up = join(early, hidden, 1, hidden, 1)
    grad_ffn_down = join(early, 2 * hidden, 1, hidden, 1)

    def gain_grad(gain, *pairs):
        summed = sum(jnp.sum(weight.astype(F32) * grad, axis=1) for weight, grad in pairs)
        return summed / gain.astype(F32)

    grad_gain_first = gain_grad(
        norm_gain, (query_weight, grad_query), (key_weight, grad_key), (value_weight, grad_value),
        (beta_weight, grad_beta), (decay_weight, grad_decay), (gate_weight, grad_gate),
    )
    grad_gain_second = gain_grad(ffn_norm_gain, (ffn_gate_weight, grad_ffn_gate), (ffn_up_weight, grad_ffn_up))
    return (
        result,
        grad_input,
        grad_query,
        grad_key,
        grad_value,
        grad_beta,
        grad_decay,
        grad_gate,
        join(late, 6 * wide + 128, 1, wide),
        grad_ffn_gate,
        grad_ffn_up,
        grad_ffn_down,
        grad_gain_first,
        grad_gain_second,
        flat[: ends[0]],
        flat[ends[0] : ends[1]],
        flat[ends[1] : ends[2]],
        grad_conv,
    )


def solution(mesh):
    tokens, weight, vector, whole = P("rows", "seq", None), P(BOTH, None), P(BOTH), P()
    return jax.shard_map(
        on_device,
        mesh=mesh,
        in_specs=(tokens, P("rows")) + (weight,) * 10 + (vector,) * 2 + (whole,) * 4 + (tokens,),
        out_specs=(tokens, tokens) + (weight,) * 10 + (vector,) * 2 + (whole,) * 4,
        check_vma=False,
    )
```

time: 510 us -> 373 us (0.73)
  waiting for transfers between devices: 177 us -> 87.7 us
  local copies, waits for them, and re-layouts: 87 us -> 50.3 us
  matrix products: 56.1 us -> 44.8 us
  starting transfers between devices: 65.8 us -> 55.8 us
  Pallas kernels: 81.3 us -> 91 us
    ppermute x60 -> x47, waiting for transfers between devices: 142 us -> 87.3 us  [swap(): lax.ppermute(array, axis, [(i, i ^ bits) for i in range(lax.axis_size(axi...]
    all_gather x2, waiting for transfers between devices: 35.7 us -> 0.27 us  [gather_rows(): whole = lax.all_gather(mine, 'rows', axis=0)]
    ppermute x60 -> x47, starting transfers between devices: 65.5 us -> 55.4 us  [swap(): lax.ppermute(array, axis, [(i, i ^ bits) for i in range(lax.axis_size(axi...]
    concatenate x7 -> x16, local copies, waits for them, and re-layouts: 12.3 us -> 2.22 us  [the longest x1 0.69 us: on_device(): jnp.concatenate(taps, axis=1)]
    pallas_call x2 -> x4, Pallas kernels: 81.3 us -> 91 us  [the longest x2 53.1 us: mixer_backward(): pl.pallas_call(functools.partial(backward_kernel, heads, first), grid_spe...]
    dot_general x5 -> x4, matrix products: 19.6 us -> 10.9 us  [outer_sum(): return lax.dot_general(left, right, FORMS['tn'], preferred_element_type=F32)]
    add x11 -> x7, other arithmetic: 8 us -> 0.07 us  [the longest x5 0.06 us: sum_over(): array = array + swap(array, axis, bits)]
    reshape x26 -> x5, local copies, waits for them, and re-layouts: 12.1 us -> 4.88 us  [the longest x2 4.81 us: by_rows(): grad = grad.astype(LOW).reshape(count, rows, size, grad.shape[1])]
  transfers between devices with their start and end apart: 65 -> 51, of which waited for: 40 -> 18; matrix products, arithmetic and copies ran while one was open for 23% -> 23% of each run, Pallas kernels for 0% -> 25%
where the time goes in v2:
time: 373 us; the launch traced here: 369 us
  Pallas kernels  91 us (24%)
  waiting for transfers between devices  87.7 us (24%)
  starting transfers between devices  55.8 us (15%)
  local copies, waits for them, and re-layouts  50.3 us (13%)
  matrix products  44.8 us (12%)
  other arithmetic  23.3 us (6%)
  between operations  16.6 us (4%)
    ppermute x47, waiting for transfers between devices, swap(): lax.ppermute(array, axis, [(i, i ^ bits) for i in range(lax.axis_size(axi...  87.3 us
    ppermute x47, starting transfers between devices, swap(): lax.ppermute(array, axis, [(i, i ^ bits) for i in range(lax.axis_size(axi...  55.4 us
    pallas_call x2, Pallas kernels, mixer_backward(): pl.pallas_call(functools.partial(backward_kernel, heads, first), grid_spe...  53.1 us
    pallas_call x2, Pallas kernels, mixer_forward(): pl.pallas_call(functools.partial(forward_kernel, heads, first), grid_spec...  37.9 us
    dot_general x7, matrix products, project(): return jnp.dot(left, right, preferred_element_type=F32)  17.3 us
    dot_general x6, matrix products, back_project(): return lax.dot_general(left, right, FORMS['nt'], preferred_element_type=F32)  16.6 us
    dot_general x4, matrix products, outer_sum(): return lax.dot_general(left, right, FORMS['tn'], preferred_element_type=F32)  10.9 us
    unnamed x151, local copies, waits for them, and re-layouts  9.72 us
  transfers between devices with their start and end apart: 51, of which 18 were waited for; matrix products, arithmetic and copies ran while one was open for 23% of the time, Pallas kernels for 25%

profile of v2, /device:TPU:0, one launch (start us, length us, event | category | flops | bytes accessed | tf_op | source)
XLA Modules:
  0.0 369.3 jit_solution(2993696635435017937)
XLA Ops:
  14.1 4.0 %collective-permute-start = (bf16[1,32,1664]{2,1,0:T(8,128)(2,1)S(1)}, bf16[1,32,1664]{2,1,0:T(8,128)(2,1)S(1)}, u32[]{:S(2)}, u32[]{:S(2)}) collective-permute-start(bf16[1,32,1664]{2,1,0:T(8,128)(2,1)S(1)} %get-tuple-element.129), channel_id=1, source_target_pairs={{0,24},{8,16},{16,8},{24,0},{1,25},{9,17},{17,9},{25,1},{2,26},{10... | collective-permute-start | bytes 319496 | tf_op jit(solution)/shard_map/ppermute | solution.py:430
  18.7 3.2 collective-permute-done
  21.9 1.7 collective-permute-done.1
  29.3 11.0 %collective-permute-done.3 = bf16[256,1024]{1,0:T(8,128)(2,1)} collective-permute-done((bf16[256,1024]{1,0:T(8,128)(2,1)S(1)}, bf16[256,1024]{1,0:T(8,128)(2,1)}, u32[]{:S(2)}, u32[]{:S(2)}) %collective-permute-start.3) | collective-permute-done | bytes 524320 | tf_op jit(solution)/shard_map/ppermute | solution.py:430
  41.4 8.7 %collective-permute-done.4 = bf16[256,1024]{1,0:T(8,128)(2,1)} collective-permute-done((bf16[256,1024]{1,0:T(8,128)(2,1)S(1)}, bf16[256,1024]{1,0:T(8,128)(2,1)}, u32[]{:S(2)}, u32[]{:S(2)}) %collective-permute-start.4) | collective-permute-done | bytes 524320 | tf_op jit(solution)/shard_map/ppermute | solution.py:430
  52.4 2.9 collective-permute-start.9
  56.5 4.9 %collective-permute-done.9 = bf16[1,32,3136]{2,1,0:T(8,128)(2,1)S(1)} collective-permute-done((bf16[1,32,3136]{2,1,0:T(8,128)(2,1)S(1)}, bf16[1,32,3136]{2,1,0:T(8,128)(2,1)S(1)}, u32[]{:S(2)}, u32[]{:S(2)}) %collective-permute-start.9) | collective-permute-done | bytes 200736 | tf_op jit(solution)/shard_map/ppermute | solution.py:430
  70.6 2.3 copy.190
  73.3 6.2 %fusion.82.mixed_ref.halo_ref = f32[1024,1664]{1,0:T(8,128)} fusion(bf16[1024,1664]{1,0:T(8,128)(2,1)S(1)} %bitcast.296, bf16[1024,1024]{1,0:T(8,128)(2,1)S(1)} %constant_dynamic-update-slice_fusion.61, f32[1024]{0:T(1024)S(1)} %get-tuple-element.241, f32[1024]{0:T(1024)S(1)} %add_rsqrt_fusion), kind=kOutput, calls=%fused_computation.112 | convolution fusion | flops 3493855232 | bytes 12328960 | tf_op jit(solution)/shard_map/dot_general | solution.py:531
  80.9 2.0 collective-permute-start.8
  85.4 18.8 %mixer_forward.2 = (bf16[512,256]{1,0:T(8,128)(2,1)}, f32[512,256]{1,0:T(8,128)}, f32[8,2,128,128]{3,2,1,0:T(8,128)}, f32[8,2,128,128]{3,2,1,0:T(8,128)}, f32[8,...) custom-call(s32[2]{0:T(128)} %pad_add_fusion.info_ref, f32[1024,1664]{1,0:T(8,128)} %fusion.82.mixed_ref.halo_ref, ...), custom_call_target="tpu_custom_call" | custom-call | flops 4096000000 | bytes 10240000 | tf_op jit(solution)/shard_map/mixer_forward/pallas_call | solution.py:368
  105.7 2.0 collective-permute-start.14
  107.7 19.2 %mixer_forward.3 = (bf16[512,256]{1,0:T(8,128)(2,1)}, f32[512,256]{1,0:T(8,128)}, f32[8,2,128,128]{3,2,1,0:T(8,128)}, f32[8,2,128,128]{3,2,1,0:T(8,128)}, f32[8,...) custom-call(s32[2]{0:T(128)} %pad_add_fusion.info_ref, f32[1024,1664]{1,0:T(8,128)} %fusion.82.mixed_ref.halo_ref, ...), custom_call_target="tpu_custom_call" | custom-call | flops 18432000000 | bytes 10240000 | tf_op jit(solution)/shard_map/mixer_forward/pallas_call | solution.py:368
  128.5 2.0 collective-permute-start.17
  133.7 3.5 copy.191
  139.1 1.7 fusion.18
  142.7 1.8 fusion.16
  144.7 2.5 multiply_reduce_fusion
  147.2 2.4 collective-permute-start.18
  151.0 6.3 %collective-permute-done.18 = bf16[128,1024]{1,0:T(8,128)(2,1)S(1)} collective-permute-done((bf16[128,1024]{1,0:T(8,128)(2,1)S(1)}, bf16[128,1024]{1,0:T(8,128)(2,1)S(1)}, u32[]{:S(2)}, u32[]{:S(2)}) %collective-permute-start.18) | collective-permute-done | bytes 262176 | tf_op jit(solution)/shard_map/ppermute | solution.py:430
  157.3 4.9 %collective-permute-done.19 = bf16[128,1024]{1,0:T(8,128)(2,1)S(1)} collective-permute-done((bf16[128,1024]{1,0:T(8,128)(2,1)S(1)}, bf16[128,1024]{1,0:T(8,128)(2,1)S(1)}, u32[]{:S(2)}, u32[]{:S(2)}) %collective-permute-start.19) | collective-permute-done | bytes 262176 | tf_op jit(solution)/shard_map/ppermute | solution.py:430
  162.3 1.7 fusion.14
  165.5 2.0 fusion.12
  168.6 1.9 convolution_convert_fusion.2
  170.5 1.9 fusion.28
  172.4 2.4 collective-permute-start.21
  175.9 3.5 convolution_convert_fusion.1
  182.8 4.6 %collective-permute-done.22 = bf16[128,1024]{1,0:T(8,128)(2,1)S(1)} collective-permute-done((bf16[128,1024]{1,0:T(8,128)(2,1)}, bf16[128,1024]{1,0:T(8,128)(2,1)S(1)}, u32[]{:S(2)}, u32[]{:S(2)}) %collective-permute-start.22) | collective-permute-done | bytes 262176 | tf_op jit(solution)/shard_map/ppermute | solution.py:430
  191.9 2.5 copy.197
  194.4 2.9 collective-permute-done.24
  197.3 5.8 %collective-permute-done.25 = bf16[128,1024]{1,0:T(8,128)(2,1)S(1)} collective-permute-done((bf16[128,1024]{1,0:T(8,128)(2,1)S(1)}, bf16[128,1024]{1,0:T(8,128)(2,1)S(1)}, u32[]{:S(2)}, u32[]{:S(2)}) %collective-permute-start.25) | collective-permute-done | bytes 262176 | tf_op jit(solution)/shard_map/ppermute | solution.py:430
  206.9 2.3 fusion.65.grad_ref
  209.8 26.6 %mixer_backward.2 = (bf16[512,1664]{1,0:T(8,128)(2,1)}, f32[8,1280]{1,0:T(8,128)}, f32[8,128]{1,0:T(8,128)}, f32[2,128,128]{2,1,0:T(8,128)}, f32[8,1280]{1,0:T(8,128)}) custom-call(s32[2]{0:T(128)} %pad_add_fusion.info_ref, f32[1024,1664]{1,0:T(8,128)} %fusion.82.mixed_ref.halo_ref, f32[1024,1664]{1,0:T(8,128)} %fusion.82.mixed_ref.halo_ref, ...), custom_call_target="tpu_custom_call" | custom-call | flops 26624000000 | bytes 10240000 | tf_op jit(solution)/shard_map/mixer_backward/pallas_call | solution.py:398
  240.4 2.3 fusion.73.grad_ref
  242.7 26.4 %mixer_backward.3 = (bf16[512,1664]{1,0:T(8,128)(2,1)}, f32[8,1280]{1,0:T(8,128)}, f32[8,128]{1,0:T(8,128)}, f32[2,128,128]{2,1,0:T(8,128)}, f32[8,1280]{1,0:T(8,128)}) custom-call(s32[2]{0:T(128)} %pad_add_fusion.info_ref, f32[1024,1664]{1,0:T(8,128)} %fusion.82.mixed_ref.halo_ref, f32[1024,1664]{1,0:T(8,128)} %fusion.82.mixed_ref.halo_ref, ...), custom_call_target="tpu_custom_call" | custom-call | flops 26624000000 | bytes 10240000 | tf_op jit(solution)/shard_map/mixer_backward/pallas_call | solution.py:398
  269.1 1.7 constant_dynamic-update-slice_fusion.6
  272.5 4.9 %convolution_convert_fusion = bf16[1024,1664]{1,0:T(8,128)(2,1)S(1)} fusion(bf16[1024,1664]{1,0:T(8,128)(2,1)S(1)} %constant_dynamic-update-slice_fusion.5, bf16[1024,1024]{1,0:T(8,128)(2,1)S(1)} %copy-done.4, f32[1024]{0:T(1024)S(1)} %get-tuple-element.241, f32[1024]{0:T(1024)S(1)} %add_rsqrt_fusion), kind=kOutput, calls=%fused_computation.9 | convolution fusion | flops 3495559168 | bytes 8921088 | tf_op jit(solution)/shard_map/dot_general | solution.py:535
  278.5 2.4 copy.199
  281.0 1.8 constant_dynamic-slice_fusion.3
  286.9 7.0 %fusion.120 = f32[1024,1024]{1,0:T(8,128)S(1)} fusion(bf16[1024,1664]{1,0:T(8,128)(2,1)} %copy-done.21, bf16[1024,1664]{1,0:T(8,128)(2,1)} %bitcast.297), kind=kOutput, calls=%fused_computation.370 | convolution fusion | flops 3489660928 | bytes 11010048 | tf_op jit(solution)/shard_map/dot_general | solution.py:539
  296.7 2.6 collective-permute-done.40
  300.2 3.1 fusion.88
  303.3 3.3 collective-permute-done.41
  308.0 1.8 collective-permute-start.36
  312.5 21.9 %collective-permute-done.42 = f32[17,1280]{1,0:T(8,128)S(1)} collective-permute-done((f32[17,1280]{1,0:T(8,128)S(1)}, f32[17,1280]{1,0:T(8,128)S(1)}, u32[]{:S(2)}, u32[]{:S(2)}) %collective-permute-start.42) | collective-permute-done | bytes 87072 | tf_op jit(solution)/shard_map/ppermute | solution.py:430
  336.7 2.7 collective-permute-done.43
  339.4 1.9 fusion.34
  341.4 3.0 fusion.38
  (403 shorter events, 96.0 us)
Async XLA Ops:
  7.2 63.4 %all-gather.6.cloned.1.call-start = ((), (), s32[]{:S(2)}) async-start(), calls=%async_computation.5 | async-start | bytes 3833856 | tf_op jit(solution)/shard_map/all_gather | solution.py:512
  14.1 7.8 %collective-permute-start = (bf16[1,32,1664]{2,1,0:T(8,128)(2,1)S(1)}, bf16[1,32,1664]{2,1,0:T(8,128)(2,1)S(1)}, u32[]{:S(2)}, u32[]{:S(2)}) collective-permute-start(bf16[1,32,1664]{2,1,0:T(8,128)(2,1)S(1)} %get-tuple-element.129), channel_id=1, source_target_pairs={{0,24},{8,16},{16,8},{24,0},{1,25},{9,17},{17,9},{25,1},{2,26},{10... | collective-permute-start | bytes 319496 | tf_op jit(solution)/shard_map/ppermute | solution.py:430
  18.1 5.5 %collective-permute-start.1 = (bf16[1,32,1664]{2,1,0:T(8,128)(2,1)S(1)}, bf16[1,32,1664]{2,1,0:T(8,128)(2,1)S(1)}, u32[]{:S(2)}, u32[]{:S(2)}) collective-permute-start(bf16[1,32,1664]{2,1,0:T(8,128)(2,1)S(1)} %get-tuple-element.130), channel_id=1, source_target_pairs={{0,8},{8,0},{16,24},{24,16},{1,9},{9,1},{17,25},{25,17},{2,10},{10... | collective-permute-start | bytes 319496 | tf_op jit(solution)/shard_map/ppermute | solution.py:430
  24.4 109.3 %all-gather.4.cloned.1.call-start = ((), (), s32[]{:S(2)}) async-start(), calls=%async_computation.2 | async-start | bytes 7372800 | tf_op jit(solution)/shard_map/all_gather | solution.py:512
  25.2 15.0 %collective-permute-start.3 = (bf16[256,1024]{1,0:T(8,128)(2,1)S(1)}, bf16[256,1024]{1,0:T(8,128)(2,1)}, u32[]{:S(2)}, u32[]{:S(2)}) collective-permute-start(bf16[256,1024]{1,0:T(8,128)(2,1)S(1)} %bitcast.289), channel_id=1, source_target_pairs={{0,8},{8,0},{16,24},{24,16},{1,9},{9,1},{17,25},{25,17},{2,10},{10... | collective-permute-start | bytes 1572872 | tf_op jit(solution)/shard_map/ppermute | solution.py:430
  26.9 23.1 %collective-permute-start.4 = (bf16[256,1024]{1,0:T(8,128)(2,1)S(1)}, bf16[256,1024]{1,0:T(8,128)(2,1)}, u32[]{:S(2)}, u32[]{:S(2)}) collective-permute-start(bf16[256,1024]{1,0:T(8,128)(2,1)S(1)} %bitcast.290), channel_id=1, source_target_pairs={{0,16},{8,24},{16,0},{24,8},{1,17},{9,25},{17,1},{25,9},{2,18},{10... | collective-permute-start | bytes 1572872 | tf_op jit(solution)/shard_map/ppermute | solution.py:430
  28.3 22.9 %collective-permute-start.5 = (bf16[256,1024]{1,0:T(8,128)(2,1)S(1)}, bf16[256,1024]{1,0:T(8,128)(2,1)}, u32[]{:S(2)}, u32[]{:S(2)}) collective-permute-start(bf16[256,1024]{1,0:T(8,128)(2,1)S(1)} %bitcast.291), channel_id=1, source_target_pairs={{0,24},{8,16},{16,8},{24,0},{1,25},{9,17},{17,9},{25,1},{2,26},{10... | collective-permute-start | bytes 1572872 | tf_op jit(solution)/shard_map/ppermute | solution.py:430
  52.4 9.0 %collective-permute-start.9 = (bf16[1,32,3136]{2,1,0:T(8,128)(2,1)S(1)}, bf16[1,32,3136]{2,1,0:T(8,128)(2,1)S(1)}, u32[]{:S(2)}, u32[]{:S(2)}) collective-permute-start(bf16[1,32,3136]{2,1,0:T(8,128)(2,1)S(1)} %get-tuple-element.149), channel_id=1, source_target_pairs={{0,24},{8,16},{16,8},{24,0},{1,25},{9,17},{17,9},{25,1},{2,26},{10... | collective-permute-start | bytes 602120 | tf_op jit(solution)/shard_map/ppermute | solution.py:430
  55.3 7.1 %collective-permute-start.10 = (bf16[1,32,3136]{2,1,0:T(8,128)(2,1)S(1)}, bf16[1,32,3136]{2,1,0:T(8,128)(2,1)S(1)}, u32[]{:S(2)}, u32[]{:S(2)}) collective-permute-start(bf16[1,32,3136]{2,1,0:T(8,128)(2,1)S(1)} %get-tuple-element.150), channel_id=1, source_target_pairs={{0,8},{8,0},{16,24},{24,16},{1,9},{9,1},{17,25},{25,17},{2,10},{10... | collective-permute-start | bytes 602120 | tf_op jit(solution)/shard_map/ppermute | solution.py:430
  56.5 7.1 %collective-permute-start.11 = (bf16[1,32,3136]{2,1,0:T(8,128)(2,1)S(1)}, bf16[1,32,3136]{2,1,0:T(8,128)(2,1)S(1)}, u32[]{:S(2)}, u32[]{:S(2)}) collective-permute-start(bf16[1,32,3136]{2,1,0:T(8,128)(2,1)S(1)} %get-tuple-element.151), channel_id=1, source_target_pairs={{0,16},{8,24},{16,0},{24,8},{1,17},{9,25},{17,1},{25,9},{2,18},{10... | collective-permute-start | bytes 602120 | tf_op jit(solution)/shard_map/ppermute | solution.py:430
  64.7 216.4 %reduce-scatter.3.cloned.1.call-start = ((), (), s32[]{:S(2)}) async-start(), calls=%async_computation.3 | async-start | bytes 5013504 | tf_op jit(solution)/shard_map/reduce_scatter | solution.py:526
  79.4 26.2 %collective-permute-start.6 = (bf16[256,1024]{1,0:T(8,128)(2,1)S(1)}, bf16[256,1024]{1,0:T(8,128)(2,1)S(1)}, u32[]{:S(2)}, u32[]{:S(2)}) collective-permute-start(bf16[256,1024]{1,0:T(8,128)(2,1)S(1)} %bitcast.307), channel_id=1, source_target_pairs={{0,8},{8,0},{16,24},{24,16},{1,9},{9,1},{17,25},{25,17},{2,10},{10... | collective-permute-start | bytes 1572872 | tf_op jit(solution)/shard_map/ppermute | solution.py:430
  80.3 27.4 %collective-permute-start.7 = (bf16[256,1024]{1,0:T(8,128)(2,1)S(1)}, bf16[256,1024]{1,0:T(8,128)(2,1)S(1)}, u32[]{:S(2)}, u32[]{:S(2)}) collective-permute-start(bf16[256,1024]{1,0:T(8,128)(2,1)S(1)} %bitcast.308), channel_id=1, source_target_pairs={{0,16},{8,24},{16,0},{24,8},{1,17},{9,25},{17,1},{25,9},{2,18},{10... | collective-permute-start | bytes 1572872 | tf_op jit(solution)/shard_map/ppermute | solution.py:430
  80.9 26.8 %collective-permute-start.8 = (bf16[256,1024]{1,0:T(8,128)(2,1)S(1)}, bf16[256,1024]{1,0:T(8,128)(2,1)S(1)}, u32[]{:S(2)}, u32[]{:S(2)}) collective-permute-start(bf16[256,1024]{1,0:T(8,128)(2,1)S(1)} %bitcast.309), channel_id=1, source_target_pairs={{0,24},{8,16},{16,8},{24,0},{1,25},{9,17},{17,9},{25,1},{2,26},{10... | collective-permute-start | bytes 1572872 | tf_op jit(solution)/shard_map/ppermute | solution.py:430
  104.1 22.7 %collective-permute-start.12 = (bf16[512,256]{1,0:T(8,128)(2,1)}, bf16[512,256]{1,0:T(8,128)(2,1)S(1)}, u32[]{:S(2)}, u32[]{:S(2)}) collective-permute-start(bf16[512,256]{1,0:T(8,128)(2,1)} %get-tuple-element.157), channel_id=1, source_target_pairs={{0,8},{8,0},{16,24},{24,16},{1,9},{9,1},{17,25},{25,17},{2,10},{10... | collective-permute-start | bytes 786440 | tf_op jit(solution)/shard_map/ppermute | solution.py:430
  105.1 21.8 %collective-permute-start.13 = (bf16[512,256]{1,0:T(8,128)(2,1)}, bf16[512,256]{1,0:T(8,128)(2,1)S(1)}, u32[]{:S(2)}, u32[]{:S(2)}) collective-permute-start(bf16[512,256]{1,0:T(8,128)(2,1)} %get-tuple-element.157), channel_id=1, source_target_pairs={{0,16},{8,24},{16,0},{24,8},{1,17},{9,25},{17,1},{25,9},{2,18},{10... | collective-permute-start | bytes 786440 | tf_op jit(solution)/shard_map/ppermute | solution.py:430
  105.7 21.3 %collective-permute-start.14 = (bf16[512,256]{1,0:T(8,128)(2,1)}, bf16[512,256]{1,0:T(8,128)(2,1)S(1)}, u32[]{:S(2)}, u32[]{:S(2)}) collective-permute-start(bf16[512,256]{1,0:T(8,128)(2,1)} %get-tuple-element.157), channel_id=1, source_target_pairs={{0,24},{8,16},{16,8},{24,0},{1,25},{9,17},{17,9},{25,1},{2,26},{10... | collective-permute-start | bytes 786440 | tf_op jit(solution)/shard_map/ppermute | solution.py:430
  126.9 17.7 %collective-permute-start.15 = (bf16[512,256]{1,0:T(8,128)(2,1)}, bf16[512,256]{1,0:T(8,128)(2,1)}, u32[]{:S(2)}, u32[]{:S(2)}) collective-permute-start(bf16[512,256]{1,0:T(8,128)(2,1)} %get-tuple-element.162), channel_id=1, source_target_pairs={{0,8},{8,0},{16,24},{24,16},{1,9},{9,1},{17,25},{25,17},{2,10},{10... | collective-permute-start | bytes 786440 | tf_op jit(solution)/shard_map/ppermute | solution.py:430
  127.9 16.8 %collective-permute-start.16 = (bf16[512,256]{1,0:T(8,128)(2,1)}, bf16[512,256]{1,0:T(8,128)(2,1)}, u32[]{:S(2)}, u32[]{:S(2)}) collective-permute-start(bf16[512,256]{1,0:T(8,128)(2,1)} %get-tuple-element.162), channel_id=1, source_target_pairs={{0,16},{8,24},{16,0},{24,8},{1,17},{9,25},{17,1},{25,9},{2,18},{10... | collective-permute-start | bytes 786440 | tf_op jit(solution)/shard_map/ppermute | solution.py:430
  128.5 16.2 %collective-permute-start.17 = (bf16[512,256]{1,0:T(8,128)(2,1)}, bf16[512,256]{1,0:T(8,128)(2,1)}, u32[]{:S(2)}, u32[]{:S(2)}) collective-permute-start(bf16[512,256]{1,0:T(8,128)(2,1)} %get-tuple-element.162), channel_id=1, source_target_pairs={{0,24},{8,16},{16,8},{24,0},{1,25},{9,17},{17,9},{25,1},{2,26},{10... | collective-permute-start | bytes 786440 | tf_op jit(solution)/shard_map/ppermute | solution.py:430
  147.2 10.1 %collective-permute-start.18 = (bf16[128,1024]{1,0:T(8,128)(2,1)S(1)}, bf16[128,1024]{1,0:T(8,128)(2,1)S(1)}, u32[]{:S(2)}, u32[]{:S(2)}) collective-permute-start(bf16[128,1024]{1,0:T(8,128)(2,1)S(1)} %get-tuple-element.166), channel_id=1, source_target_pairs={{0,24},{8,16},{16,8},{24,0},{1,25},{9,17},{17,9},{25,1},{2,26},{10... | collective-permute-start | bytes 786440 | tf_op jit(solution)/shard_map/ppermute | solution.py:430
  149.6 12.6 %collective-permute-start.19 = (bf16[128,1024]{1,0:T(8,128)(2,1)S(1)}, bf16[128,1024]{1,0:T(8,128)(2,1)S(1)}, u32[]{:S(2)}, u32[]{:S(2)}) collective-permute-start(bf16[128,1024]{1,0:T(8,128)(2,1)S(1)} %get-tuple-element.167), channel_id=1, source_target_pairs={{0,8},{8,0},{16,24},{24,16},{1,9},{9,1},{17,25},{25,17},{2,10},{10... | collective-permute-start | bytes 786440 | tf_op jit(solution)/shard_map/ppermute | solution.py:430
  150.2 12.1 %collective-permute-start.20 = (bf16[128,1024]{1,0:T(8,128)(2,1)S(1)}, bf16[128,1024]{1,0:T(8,128)(2,1)S(1)}, u32[]{:S(2)}, u32[]{:S(2)}) collective-permute-start(bf16[128,1024]{1,0:T(8,128)(2,1)S(1)} %get-tuple-element.168), channel_id=1, source_target_pairs={{0,16},{8,24},{16,0},{24,8},{1,17},{9,25},{17,1},{25,9},{2,18},{10... | collective-permute-start | bytes 786440 | tf_op jit(solution)/shard_map/ppermute | solution.py:430
  172.4 10.4 %collective-permute-start.21 = (bf16[128,1024]{1,0:T(8,128)(2,1)}, bf16[128,1024]{1,0:T(8,128)(2,1)S(1)}, u32[]{:S(2)}, u32[]{:S(2)}) collective-permute-start(bf16[128,1024]{1,0:T(8,128)(2,1)} %get-tuple-element.170), channel_id=1, source_target_pairs={{0,24},{8,16},{16,8},{24,0},{1,25},{9,17},{17,9},{25,1},{2,26},{10... | collective-permute-start | bytes 786440 | tf_op jit(solution)/shard_map/ppermute | solution.py:430
  174.8 12.6 %collective-permute-start.22 = (bf16[128,1024]{1,0:T(8,128)(2,1)}, bf16[128,1024]{1,0:T(8,128)(2,1)S(1)}, u32[]{:S(2)}, u32[]{:S(2)}) collective-permute-start(bf16[128,1024]{1,0:T(8,128)(2,1)} %get-tuple-element.171), channel_id=1, source_target_pairs={{0,8},{8,0},{16,24},{24,16},{1,9},{9,1},{17,25},{25,17},{2,10},{10... | collective-permute-start | bytes 786440 | tf_op jit(solution)/shard_map/ppermute | solution.py:430
  175.3 12.1 %collective-permute-start.23 = (bf16[128,1024]{1,0:T(8,128)(2,1)}, bf16[128,1024]{1,0:T(8,128)(2,1)S(1)}, u32[]{:S(2)}, u32[]{:S(2)}) collective-permute-start(bf16[128,1024]{1,0:T(8,128)(2,1)} %get-tuple-element.172), channel_id=1, source_target_pairs={{0,16},{8,24},{16,0},{24,8},{1,17},{9,25},{17,1},{25,9},{2,18},{10... | collective-permute-start | bytes 786440 | tf_op jit(solution)/shard_map/ppermute | solution.py:430
  188.0 9.2 %collective-permute-start.24 = (bf16[128,1024]{1,0:T(8,128)(2,1)S(1)}, bf16[128,1024]{1,0:T(8,128)(2,1)S(1)}, u32[]{:S(2)}, u32[]{:S(2)}) collective-permute-start(bf16[128,1024]{1,0:T(8,128)(2,1)S(1)} %add_convert_fusion), channel_id=1, source_target_pairs={{0,8},{8,0},{16,24},{24,16},{1,9},{9,1},{17,25},{25,17},{2,10},{10... | collective-permute-start | bytes 786440 | tf_op jit(solution)/shard_map/ppermute | solution.py:430
  189.6 13.5 %collective-permute-start.25 = (bf16[128,1024]{1,0:T(8,128)(2,1)S(1)}, bf16[128,1024]{1,0:T(8,128)(2,1)S(1)}, u32[]{:S(2)}, u32[]{:S(2)}) collective-permute-start(bf16[128,1024]{1,0:T(8,128)(2,1)S(1)} %add_convert_fusion), channel_id=1, source_target_pairs={{0,16},{8,24},{16,0},{24,8},{1,17},{9,25},{17,1},{25,9},{2,18},{10... | collective-permute-start | bytes 786440 | tf_op jit(solution)/shard_map/ppermute | solution.py:430
  191.0 12.1 %collective-permute-start.26 = (bf16[128,1024]{1,0:T(8,128)(2,1)S(1)}, bf16[128,1024]{1,0:T(8,128)(2,1)S(1)}, u32[]{:S(2)}, u32[]{:S(2)}) collective-permute-start(bf16[128,1024]{1,0:T(8,128)(2,1)S(1)} %add_convert_fusion), channel_id=1, source_target_pairs={{0,24},{8,16},{16,8},{24,0},{1,25},{9,17},{17,9},{25,1},{2,26},{10... | collective-permute-start | bytes 786440 | tf_op jit(solution)/shard_map/ppermute | solution.py:430
  203.1 141.3 %reduce-scatter.5.cloned.1.call-start = ((), (), s32[]{:S(2)}) async-start(), calls=%async_computation.4 | async-start | bytes 4423680 | tf_op jit(solution)/shard_map/reduce_scatter | solution.py:526
  203.1 33.4 %collective-permute-start.27 = (bf16[128,1024]{1,0:T(8,128)(2,1)S(1)}, bf16[128,1024]{1,0:T(8,128)(2,1)S(1)}, u32[]{:S(2)}, u32[]{:S(2)}) collective-permute-start(bf16[128,1024]{1,0:T(8,128)(2,1)S(1)} %add_convert_fusion.1), channel_id=1, source_target_pairs={{0,8},{8,0},{16,24},{24,16},{1,9},{9,1},{17,25},{25,17},{2,10},{10... | collective-permute-start | bytes 786440 | tf_op jit(solution)/shard_map/ppermute | solution.py:430
  204.4 32.2 %collective-permute-start.28 = (bf16[128,1024]{1,0:T(8,128)(2,1)S(1)}, bf16[128,1024]{1,0:T(8,128)(2,1)S(1)}, u32[]{:S(2)}, u32[]{:S(2)}) collective-permute-start(bf16[128,1024]{1,0:T(8,128)(2,1)S(1)} %add_convert_fusion.1), channel_id=1, source_target_pairs={{0,16},{8,24},{16,0},{24,8},{1,17},{9,25},{17,1},{25,9},{2,18},{10... | collective-permute-start | bytes 786440 | tf_op jit(solution)/shard_map/ppermute | solution.py:430
  205.3 31.3 %collective-permute-start.29 = (bf16[128,1024]{1,0:T(8,128)(2,1)S(1)}, bf16[128,1024]{1,0:T(8,128)(2,1)S(1)}, u32[]{:S(2)}, u32[]{:S(2)}) collective-permute-start(bf16[128,1024]{1,0:T(8,128)(2,1)S(1)} %add_convert_fusion.1), channel_id=1, source_target_pairs={{0,24},{8,16},{16,8},{24,0},{1,25},{9,17},{17,9},{25,1},{2,26},{10... | collective-permute-start | bytes 786440 | tf_op jit(solution)/shard_map/ppermute | solution.py:430
  236.6 44.4 %collective-permute-start.30 = (bf16[256,1024]{1,0:T(8,128)(2,1)}, bf16[256,1024]{1,0:T(8,128)(2,1)}, u32[]{:S(2)}, u32[]{:S(2)}) collective-permute-start(bf16[256,1024]{1,0:T(8,128)(2,1)} %get-tuple-element.207), channel_id=1, source_target_pairs={{0,24},{8,16},{16,8},{24,0},{1,25},{9,17},{17,9},{25,1},{2,26},{10... | collective-permute-start | bytes 1572872 | tf_op jit(solution)/shard_map/ppermute | solution.py:430
  238.1 42.9 %collective-permute-start.31 = (bf16[256,1024]{1,0:T(8,128)(2,1)}, bf16[256,1024]{1,0:T(8,128)(2,1)}, u32[]{:S(2)}, u32[]{:S(2)}) collective-permute-start(bf16[256,1024]{1,0:T(8,128)(2,1)} %get-tuple-element.208), channel_id=1, source_target_pairs={{0,8},{8,0},{16,24},{24,16},{1,9},{9,1},{17,25},{25,17},{2,10},{10... | collective-permute-start | bytes 1572872 | tf_op jit(solution)/shard_map/ppermute | solution.py:430
  239.6 41.3 %collective-permute-start.32 = (bf16[256,1024]{1,0:T(8,128)(2,1)}, bf16[256,1024]{1,0:T(8,128)(2,1)}, u32[]{:S(2)}, u32[]{:S(2)}) collective-permute-start(bf16[256,1024]{1,0:T(8,128)(2,1)} %get-tuple-element.209), channel_id=1, source_target_pairs={{0,16},{8,24},{16,0},{24,8},{1,17},{9,25},{17,1},{25,9},{2,18},{10... | collective-permute-start | bytes 1572872 | tf_op jit(solution)/shard_map/ppermute | solution.py:430
  282.8 25.1 %collective-permute-start.33 = (bf16[1,32,2112]{2,1,0:T(8,128)(2,1)}, bf16[1,32,2112]{2,1,0:T(8,128)(2,1)S(1)}, u32[]{:S(2)}, u32[]{:S(2)}) collective-permute-start(bf16[1,32,2112]{2,1,0:T(8,128)(2,1)} %get-tuple-element.217), channel_id=1, source_target_pairs={{0,24},{8,16},{16,8},{24,0},{1,25},{9,17},{17,9},{25,1},{2,26},{10... | collective-permute-start | bytes 405512 | tf_op jit(solution)/shard_map/ppermute | solution.py:430
  284.3 25.5 %collective-permute-start.34 = (bf16[1,32,2112]{2,1,0:T(8,128)(2,1)}, bf16[1,32,2112]{2,1,0:T(8,128)(2,1)}, u32[]{:S(2)}, u32[]{:S(2)}) collective-permute-start(bf16[1,32,2112]{2,1,0:T(8,128)(2,1)} %get-tuple-element.218), channel_id=1, source_target_pairs={{0,8},{8,0},{16,24},{24,16},{1,9},{9,1},{17,25},{25,17},{2,10},{10... | collective-permute-start | bytes 405512 | tf_op jit(solution)/shard_map/ppermute | solution.py:430
  285.8 24.4 %collective-permute-start.35 = (bf16[1,32,2112]{2,1,0:T(8,128)(2,1)}, bf16[1,32,2112]{2,1,0:T(8,128)(2,1)S(1)}, u32[]{:S(2)}, u32[]{:S(2)}) collective-permute-start(bf16[1,32,2112]{2,1,0:T(8,128)(2,1)} %get-tuple-element.219), channel_id=1, source_target_pairs={{0,16},{8,24},{16,0},{24,8},{1,17},{9,25},{17,1},{25,9},{2,18},{10... | collective-permute-start | bytes 405512 | tf_op jit(solution)/shard_map/ppermute | solution.py:430
  286.8 7.1 %collective-permute-start.39 = (f32[5,1280]{1,0:T(8,128)S(1)}, f32[5,1280]{1,0:T(8,128)S(1)}, u32[]{:S(2)}, u32[]{:S(2)}) collective-permute-start(f32[5,1280]{1,0:T(8,128)S(1)} %pad_maximum_fusion.13), channel_id=1, source_target_pairs={{0,1},{1,0},{2,3},{3,2},{4,5},{5,4},{6,7},{7,6},{8,9},{9,8},{10,11... | collective-permute-start | bytes 76808 | tf_op jit(solution)/shard_map/ppermute | solution.py:430
  295.2 44.2 %collective-permute-start.38 = (bf16[256,1024]{1,0:T(8,128)(2,1)}, bf16[256,1024]{1,0:T(8,128)(2,1)}, u32[]{:S(2)}, u32[]{:S(2)}) collective-permute-start(bf16[256,1024]{1,0:T(8,128)(2,1)} %get-tuple-element.270), channel_id=1, source_target_pairs={{0,16},{8,24},{16,0},{24,8},{1,17},{9,25},{17,1},{25,9},{2,18},{10... | collective-permute-start | bytes 1572872 | tf_op jit(solution)/shard_map/ppermute | solution.py:430
  299.3 7.3 %collective-permute-start.41 = (f32[5,1280]{1,0:T(8,128)S(1)}, f32[5,1280]{1,0:T(8,128)S(1)}, u32[]{:S(2)}, u32[]{:S(2)}) collective-permute-start(f32[5,1280]{1,0:T(8,128)S(1)} %add.453), channel_id=1, source_target_pairs={{0,4},{1,5},{2,6},{3,7},{4,0},{5,1},{6,2},{7,3},{8,12},{9,13},{10,... | collective-permute-start | bytes 76808 | tf_op jit(solution)/shard_map/ppermute | solution.py:430
  306.6 32.8 %collective-permute-start.37 = (bf16[256,1024]{1,0:T(8,128)(2,1)}, bf16[256,1024]{1,0:T(8,128)(2,1)S(1)}, u32[]{:S(2)}, u32[]{:S(2)}) collective-permute-start(bf16[256,1024]{1,0:T(8,128)(2,1)} %get-tuple-element.269), channel_id=1, source_target_pairs={{0,8},{8,0},{16,24},{24,16},{1,9},{9,1},{17,25},{25,17},{2,10},{10... | collective-permute-start | bytes 1572872 | tf_op jit(solution)/shard_map/ppermute | solution.py:430
  308.0 31.4 %collective-permute-start.36 = (bf16[256,1024]{1,0:T(8,128)(2,1)}, bf16[256,1024]{1,0:T(8,128)(2,1)S(1)}, u32[]{:S(2)}, u32[]{:S(2)}) collective-permute-start(bf16[256,1024]{1,0:T(8,128)(2,1)} %get-tuple-element.268), channel_id=1, source_target_pairs={{0,24},{8,16},{16,8},{24,0},{1,25},{9,17},{17,9},{25,1},{2,26},{10... | collective-permute-start | bytes 1572872 | tf_op jit(solution)/shard_map/ppermute | solution.py:430
  309.8 24.6 %collective-permute-start.42 = (f32[17,1280]{1,0:T(8,128)S(1)}, f32[17,1280]{1,0:T(8,128)S(1)}, u32[]{:S(2)}, u32[]{:S(2)}) collective-permute-start(f32[17,1280]{1,0:T(8,128)S(1)} %pad_maximum_fusion.12), channel_id=1, source_target_pairs={{0,8},{8,0},{16,24},{24,16},{1,9},{9,1},{17,25},{25,17},{2,10},{10... | collective-permute-start | bytes 261128 | tf_op jit(solution)/shard_map/ppermute | solution.py:430
  346.6 8.6 %collective-permute-start.44 = (bf16[1,32,1920]{2,1,0:T(8,128)(2,1)S(1)}, bf16[1,32,1920]{2,1,0:T(8,128)(2,1)S(1)}, u32[]{:S(2)}, u32[]{:S(2)}) collective-permute-start(bf16[1,32,1920]{2,1,0:T(8,128)(2,1)S(1)} %get-tuple-element.232), channel_id=1, source_target_pairs={{0,24},{8,16},{16,8},{24,0},{1,25},{9,17},{17,9},{25,1},{2,26},{10... | collective-permute-start | bytes 368648 | tf_op jit(solution)/shard_map/ppermute | solution.py:430
  348.0 7.1 %collective-permute-start.45 = (bf16[1,32,1920]{2,1,0:T(8,128)(2,1)S(1)}, bf16[1,32,1920]{2,1,0:T(8,128)(2,1)S(1)}, u32[]{:S(2)}, u32[]{:S(2)}) collective-permute-start(bf16[1,32,1920]{2,1,0:T(8,128)(2,1)S(1)} %get-tuple-element.233), channel_id=1, source_target_pairs={{0,8},{8,0},{16,24},{24,16},{1,9},{9,1},{17,25},{25,17},{2,10},{10... | collective-permute-start | bytes 368648 | tf_op jit(solution)/shard_map/ppermute | solution.py:430
  349.6 5.5 %collective-permute-start.46 = (bf16[1,32,1920]{2,1,0:T(8,128)(2,1)S(1)}, bf16[1,32,1920]{2,1,0:T(8,128)(2,1)S(1)}, u32[]{:S(2)}, u32[]{:S(2)}) collective-permute-start(bf16[1,32,1920]{2,1,0:T(8,128)(2,1)S(1)} %get-tuple-element.234), channel_id=1, source_target_pairs={{0,16},{8,24},{16,0},{24,8},{1,17},{9,25},{17,1},{25,9},{2,18},{10... | collective-permute-start | bytes 368648 | tf_op jit(solution)/shard_map/ppermute | solution.py:430
  (64 other events, 527.4 us)
Sparse Core Ops, SparseCore 0:
  24.6 41.6 all-gather.5
  67.9 65.8 all-gather.3
  203.2 50.1 reduce-scatter.2
  281.2 47.0 reduce-scatter.4
